TPU v7x, 32 devices: a whole 2x2x4 slice. The times are simulated.
32 devices in a mesh: frames: 16 (over z, y, x), mp: 2 (over core).
Axes of the slice: x: 2, y: 2, z: 4, core: 2. Of those that a mesh axis runs over, the one named last changes fastest.
Arguments:
- tokens: bfloat16 [2, 16, 256, 1024], P(None, 'frames', 'mp'), may hold values from -6 to 6
- cotangent: bfloat16 [2, 16, 256, 1024], P(None, 'frames', 'mp'), may hold values from -6 to 6
- scene_ids: int32 [2, 16], replicated, may hold values from 0 to 7, never falling along the last dimension, each value on 1 to 4 neighbouring positions
- input_weight: bfloat16 [2, 1024, 3, 1024], P(None, 'frames', None, 'mp'), may hold values from -0.1875 to 0.1875
- output_weight: bfloat16 [2, 1024, 1024], P(None, 'frames', 'mp'), may hold values from -1 to 1
- up_weight: bfloat16 [2, 1024, 4096], P(None, 'frames', 'mp'), may hold values from -0.1875 to 0.1875
- down_weight: bfloat16 [2, 1024, 4096], P(None, 'frames', 'mp'), may hold values from -0.09375 to 0.09375
- norm_params: float32 [2, 6, 1024], replicated
- head_gains: float32 [2, 2, 64], replicated, may hold values from 0.5 to 1.5
Outputs:
- result: bfloat16 [2, 16, 256, 1024], P(None, 'frames', 'mp')
- token_grad: float32 [2, 16, 256, 1024], P(None, 'frames', 'mp')
- input_grad: float32 [2, 1024, 3, 1024], P(None, 'frames', None, 'mp')
- output_grad: float32 [2, 1024, 1024], P(None, 'frames', 'mp')
- up_grad: float32 [2, 1024, 4096], P(None, 'frames', 'mp')
- down_grad: float32 [2, 1024, 4096], P(None, 'frames', 'mp')
- norm_grad: float32 [2, 6, 1024], replicated
- gain_grad: float32 [2, 2, 64], replicated
Inputs may be any that keep to these rules, and one draw needn't show every extreme that they name: `scene_ids`: along each row the scene numbers never fall, so the frames of one scene are consecutive; each scene has 1 to 4 frames and some scene has exactly 4.
All inputs are finite; a program needn't handle non-finite values.
Results may differ from a plain program's by a relative error of at most 0.015.
Values may be sent and summed in bfloat16 or wider, within the bound.
No kernel may reach another device: no remote copies, remote signals or barrier semaphores. Data moves between devices by JAX's collectives and lax.ppermute only.
A program may use at most 256 MiB of HBM per device.

v0:
```python
import jax
import jax.numpy as jnp
from jax import lax
from jax.sharding import PartitionSpec as P

MAXF = 4


ROW_EPS = 1e-06
HEAD_EPS = 1e-05
NEG_FILL = -1e30


def from_behind(block, axis, distance):
    devices = range(lax.axis_size(axis))
    route = [(i - distance, i) for i in devices if i - distance in devices]
    return lax.ppermute(block, axis, route)


def layer_norm(values, gain_row, bias_row, epsilon):
    centred = values - jnp.mean(values, axis=-1, keepdims=True)
    spread = jnp.mean(centred * centred, axis=-1, keepdims=True)
    return centred * lax.rsqrt(spread + epsilon) * gain_row + bias_row


def row_norm(values, gain_row, bias_row):
    return layer_norm(values, gain_row, bias_row, ROW_EPS)


def head_norm(values, gain_row):
    return layer_norm(values, gain_row, 0.0, HEAD_EPS)


def exact_gelu(values):
    return jax.nn.gelu(values, approximate=False)


def full_rows(values):
    return lax.all_gather(values, "mp", axis=0, tiled=True)


def row_products(left_rows, weight, pattern):
    return lax.psum_scatter(
        jnp.einsum(pattern, left_rows, weight, preferred_element_type=jnp.float32).astype(
            jnp.bfloat16
        ),
        "mp",
        scatter_dimension=0,
        tiled=True,
    ).astype(jnp.float32)


def scene_flags(scene_row, span_frames):
    frame_total = scene_row.shape[0]
    here_index = lax.axis_index("frames")
    here_scene = lax.dynamic_index_in_dim(scene_row, here_index, 0, keepdims=False)
    member_flags = []
    for offset in range(-span_frames, span_frames + 1):
        position = here_index + offset
        inside = jnp.logical_and(position >= 0, position < frame_total)
        neighbour = lax.dynamic_index_in_dim(
            scene_row, jnp.clip(position, 0, frame_total - 1), 0, keepdims=False
        )
        member_flags.append(jnp.logical_and(inside, neighbour == here_scene))
    return member_flags


def neighbour_pieces(key_value, span_frames):
    pieces = []
    for offset in range(-span_frames, span_frames + 1):
        if offset == 0:
            pieces.append(key_value)
        else:
            pieces.append(from_behind(key_value, "frames", -offset))
    return pieces


def return_pairs(d_pairs, span_frames):
    collected = jnp.zeros_like(d_pairs[0])
    for offset, d_pair in zip(range(-span_frames, span_frames + 1), d_pairs):
        if offset == 0:
            collected = collected + d_pair
        else:
            collected = collected + from_behind(
                d_pair.astype(jnp.bfloat16), "frames", offset
            ).astype(d_pair.dtype)
    return collected


def split_pair(piece, head_count):
    rows_frame = piece.shape[0]
    return (
        piece[:, 0].reshape(rows_frame, head_count, -1),
        piece[:, 1].reshape(rows_frame, head_count, -1),
    )


def scores_for(queries, keys_block, factor):
    return (
        jnp.einsum("qhd,khd->hqk", queries, keys_block, preferred_element_type=jnp.float32) * factor
    )


def keep_first(running, piece):
    return running


def attend_forward(queries, pieces, member_flags, factor):
    rows_frame, head_count = (queries.shape[0], queries.shape[1])

    def stats_step(stats, piece):
        row_max, row_total = stats
        scores = scores_for(queries, split_pair(piece, head_count)[0], factor)
        new_max = jnp.maximum(row_max, jnp.max(scores, axis=-1))
        row_total = row_total * jnp.exp(row_max - new_max) + jnp.sum(
            jnp.exp(scores - new_max[:, :, None]), axis=-1
        )
        return (new_max, row_total)

    stats = (
        jnp.full((head_count, rows_frame), NEG_FILL, jnp.float32),
        jnp.zeros((head_count, rows_frame), jnp.float32),
    )
    for member, piece in zip(member_flags, pieces):
        stats = lax.cond(member, stats_step, keep_first, stats, piece)
    log_total = stats[0] + jnp.log(stats[1])

    def output_step(running, piece):
        keys_block, values_block = split_pair(piece, head_count)
        weights = jnp.exp(scores_for(queries, keys_block, factor) - log_total[:, :, None]).astype(
            jnp.bfloat16
        )
        return running + jnp.einsum(
            "hqk,khd->qhd", weights, values_block, preferred_element_type=jnp.float32
        )

    running = jnp.zeros(queries.shape, jnp.float32)
    for member, piece in zip(member_flags, pieces):
        running = lax.cond(member, output_step, keep_first, running, piece)
    return (running.astype(jnp.bfloat16), log_total)


def attend_backward(queries, pieces, member_flags, factor, log_total, d_attn):
    rows_frame, head_count = (queries.shape[0], queries.shape[1])

    def delta_step(running, piece):
        keys_block, values_block = split_pair(piece, head_count)
        probs = jnp.exp(scores_for(queries, keys_block, factor) - log_total[:, :, None])
        d_probs = jnp.einsum(
            "qhd,khd->hqk", d_attn, values_block, preferred_element_type=jnp.float32
        )
        return running + jnp.sum(probs * d_probs, axis=-1)

    delta = jnp.zeros((head_count, rows_frame), jnp.float32)
    for member, piece in zip(member_flags, pieces):
        delta = lax.cond(member, delta_step, keep_first, delta, piece)

    def grad_step(piece):
        keys_block, values_block = split_pair(piece, head_count)
        probs = jnp.exp(scores_for(queries, keys_block, factor) - log_total[:, :, None])
        d_probs = jnp.einsum(
            "qhd,khd->hqk", d_attn, values_block, preferred_element_type=jnp.float32
        )
        d_scores = (probs * (d_probs - delta[:, :, None])).astype(jnp.bfloat16)
        d_query = (
            jnp.einsum("hqk,khd->qhd", d_scores, keys_block, preferred_element_type=jnp.float32)
            * factor
        )
        d_keys = (
            jnp.einsum("hqk,qhd->khd", d_scores, queries, preferred_element_type=jnp.float32)
            * factor
        )
        d_values = jnp.einsum(
            "hqk,qhd->khd", probs.astype(jnp.bfloat16), d_attn, preferred_element_type=jnp.float32
        )
        return (d_query, jnp.stack([d_keys, d_values], axis=1).reshape(rows_frame, 2, -1))

    def grad_skip(piece):
        return (jnp.zeros(queries.shape, jnp.float32), jnp.zeros(piece.shape, jnp.float32))

    d_query_total = jnp.zeros(queries.shape, jnp.float32)
    d_pairs = []
    for member, piece in zip(member_flags, pieces):
        d_query, d_pair = lax.cond(member, grad_step, grad_skip, piece)
        d_query_total = d_query_total + d_query
        d_pairs.append(d_pair)
    return (d_query_total, d_pairs)


def block_forward(
    residual,
    weight_in,
    weight_out,
    weight_up,
    weight_down,
    vectors,
    head_gain,
    scene_row,
    span_frames,
):
    head_dim = head_gain.shape[1]
    head_count = weight_in.shape[2] // head_dim
    factor = head_dim ** (-0.5)
    normed = row_norm(residual, vectors[0], vectors[1]).astype(jnp.bfloat16)
    normed_all = full_rows(normed)
    rows_frame = normed_all.shape[0]
    projected = jnp.einsum("rd,dcf->rcf", normed_all, weight_in, preferred_element_type=jnp.float32)
    head_parts = projected.reshape(rows_frame, 3, head_count, head_dim)
    queries = head_norm(head_parts[:, 0], head_gain[0]).astype(jnp.bfloat16)
    keys_own = head_norm(head_parts[:, 1], head_gain[1]).astype(jnp.bfloat16)
    values_own = head_parts[:, 2].astype(jnp.bfloat16)
    key_value = jnp.stack([keys_own, values_own], axis=1).reshape(
        rows_frame, 2, head_count * head_dim
    )
    pieces = neighbour_pieces(key_value, span_frames)
    member_flags = scene_flags(scene_row, span_frames)
    attended, log_total = attend_forward(queries, pieces, member_flags, factor)
    attended_flat = attended.reshape(rows_frame, head_count * head_dim)
    branch = row_products(attended_flat, weight_out, "rf,ef->re")
    residual_mid = residual + vectors[2] * branch
    normed_mid = row_norm(residual_mid, vectors[3], vectors[4]).astype(jnp.bfloat16)
    normed_mid_all = full_rows(normed_mid)
    hidden_pre = jnp.einsum(
        "rd,df->rf", normed_mid_all, weight_up, preferred_element_type=jnp.float32
    )
    active = exact_gelu(hidden_pre).astype(jnp.bfloat16)
    mlp_out = row_products(active, weight_down, "rf,ef->re")
    residual_out = residual_mid + vectors[5] * mlp_out
    stored = {
        "residual": residual,
        "normed_all": normed_all,
        "projected": projected,
        "queries": queries,
        "pieces": pieces,
        "flags": member_flags,
        "log_total": log_total,
        "attended": attended_flat,
        "branch": branch,
        "residual_mid": residual_mid,
        "normed_mid_all": normed_mid_all,
        "hidden_pre": hidden_pre,
        "active": active,
        "mlp_out": mlp_out,
    }
    return (residual_out, stored)


def block_backward(
    d_out, stored, weight_in, weight_out, weight_up, weight_down, vectors, head_gain, span_frames
):
    head_dim = head_gain.shape[1]
    head_count = weight_in.shape[2] // head_dim
    factor = head_dim ** (-0.5)
    rows_frame = stored["normed_all"].shape[0]
    d_mlp = (vectors[5] * d_out).astype(jnp.bfloat16)
    grad_mlp_scale = jnp.sum(d_out * stored["mlp_out"], axis=0)
    d_mlp_all = full_rows(d_mlp)
    d_active = jnp.einsum("re,ef->rf", d_mlp_all, weight_down, preferred_element_type=jnp.float32)
    grad_down = jnp.einsum(
        "re,rf->ef", d_mlp_all, stored["active"], preferred_element_type=jnp.float32
    )
    gelu_back = jax.vjp(exact_gelu, stored["hidden_pre"])[1]
    d_hidden = gelu_back(d_active)[0].astype(jnp.bfloat16)
    grad_up = jnp.einsum(
        "rd,rf->df", stored["normed_mid_all"], d_hidden, preferred_element_type=jnp.float32
    )
    d_normed_mid = row_products(d_hidden, weight_up, "rf,df->rd")
    mid_back = jax.vjp(row_norm, stored["residual_mid"], vectors[3], vectors[4])[1]
    d_resid_part, grad_gain_mid, grad_bias_mid = mid_back(d_normed_mid)
    d_resid_mid = d_out + d_resid_part
    d_branch = (vectors[2] * d_resid_mid).astype(jnp.bfloat16)
    grad_attn_scale = jnp.sum(d_resid_mid * stored["branch"], axis=0)
    d_branch_all = full_rows(d_branch)
    d_attended = jnp.einsum(
        "re,ef->rf", d_branch_all, weight_out, preferred_element_type=jnp.float32
    ).astype(jnp.bfloat16)
    grad_out = jnp.einsum(
        "re,rf->ef", d_branch_all, stored["attended"], preferred_element_type=jnp.float32
    )
    d_query, d_pairs = attend_backward(
        stored["queries"],
        stored["pieces"],
        stored["flags"],
        factor,
        stored["log_total"],
        d_attended.reshape(rows_frame, head_count, head_dim),
    )
    d_pair_own = return_pairs(d_pairs, span_frames).reshape(rows_frame, 2, head_count, head_dim)
    head_parts = stored["projected"].reshape(rows_frame, 3, head_count, head_dim)
    query_back = jax.vjp(head_norm, head_parts[:, 0], head_gain[0])[1]
    d_query_raw, grad_query_gain = query_back(d_query)
    key_back = jax.vjp(head_norm, head_parts[:, 1], head_gain[1])[1]
    d_key_raw, grad_key_gain = key_back(d_pair_own[:, 0])
    d_projected = (
        jnp.stack([d_query_raw, d_key_raw, d_pair_own[:, 1]], axis=1)
        .reshape(rows_frame, 3, head_count * head_dim)
        .astype(jnp.bfloat16)
    )
    grad_in = jnp.einsum(
        "rd,rcf->dcf", stored["normed_all"], d_projected, preferred_element_type=jnp.float32
    )
    d_normed = row_products(d_projected, weight_in, "rcf,dcf->rd")
    first_back = jax.vjp(row_norm, stored["residual"], vectors[0], vectors[1])[1]
    d_resid_first, grad_gain, grad_bias = first_back(d_normed)
    d_residual = d_resid_mid + d_resid_first
    norm_grads = jnp.stack(
        [grad_gain, grad_bias, grad_attn_scale, grad_gain_mid, grad_bias_mid, grad_mlp_scale]
    )
    gain_grads = jnp.stack([grad_query_gain, grad_key_gain])
    return (d_residual, (grad_in, grad_out, grad_up, grad_down), norm_grads, gain_grads)


def body(
    tokens,
    cotangent,
    scene_ids,
    input_weight,
    output_weight,
    up_weight,
    down_weight,
    norm_params,
    head_gains,
):
    portions = tokens.shape[0]
    span_global = MAXF - 1
    shards = (input_weight, output_weight, up_weight, down_weight)
    norm_total = jnp.zeros(norm_params.shape, jnp.float32)
    gain_total = jnp.zeros(head_gains.shape, jnp.float32)
    full_total = None
    shard_total = None
    results = []
    token_grads = []
    for portion in range(portions):
        gathered = (
            lax.all_gather(shards[0], "frames", axis=1, tiled=True),
            lax.all_gather(shards[1], "frames", axis=1, tiled=True),
            lax.all_gather(shards[2], "frames", axis=1, tiled=True),
            lax.all_gather(shards[3], "frames", axis=1, tiled=True),
        )
        residual = tokens[portion, 0].astype(jnp.float32)
        stores = []
        for layer in range(2):
            span_frames = span_global if layer == 1 else 0
            residual, stored = block_forward(
                residual,
                gathered[0][layer],
                gathered[1][layer],
                gathered[2][layer],
                gathered[3][layer],
                norm_params[layer],
                head_gains[layer],
                scene_ids[portion],
                span_frames,
            )
            stores.append(stored)
        results.append(residual.astype(jnp.bfloat16))
        d_residual = cotangent[portion, 0].astype(jnp.float32)
        layer_grads = [None, None]
        for layer in (1, 0):
            span_frames = span_global if layer == 1 else 0
            d_residual, weight_grads, norm_grads, gain_grads = block_backward(
                d_residual,
                stores[layer],
                gathered[0][layer],
                gathered[1][layer],
                gathered[2][layer],
                gathered[3][layer],
                norm_params[layer],
                head_gains[layer],
                span_frames,
            )
            layer_grads[layer] = weight_grads
            norm_total = norm_total.at[layer].add(norm_grads)
            gain_total = gain_total.at[layer].add(gain_grads)
        token_grads.append(d_residual)
        stacked = tuple(
            (
                jnp.stack([layer_grads[0][member_index], layer_grads[1][member_index]])
                for member_index in range(4)
            )
        )
        full_total = (
            stacked
            if full_total is None
            else tuple((earlier + latest for earlier, latest in zip(full_total, stacked)))
        )
    shard_total = (
        lax.psum_scatter(full_total[0], "frames", scatter_dimension=1, tiled=True),
        lax.psum_scatter(full_total[1], "frames", scatter_dimension=1, tiled=True),
        lax.psum_scatter(full_total[2], "frames", scatter_dimension=1, tiled=True),
        lax.psum_scatter(full_total[3], "frames", scatter_dimension=1, tiled=True),
    )
    norm_sum, gain_sum = lax.psum((norm_total, gain_total), ("frames", "mp"))
    result = jnp.stack(results)[:, None]
    token_grad = jnp.stack(token_grads)[:, None]
    return (
        result,
        token_grad,
        shard_total[0],
        shard_total[1],
        shard_total[2],
        shard_total[3],
        norm_sum,
        gain_sum,
    )


def solution(mesh):
    placed = (
        P(None, "frames", "mp", None),
        P(None, "frames", "mp", None),
        P(),
        P(None, "frames", None, "mp"),
        P(None, "frames", "mp"),
        P(None, "frames", "mp"),
        P(None, "frames", "mp"),
        P(),
        P(),
    )
    return jax.shard_map(
        body,
        mesh=mesh,
        in_specs=placed,
        out_specs=(
            P(None, "frames", "mp", None),
            P(None, "frames", "mp", None),
            P(None, "frames", None, "mp"),
            P(None, "frames", "mp"),
            P(None, "frames", "mp"),
            P(None, "frames", "mp"),
            P(),
            P(),
        ),
        check_vma=False,
    )
```

profile of v0, /device:TPU:4, one launch (start us, length us, event | category | flops | bytes accessed | tf_op | source)
XLA Modules:
  0.0 2038.3 jit_solution(14199039401730108756)
XLA Ops:
  18.9 87.1 %all-gather.5.cloned.1.call-done = bf16[2,1024,3,512]{3,1,2,0:T(8,128)(2,1)} async-done(((bf16[2,64,3,512]{3,1,2,0:T(8,128)(2,1)}), bf16[2,1024,3,512]{3,1,2,0:T(8,128)(2,1)}) %all-gather.5.cloned.1.call-update) | async-done | bytes 6291472 | tf_op jit(solution)/shard_map/all_gather | solution.py:335
  106.0 5.2 slice_bitcast_fusion.20
  124.3 43.6 %all-gather.7.cloned.1.call-done = bf16[2,1024,512]{2,1,0:T(8,128)(2,1)} async-done(((bf16[2,64,512]{2,1,0:T(8,128)(2,1)}), bf16[2,1024,512]{2,1,0:T(8,128)(2,1)}) %all-gather.7.cloned.1.call-update) | async-done | bytes 2097168 | tf_op jit(solution)/shard_map/all_gather | solution.py:336
  171.7 5.7 reduce-scatter.21.cloned.1.call-done
  195.1 8.0 reduce-scatter.29.cloned.1.call-done
  211.9 107.5 %all-gather.9.cloned.1.call-done = bf16[2,1024,2048]{2,1,0:T(8,128)(2,1)} async-done(((bf16[2,64,2048]{2,1,0:T(8,128)(2,1)}), bf16[2,1024,2048]{2,1,0:T(8,128)(2,1)}) %all-gather.9.cloned.1.call-update) | async-done | bytes 8388624 | tf_op jit(solution)/shard_map/all_gather | solution.py:337
  319.5 8.6 multiply_convert_fusion.19
  328.1 104.9 %all-gather.11.cloned.1.call-done = bf16[2,1024,2048]{2,1,0:T(8,128)(2,1)} async-done(((bf16[2,64,2048]{2,1,0:T(8,128)(2,1)}), bf16[2,1024,2048]{2,1,0:T(8,128)(2,1)}) %all-gather.11.cloned.1.call-update) | async-done | bytes 8388624 | tf_op jit(solution)/shard_map/all_gather | solution.py:338
  437.4 8.6 multiply_convert_fusion.17
  451.5 4.7 copy.87
  500.5 10.0 collective-permute-done.7
  510.4 14.9 collective-permute-start
  563.7 4.8 collective-permute-start.3
  579.6 29.6 %collective-permute-done.1 = bf16[256,2,512]{0,2,1:T(8,128)(2,1)} collective-permute-done((bf16[256,2,512]{0,2,1:T(8,128)(2,1)S(1)}, bf16[256,2,512]{0,2,1:T(8,128)(2,1)}, u32[]{:S(2)}, u32[]{:S(2)}) %collective-permute-start.1) | collective-permute-done | bytes 524320 | tf_op jit(solution)/shard_map/ppermute | solution.py:17
  640.8 5.5 reduce-scatter.25.cloned.1.call-done
  650.6 8.7 multiply_convert_fusion.16
  664.1 8.7 multiply_convert_fusion.18
  678.4 9.2 reduce-scatter.27.cloned.1.call-done
  691.8 4.8 add_convert_fusion.1
  704.2 5.4 add_convert_fusion.3
  715.1 9.0 reduce-scatter.37.cloned.1.call-done
  746.0 5.0 conditional.120
  753.0 4.8 conditional.121
  759.7 4.8 conditional.123
  767.3 8.3 collective-permute-start.22
  795.9 4.7 conditional.105
  801.4 4.9 conditional.107
  814.9 5.1 collective-permute-start.14
  820.0 5.3 collective-permute-start.15
  825.3 4.8 collective-permute-start.16
  830.2 5.1 collective-permute-start.17
  847.0 5.6 collective-permute-done.16
  852.7 13.6 collective-permute-done.17
  894.6 4.7 reduce-scatter.47.cloned.1.call-done
  899.3 11.9 reduce-scatter.39.cloned.1.call-done
  928.6 5.4 add_convert_fusion.2
  934.1 4.7 fusion.284
  939.0 9.2 reduce-scatter.41.cloned.1.call-done
  965.4 7.8 conditional.127
  973.2 8.3 conditional.111
  1014.3 6.2 maximum_add_fusion.2
  1026.2 4.6 convolution_bitcast_fusion.3
  1030.8 10.5 maximum_add_fusion.1
  1051.4 10.6 maximum_add_fusion
  1067.6 44.7 %all-reduce = (f32[2,6,1024]{2,1,0:T(8,128)S(1)}, f32[2,2,64]{2,1,0:T(2,128)}) all-reduce(f32[2,6,1024]{2,1,0:T(8,128)S(1)} %fusion.388, f32[2,2,64]{2,1,0:T(2,128)S(1)} %constant_dynamic-update-slice_fusion), channel_id=1, replica_groups=mesh['frames'=16,'mp'=2] {'frames','mp'}, use_global_device_ids=true, to_apply=%region_284.285 | all-reduce | flops 12544 | bytes 100352 | tf_op jit(solution)/shard_map/psum | solution.py:393
  1114.5 212.0 %reduce-scatter.53.cloned.1.call-done = f32[2,64,3,512]{3,1,2,0:T(8,128)} async-done(((f32[2,1024,3,512]{3,1,2,0:T(8,128)}), f32[2,64,3,512]{3,1,2,0:T(8,128)}) %reduce-scatter.53.cloned.1.call-update) | async-done | bytes 786448 | tf_op jit(solution)/shard_map/reduce_scatter | solution.py:388
  1326.4 349.7 %reduce-scatter.59.cloned.1.call-done = f32[2,64,2048]{2,1,0:T(8,128)} async-done(((f32[2,1024,2048]{2,1,0:T(8,128)}), f32[2,64,2048]{2,1,0:T(8,128)}) %reduce-scatter.59.cloned.1.call-update) | async-done | bytes 1048592 | tf_op jit(solution)/shard_map/reduce_scatter | solution.py:391
  1676.2 354.8 %reduce-scatter.57.cloned.1.call-done = f32[2,64,2048]{2,1,0:T(8,128)} async-done(((f32[2,1024,2048]{2,1,0:T(8,128)}), f32[2,64,2048]{2,1,0:T(8,128)}) %reduce-scatter.57.cloned.1.call-update) | async-done | bytes 1048592 | tf_op jit(solution)/shard_map/reduce_scatter | solution.py:390
  (1160 shorter events, 531.9 us)
Async XLA Ops:
  7.2 98.8 %all-gather.5.cloned.1.call-start = ((), (), s32[]{:S(2)}) async-start(), calls=%async_computation.20 | async-start | bytes 6684672 | tf_op jit(solution)/shard_map/all_gather | solution.py:335
  7.9 159.9 %all-gather.7.cloned.1.call-start = ((), (), s32[]{:S(2)}) async-start(), calls=%async_computation.21 | async-start | bytes 2228224 | tf_op jit(solution)/shard_map/all_gather | solution.py:336
  8.7 168.8 %reduce-scatter.21.cloned.1.call-start = ((), (), s32[]{:S(2)}) async-start(), calls=%async_computation.22 | async-start | bytes 786432 | tf_op jit(solution)/shard_map/reduce_scatter | solution.py:43
  170.4 32.8 %reduce-scatter.29.cloned.1.call-start = ((), (), s32[]{:S(2)}) async-start(), calls=%async_computation.28 | async-start | bytes 786432 | tf_op jit(solution)/shard_map/reduce_scatter | solution.py:43
  193.9 125.6 %all-gather.9.cloned.1.call-start = ((), (), s32[]{:S(2)}) async-start(), calls=%async_computation.23 | async-start | bytes 8912896 | tf_op jit(solution)/shard_map/all_gather | solution.py:337
  194.5 238.5 %all-gather.11.cloned.1.call-start = ((), (), s32[]{:S(2)}) async-start(), calls=%async_computation.24 | async-start | bytes 8912896 | tf_op jit(solution)/shard_map/all_gather | solution.py:338
  195.1 261.2 %reduce-scatter.23.cloned.1.call-start = ((), (), s32[]{:S(2)}) async-start(), calls=%async_computation.25 | async-start | bytes 786432 | tf_op jit(solution)/shard_map/reduce_scatter | solution.py:43
  437.3 20.7 %reduce-scatter.31.cloned.1.call-start = ((), (), s32[]{:S(2)}) async-start(), calls=%async_computation.29 | async-start | bytes 786432 | tf_op jit(solution)/shard_map/reduce_scatter | solution.py:43
  451.5 189.4 %reduce-scatter.33.cloned.1.call-start = ((), (), s32[]{:S(2)}) async-start(), calls=%async_computation.30 | async-start | bytes 786432 | tf_op jit(solution)/shard_map/reduce_scatter | solution.py:43
  471.1 25.2 %collective-permute-start.6 = (bf16[256,2,512]{0,2,1:T(8,128)(2,1)}, bf16[256,2,512]{0,2,1:T(8,128)(2,1)S(1)}, u32[]{:S(2)}, u32[]{:S(2)}) collective-permute-start(bf16[256,2,512]{0,2,1:T(8,128)(2,1)} %pad_maximum_fusion.21), channel_id=1, source_target_pairs={{0,6},{2,8},{4,10},{6,12},{8,14},{10,16},{12,18},{14,20},{16,22},{... | collective-permute-start | bytes 1572872 | tf_op jit(solution)/shard_map/ppermute | solution.py:17
  483.1 27.3 %collective-permute-start.7 = (bf16[256,2,512]{0,2,1:T(8,128)(2,1)}, bf16[256,2,512]{0,2,1:T(8,128)(2,1)}, u32[]{:S(2)}, u32[]{:S(2)}) collective-permute-start(bf16[256,2,512]{0,2,1:T(8,128)(2,1)} %pad_maximum_fusion.21), channel_id=1, source_target_pairs={{0,4},{2,6},{4,8},{6,10},{8,12},{10,14},{12,16},{14,18},{16,20},{1... | collective-permute-start | bytes 1572872 | tf_op jit(solution)/shard_map/ppermute | solution.py:17
  486.5 42.7 %collective-permute-start.8 = (bf16[256,2,512]{0,2,1:T(8,128)(2,1)}, bf16[256,2,512]{0,2,1:T(8,128)(2,1)}, u32[]{:S(2)}, u32[]{:S(2)}) collective-permute-start(bf16[256,2,512]{0,2,1:T(8,128)(2,1)} %pad_maximum_fusion.21), channel_id=1, source_target_pairs={{0,2},{2,4},{4,6},{6,8},{8,10},{10,12},{12,14},{14,16},{16,18},{18... | collective-permute-start | bytes 1572872 | tf_op jit(solution)/shard_map/ppermute | solution.py:17
  489.0 47.9 %collective-permute-start.9 = (bf16[256,2,512]{0,2,1:T(8,128)(2,1)}, bf16[256,2,512]{0,2,1:T(8,128)(2,1)}, u32[]{:S(2)}, u32[]{:S(2)}) collective-permute-start(bf16[256,2,512]{0,2,1:T(8,128)(2,1)} %pad_maximum_fusion.21), channel_id=1, source_target_pairs={{2,0},{4,2},{6,4},{8,6},{10,8},{12,10},{14,12},{16,14},{18,16},{20... | collective-permute-start | bytes 1572872 | tf_op jit(solution)/shard_map/ppermute | solution.py:17
  493.3 47.5 %collective-permute-start.10 = (bf16[256,2,512]{0,2,1:T(8,128)(2,1)}, bf16[256,2,512]{0,2,1:T(8,128)(2,1)}, u32[]{:S(2)}, u32[]{:S(2)}) collective-permute-start(bf16[256,2,512]{0,2,1:T(8,128)(2,1)} %pad_maximum_fusion.21), channel_id=1, source_target_pairs={{4,0},{6,2},{8,4},{10,6},{12,8},{14,10},{16,12},{18,14},{20,16},{2... | collective-permute-start | bytes 1572872 | tf_op jit(solution)/shard_map/ppermute | solution.py:17
  496.3 44.5 %collective-permute-start.11 = (bf16[256,2,512]{0,2,1:T(8,128)(2,1)}, bf16[256,2,512]{0,2,1:T(8,128)(2,1)}, u32[]{:S(2)}, u32[]{:S(2)}) collective-permute-start(bf16[256,2,512]{0,2,1:T(8,128)(2,1)} %pad_maximum_fusion.21), channel_id=1, source_target_pairs={{6,0},{8,2},{10,4},{12,6},{14,8},{16,10},{18,12},{20,14},{22,16},{... | collective-permute-start | bytes 1572872 | tf_op jit(solution)/shard_map/ppermute | solution.py:17
  510.4 60.0 %collective-permute-start = (bf16[256,2,512]{0,2,1:T(8,128)(2,1)S(1)}, bf16[256,2,512]{0,2,1:T(8,128)(2,1)S(1)}, u32[]{:S(2)}, u32[]{:S(2)}) collective-permute-start(bf16[256,2,512]{0,2,1:T(8,128)(2,1)S(1)} %copy-done.22), channel_id=1, source_target_pairs={{0,6},{2,8},{4,10},{6,12},{8,14},{10,16},{12,18},{14,20},{16,22},{... | collective-permute-start | bytes 1572872 | tf_op jit(solution)/shard_map/ppermute | solution.py:17
  559.8 86.5 %reduce-scatter.25.cloned.1.call-start = ((), (), s32[]{:S(2)}) async-start(), calls=%async_computation.26 | async-start | bytes 786432 | tf_op jit(solution)/shard_map/reduce_scatter | solution.py:43
  559.9 49.3 %collective-permute-start.1 = (bf16[256,2,512]{0,2,1:T(8,128)(2,1)S(1)}, bf16[256,2,512]{0,2,1:T(8,128)(2,1)}, u32[]{:S(2)}, u32[]{:S(2)}) collective-permute-start(bf16[256,2,512]{0,2,1:T(8,128)(2,1)S(1)} %copy-done.22), channel_id=1, source_target_pairs={{0,4},{2,6},{4,8},{6,10},{8,12},{10,14},{12,16},{14,18},{16,20},{1... | collective-permute-start | bytes 1572872 | tf_op jit(solution)/shard_map/ppermute | solution.py:17
  561.8 47.3 %collective-permute-start.2 = (bf16[256,2,512]{0,2,1:T(8,128)(2,1)S(1)}, bf16[256,2,512]{0,2,1:T(8,128)(2,1)}, u32[]{:S(2)}, u32[]{:S(2)}) collective-permute-start(bf16[256,2,512]{0,2,1:T(8,128)(2,1)S(1)} %copy-done.22), channel_id=1, source_target_pairs={{0,2},{2,4},{4,6},{6,8},{8,10},{10,12},{12,14},{14,16},{16,18},{18... | collective-permute-start | bytes 1572872 | tf_op jit(solution)/shard_map/ppermute | solution.py:17
  563.7 52.2 %collective-permute-start.3 = (bf16[256,2,512]{0,2,1:T(8,128)(2,1)S(1)}, bf16[256,2,512]{0,2,1:T(8,128)(2,1)}, u32[]{:S(2)}, u32[]{:S(2)}) collective-permute-start(bf16[256,2,512]{0,2,1:T(8,128)(2,1)S(1)} %copy-done.22), channel_id=1, source_target_pairs={{2,0},{4,2},{6,4},{8,6},{10,8},{12,10},{14,12},{16,14},{18,16},{20... | collective-permute-start | bytes 1572872 | tf_op jit(solution)/shard_map/ppermute | solution.py:17
  568.6 51.2 %collective-permute-start.4 = (bf16[256,2,512]{0,2,1:T(8,128)(2,1)S(1)}, bf16[256,2,512]{0,2,1:T(8,128)(2,1)}, u32[]{:S(2)}, u32[]{:S(2)}) collective-permute-start(bf16[256,2,512]{0,2,1:T(8,128)(2,1)S(1)} %copy-done.22), channel_id=1, source_target_pairs={{4,0},{6,2},{8,4},{10,6},{12,8},{14,10},{16,12},{18,14},{20,16},{2... | collective-permute-start | bytes 1572872 | tf_op jit(solution)/shard_map/ppermute | solution.py:17
  570.5 53.1 %collective-permute-start.5 = (bf16[256,2,512]{0,2,1:T(8,128)(2,1)S(1)}, bf16[256,2,512]{0,2,1:T(8,128)(2,1)S(1)}, u32[]{:S(2)}, u32[]{:S(2)}) collective-permute-start(bf16[256,2,512]{0,2,1:T(8,128)(2,1)S(1)} %copy-done.22), channel_id=1, source_target_pairs={{6,0},{8,2},{10,4},{12,6},{14,8},{16,10},{18,12},{20,14},{22,16},{... | collective-permute-start | bytes 1572872 | tf_op jit(solution)/shard_map/ppermute | solution.py:17
  640.7 37.7 %reduce-scatter.35.cloned.1.call-start = ((), (), s32[]{:S(2)}) async-start(), calls=%async_computation.31 | async-start | bytes 786432 | tf_op jit(solution)/shard_map/reduce_scatter | solution.py:43
  661.5 26.1 %reduce-scatter.27.cloned.1.call-start = ((), (), s32[]{:S(2)}) async-start(), calls=%async_computation.27 | async-start | bytes 786432 | tf_op jit(solution)/shard_map/reduce_scatter | solution.py:43
  678.4 36.8 %reduce-scatter.45.cloned.1.call-start = ((), (), s32[]{:S(2)}) async-start(), calls=%async_computation.36 | async-start | bytes 786432 | tf_op jit(solution)/shard_map/reduce_scatter | solution.py:43
  702.0 22.2 %reduce-scatter.37.cloned.1.call-start = ((), (), s32[]{:S(2)}) async-start(), calls=%async_computation.32 | async-start | bytes 786432 | tf_op jit(solution)/shard_map/reduce_scatter | solution.py:43
  714.9 184.5 %reduce-scatter.47.cloned.1.call-start = ((), (), s32[]{:S(2)}) async-start(), calls=%async_computation.37 | async-start | bytes 786432 | tf_op jit(solution)/shard_map/reduce_scatter | solution.py:43
  744.7 46.0 %collective-permute-start.18 = (bf16[256,2,512]{0,2,1:T(8,128)(2,1)}, bf16[256,2,512]{0,2,1:T(8,128)(2,1)}, u32[]{:S(2)}, u32[]{:S(2)}) collective-permute-start(bf16[256,2,512]{0,2,1:T(8,128)(2,1)} %get-tuple-element.1285), channel_id=1, source_target_pairs={{6,0},{8,2},{10,4},{12,6},{14,8},{16,10},{18,12},{20,14},{22,16},{... | collective-permute-start | bytes 1572872 | tf_op jit(solution)/shard_map/ppermute | solution.py:17
  751.0 41.8 %collective-permute-start.19 = (bf16[256,2,512]{0,2,1:T(8,128)(2,1)}, bf16[256,2,512]{0,2,1:T(8,128)(2,1)}, u32[]{:S(2)}, u32[]{:S(2)}) collective-permute-start(bf16[256,2,512]{0,2,1:T(8,128)(2,1)} %get-tuple-element.1286), channel_id=1, source_target_pairs={{4,0},{6,2},{8,4},{10,6},{12,8},{14,10},{16,12},{18,14},{20,16},{2... | collective-permute-start | bytes 1572872 | tf_op jit(solution)/shard_map/ppermute | solution.py:17
  757.8 55.2 %collective-permute-start.20 = (bf16[256,2,512]{0,2,1:T(8,128)(2,1)}, bf16[256,2,512]{0,2,1:T(8,128)(2,1)}, u32[]{:S(2)}, u32[]{:S(2)}) collective-permute-start(bf16[256,2,512]{0,2,1:T(8,128)(2,1)} %get-tuple-element.1287), channel_id=1, source_target_pairs={{2,0},{4,2},{6,4},{8,6},{10,8},{12,10},{14,12},{16,14},{18,16},{20... | collective-permute-start | bytes 1572872 | tf_op jit(solution)/shard_map/ppermute | solution.py:17
  764.5 50.4 %collective-permute-start.21 = (bf16[256,2,512]{0,2,1:T(8,128)(2,1)}, bf16[256,2,512]{0,2,1:T(8,128)(2,1)}, u32[]{:S(2)}, u32[]{:S(2)}) collective-permute-start(bf16[256,2,512]{0,2,1:T(8,128)(2,1)} %get-tuple-element.1289), channel_id=1, source_target_pairs={{0,2},{2,4},{4,6},{6,8},{8,10},{10,12},{12,14},{14,16},{16,18},{18... | collective-permute-start | bytes 1572872 | tf_op jit(solution)/shard_map/ppermute | solution.py:17
  767.3 52.7 %collective-permute-start.22 = (bf16[256,2,512]{0,2,1:T(8,128)(2,1)}, bf16[256,2,512]{0,2,1:T(8,128)(2,1)}, u32[]{:S(2)}, u32[]{:S(2)}) collective-permute-start(bf16[256,2,512]{0,2,1:T(8,128)(2,1)} %get-tuple-element.1290), channel_id=1, source_target_pairs={{0,4},{2,6},{4,8},{6,10},{8,12},{10,14},{12,16},{14,18},{16,20},{1... | collective-permute-start | bytes 1572872 | tf_op jit(solution)/shard_map/ppermute | solution.py:17
  790.8 34.5 %collective-permute-start.23 = (bf16[256,2,512]{0,2,1:T(8,128)(2,1)}, bf16[256,2,512]{0,2,1:T(8,128)(2,1)}, u32[]{:S(2)}, u32[]{:S(2)}) collective-permute-start(bf16[256,2,512]{0,2,1:T(8,128)(2,1)} %copy-done.161), channel_id=1, source_target_pairs={{0,6},{2,8},{4,10},{6,12},{8,14},{10,16},{12,18},{14,20},{16,22},{... | collective-permute-start | bytes 1572872 | tf_op jit(solution)/shard_map/ppermute | solution.py:17
  792.9 37.3 %collective-permute-start.12 = (bf16[256,2,512]{0,2,1:T(8,128)(2,1)}, bf16[256,2,512]{0,2,1:T(8,128)(2,1)}, u32[]{:S(2)}, u32[]{:S(2)}) collective-permute-start(bf16[256,2,512]{0,2,1:T(8,128)(2,1)} %get-tuple-element.1267), channel_id=1, source_target_pairs={{6,0},{8,2},{10,4},{12,6},{14,8},{16,10},{18,12},{20,14},{22,16},{... | collective-permute-start | bytes 1572872 | tf_op jit(solution)/shard_map/ppermute | solution.py:17
  813.0 34.0 %collective-permute-start.13 = (bf16[256,2,512]{0,2,1:T(8,128)(2,1)}, bf16[256,2,512]{0,2,1:T(8,128)(2,1)}, u32[]{:S(2)}, u32[]{:S(2)}) collective-permute-start(bf16[256,2,512]{0,2,1:T(8,128)(2,1)} %get-tuple-element.1268), channel_id=1, source_target_pairs={{4,0},{6,2},{8,4},{10,6},{12,8},{14,10},{16,12},{18,14},{20,16},{2... | collective-permute-start | bytes 1572872 | tf_op jit(solution)/shard_map/ppermute | solution.py:17
  814.9 32.1 %collective-permute-start.14 = (bf16[256,2,512]{0,2,1:T(8,128)(2,1)}, bf16[256,2,512]{0,2,1:T(8,128)(2,1)}, u32[]{:S(2)}, u32[]{:S(2)}) collective-permute-start(bf16[256,2,512]{0,2,1:T(8,128)(2,1)} %get-tuple-element.1269), channel_id=1, source_target_pairs={{2,0},{4,2},{6,4},{8,6},{10,8},{12,10},{14,12},{16,14},{18,16},{20... | collective-permute-start | bytes 1572872 | tf_op jit(solution)/shard_map/ppermute | solution.py:17
  820.0 27.0 %collective-permute-start.15 = (bf16[256,2,512]{0,2,1:T(8,128)(2,1)}, bf16[256,2,512]{0,2,1:T(8,128)(2,1)}, u32[]{:S(2)}, u32[]{:S(2)}) collective-permute-start(bf16[256,2,512]{0,2,1:T(8,128)(2,1)} %get-tuple-element.1271), channel_id=1, source_target_pairs={{0,2},{2,4},{4,6},{6,8},{8,10},{10,12},{12,14},{14,16},{16,18},{18... | collective-permute-start | bytes 1572872 | tf_op jit(solution)/shard_map/ppermute | solution.py:17
  825.3 27.3 %collective-permute-start.16 = (bf16[256,2,512]{0,2,1:T(8,128)(2,1)}, bf16[256,2,512]{0,2,1:T(8,128)(2,1)}, u32[]{:S(2)}, u32[]{:S(2)}) collective-permute-start(bf16[256,2,512]{0,2,1:T(8,128)(2,1)} %copy-done.162), channel_id=1, source_target_pairs={{0,4},{2,6},{4,8},{6,10},{8,12},{10,14},{12,16},{14,18},{16,20},{1... | collective-permute-start | bytes 1572872 | tf_op jit(solution)/shard_map/ppermute | solution.py:17
  830.2 36.1 %collective-permute-start.17 = (bf16[256,2,512]{0,2,1:T(8,128)(2,1)}, bf16[256,2,512]{0,2,1:T(8,128)(2,1)}, u32[]{:S(2)}, u32[]{:S(2)}) collective-permute-start(bf16[256,2,512]{0,2,1:T(8,128)(2,1)} %get-tuple-element.1273), channel_id=1, source_target_pairs={{0,6},{2,8},{4,10},{6,12},{8,14},{10,16},{12,18},{14,20},{16,22},{... | collective-permute-start | bytes 1572872 | tf_op jit(solution)/shard_map/ppermute | solution.py:17
  887.9 23.4 %reduce-scatter.39.cloned.1.call-start = ((), (), s32[]{:S(2)}) async-start(), calls=%async_computation.33 | async-start | bytes 786432 | tf_op jit(solution)/shard_map/reduce_scatter | solution.py:43
  894.6 44.4 %reduce-scatter.49.cloned.1.call-start = ((), (), s32[]{:S(2)}) async-start(), calls=%async_computation.38 | async-start | bytes 786432 | tf_op jit(solution)/shard_map/reduce_scatter | solution.py:43
  926.0 22.1 %reduce-scatter.41.cloned.1.call-start = ((), (), s32[]{:S(2)}) async-start(), calls=%async_computation.34 | async-start | bytes 786432 | tf_op jit(solution)/shard_map/reduce_scatter | solution.py:43
  938.9 125.3 %reduce-scatter.51.cloned.1.call-start = ((), (), s32[]{:S(2)}) async-start(), calls=%async_computation.39 | async-start | bytes 786432 | tf_op jit(solution)/shard_map/reduce_scatter | solution.py:43
  995.0 69.3 %reduce-scatter.43.cloned.1.call-start = ((), (), s32[]{:S(2)}) async-start(), calls=%async_computation.35 | async-start | bytes 786432 | tf_op jit(solution)/shard_map/reduce_scatter | solution.py:43
  1000.0 114.5 %reduce-scatter.55.cloned.1.call-start = ((), (), s32[]{:S(2)}) async-start(), calls=%async_computation.41 | async-start | bytes 4456448 | tf_op jit(solution)/shard_map/reduce_scatter | solution.py:389
  1006.9 319.6 %reduce-scatter.53.cloned.1.call-start = ((), (), s32[]{:S(2)}) async-start(), calls=%async_computation.40 | async-start | bytes 13369344 | tf_op jit(solution)/shard_map/reduce_scatter | solution.py:388
  1020.6 655.6 %reduce-scatter.59.cloned.1.call-start = ((), (), s32[]{:S(2)}) async-start(), calls=%async_computation.43 | async-start | bytes 17825792 | tf_op jit(solution)/shard_map/reduce_scatter | solution.py:391
  1041.4 989.6 %reduce-scatter.57.cloned.1.call-start = ((), (), s32[]{:S(2)}) async-start(), calls=%async_computation.42 | async-start | bytes 17825792 | tf_op jit(solution)/shard_map/reduce_scatter | solution.py:390
  (285 other events, 5569.6 us)
Sparse Core Ops, SparseCore 0:
  10.8 95.1 all-gather.4
  108.8 59.0 all-gather.6
  170.7 6.7 reduce-scatter.20
  194.0 9.1 reduce-scatter.28
  205.8 113.6 all-gather.8
  322.1 110.9 all-gather.10
  437.4 6.3 reduce-scatter.22
  451.6 6.3 reduce-scatter.30
  559.9 5.4 reduce-scatter.32
  640.9 5.4 reduce-scatter.24
  661.6 9.1 reduce-scatter.34
  678.5 9.1 reduce-scatter.26
  702.1 9.1 reduce-scatter.44
  715.0 9.1 reduce-scatter.36
  888.0 11.3 reduce-scatter.46
  902.1 9.1 reduce-scatter.38
  926.1 9.0 reduce-scatter.48
  939.0 9.0 reduce-scatter.40
  995.1 9.1 reduce-scatter.50
  1006.5 9.0 reduce-scatter.42
  1018.5 95.1 reduce-scatter.54
  1119.9 206.4 reduce-scatter.52
  1329.4 346.7 reduce-scatter.58
  1679.0 351.9 reduce-scatter.56
where the time goes:
time: 2050 us; the launch traced here: 2040 us
  waiting for transfers between devices  1390 us (68%)
  matrix products  217 us (11%)
  other arithmetic  122 us (6%)
  local copies, waits for them, and re-layouts  105 us (5%)
  starting transfers between devices  86.9 us (4%)
  blocking collectives  81.9 us (4%)
  between operations  36.4 us (2%)
    reduce_scatter x1, waiting for transfers between devices, body(): lax.psum_scatter(full_total[2], 'frames', scatter_dimension=1, tiled=True)  355 us
    reduce_scatter x1, waiting for transfers between devices, body(): lax.psum_scatter(full_total[3], 'frames', scatter_dimension=1, tiled=True)  350 us
    reduce_scatter x1, waiting for transfers between devices, body(): lax.psum_scatter(full_total[0], 'frames', scatter_dimension=1, tiled=True)  212 us
    all_gather x1, waiting for transfers between devices, body(): lax.all_gather(shards[2], 'frames', axis=1, tiled=True)  108 us
    all_gather x1, waiting for transfers between devices, body(): lax.all_gather(shards[3], 'frames', axis=1, tiled=True)  105 us
    all_gather x1, waiting for transfers between devices, body(): lax.all_gather(shards[0], 'frames', axis=1, tiled=True)  87.1 us
    ppermute x24, starting transfers between devices, from_behind(): return lax.ppermute(block, axis, route)  85.3 us
    reduce_scatter x16, waiting for transfers between devices, row_products(): lax.psum_scatter(jnp.einsum(pattern, left_rows, weight, preferred_element...  65.1 us
  transfers between devices with their start and end apart: 48, of which 20 were waited for; matrix products, arithmetic and copies ran while one was open for 14% of the time, Pallas kernels for 0%

commit v1 on v0

v1 whole, which is shorter than its diff:
```python
import functools

import jax
import jax.numpy as jnp
import numpy as np
from jax import lax
from jax.experimental import pallas as pl
from jax.experimental.pallas import tpu as pltpu
from jax.sharding import PartitionSpec as P

BF = jnp.bfloat16
F32 = jnp.float32
ROW_EPS = 1e-06
HEAD_EPS = 1e-05
PIECES = 16
SWAPS = 1
COST = 1
PLANE = 4
REACH = 3
AXES = ("frames", "mp")

NN = (((1,), (0,)), ((), ()))
NT = (((1,), (1,)), ((), ()))
TN = (((0,), (0,)), ((), ()))

VM = pl.BlockSpec(memory_space=pltpu.VMEM)
SM = pl.BlockSpec(memory_space=pltpu.SMEM)
ANY = pl.BlockSpec(memory_space=pl.ANY)


def dot(left, right, dims=NN):
    return lax.dot_general(left, right, dims, preferred_element_type=F32)


def call(body, outs, in_specs, out_specs, scratch, flops, moved, name):
    return pl.pallas_call(
        body,
        out_shape=outs,
        in_specs=in_specs,
        out_specs=out_specs,
        scratch_shapes=scratch,
        compiler_params=pltpu.CompilerParams(vmem_limit_bytes=60 * 1024 * 1024),
        cost_estimate=pl.CostEstimate(flops=flops // COST, bytes_accessed=moved // COST, transcendentals=0),
        name=name,
    )


class Routes:
    def __init__(self, n):
        lines = n // PLANE
        self.n, self.lines = n, lines
        order = [0] + list(range(1, lines, 2)) + sorted(range(2, lines, 2), reverse=True)
        following = {z: order[(i + 1) % lines] for i, z in enumerate(order)}
        spot = {z: i for i, z in enumerate(order)}
        self.back = np.array([[order[(spot[z] - k) % lines] for z in range(lines)] for k in range(lines)], np.int32)
        self.steps = np.array([[(spot[z] - spot[w]) % lines for w in range(lines)] for z in range(lines)], np.int32)
        self.ring = [
            (f * 2 + c, (following[f // PLANE] * PLANE + f % PLANE) * 2 + c) for f in range(n) for c in range(2)
        ]
        self.one = [(f * 2 + c, (f ^ (1 + c)) * 2 + c) for f in range(n) for c in range(2)]
        self.two = [(f * 2 + c, (f ^ (2 - c)) * 2 + c) for f in range(n) for c in range(2)]

    def send(self, block, route):
        return lax.ppermute(block, AXES, route)

    def swap(self, block):
        return lax.ppermute(block, "mp", [(0, 1), (1, 0)])

    def swap_parts(self, block):
        rows = block.shape[0] // SWAPS
        return jnp.concatenate([self.swap(block[i * rows : (i + 1) * rows]) for i in range(SWAPS)])

    def member(self, block, distance):
        return lax.ppermute(block, "frames", [(f, f ^ distance) for f in range(self.n)])

    def members(self, blocks):
        return [blocks[0]] + [self.member(blocks[d], d) for d in range(1, PLANE)]

    def up(self, block):
        return lax.ppermute(block, "frames", [(f, f + PLANE) for f in range(self.n - PLANE)])

    def down(self, block):
        return lax.ppermute(block, "frames", [(f + PLANE, f) for f in range(self.n - PLANE)])

    def tables(self):
        frame, core = lax.axis_index("frames"), lax.axis_index("mp")
        low, high = 1 + core, 2 - core
        bits = jnp.arange(2, dtype=jnp.int32)
        line = PLANE * jnp.asarray(self.back)[:, frame // PLANE]
        near = ((frame // low) % 2 ^ bits) * low
        far = ((frame // high) % 2 ^ bits) * high
        middle = line[None, :, None] + near[None, None, :] + far[:, None, None]
        first = line[None, None, :] + near[None, :, None] + far[:, None, None]
        every = jnp.arange(self.n, dtype=jnp.int32)
        k = jnp.repeat(jnp.asarray(self.steps)[frame // PLANE], PLANE)
        j = (every // low) % 2 ^ (frame // low) % 2
        h = (every // high) % 2 ^ (frame // high) % 2
        half = self.n // 2
        place_middle = h * half + k * 2 + j
        place_first = h * half + j * self.lines + k
        return [t.reshape(-1).astype(jnp.int32) for t in (middle, first, place_middle, place_first)]

    def total(self, block):
        block = block + self.swap(block)
        distance = 1
        while distance < self.n:
            block = block + self.member(block, distance)
            distance *= 2
        return block


class Clock:
    def __init__(self, active):
        self.active, self.waited = active, []

    def wait(self, *values):
        self.waited = (self.waited + list(values))[-6:]

    def late(self, value):
        if not (self.active and self.waited):
            return value
        return lax.optimization_barrier((value, self.waited))[0]


class Gather:
    def __init__(self, routes, clock, shard, line_first, name):
        self.routes, self.clock, self.near, self.line_first, self.name = routes, clock, shard, line_first, name

    def line(self):
        with jax.named_scope(self.name + "_line"):
            source = self.clock.late(self.near)
            pieces = [source]
            for _ in range(1, self.routes.lines):
                pieces.append(self.routes.send(pieces[-1], self.routes.ring))
            self.near = jnp.stack(pieces) if self.line_first else jnp.concatenate(pieces)

    def one(self):
        with jax.named_scope(self.name + "_one"):
            source = self.clock.late(self.near)
            got = self.routes.send(source, self.routes.one)
            self.near = jnp.concatenate([source, got]) if self.line_first else jnp.stack([source, got])

    def two(self):
        with jax.named_scope(self.name + "_two"):
            self.near = self.clock.late(self.near)
            self.far = self.routes.send(self.near, self.routes.two)

    def wait(self):
        self.clock.wait(self.near)

    def end(self):
        self.clock.wait(self.far)
        return self.near, self.far


class Scatter:
    def __init__(self, routes, clock, pair, line_last, name):
        self.routes, self.clock, self.line_last, self.name = routes, clock, line_last, name
        keep, give = pair
        self.shape = ((2, routes.lines) if line_last else (routes.lines, 2)) + keep.shape[1:]
        self.keep, self.give = keep.reshape(self.shape), give

    def wait(self):
        self.clock.wait(*self.last)

    def two(self):
        with jax.named_scope(self.name + "_two"):
            give = self.clock.late(self.give)
            got = self.routes.send(give, self.routes.two)
            self.last = [got]
            self.got = got.reshape(self.shape)

    def pair(self, *index):
        return self.keep[index].astype(F32) + self.got[index].astype(F32)

    def one(self):
        with jax.named_scope(self.name + "_one"):
            block = self.pair(1).astype(BF) if self.line_last else self.run[1].astype(BF)
            self.more = self.routes.send(self.clock.late(block), self.routes.one)
            self.last = [self.more]
            if not self.line_last:
                self.run = self.run[0] + self.more.astype(F32)

    def local(self, k):
        return self.pair(0, k) + self.more[k].astype(F32) if self.line_last else self.pair(k)

    def line(self):
        with jax.named_scope(self.name + "_line"):
            lines = self.routes.lines
            run = self.local(1 % lines)
            for k in range(1, lines):
                block = run.astype(BF)
                got = self.routes.send(self.clock.late(block) if k == 1 else block, self.routes.ring)
                run = self.local((k + 1) % lines) + got.astype(F32)
            self.last = [got]
            self.run = run


class Whole:
    def __init__(self, value):
        self.run = self.give = value

    def line(self):
        pass

    one = two = wait = line

    def end(self):
        return self.run


def fetch(meta, base, near, far, into, sems):
    half, rows = near.shape[0], near.shape[1]
    copies = []
    for side, source in ((0, near), (1, far)):
        for p in range(half):
            q = side * half + p
            row = pl.multiple_of(meta[base + q] * rows, rows)
            copy = pltpu.make_async_copy(source.at[p], into.at[pl.ds(row, rows), :], sems.at[q])
            copy.start()
            copies.append(copy)
    return copies


def finish(copies):
    for copy in copies:
        copy.wait()


def norm_parts(values):
    centred = values - jnp.mean(values, axis=-1, keepdims=True)
    scale = lax.rsqrt(jnp.mean(centred * centred, axis=-1, keepdims=True) + ROW_EPS)
    return centred * scale, scale


def head_matrix(width, head):
    row = lax.broadcasted_iota(jnp.int32, (width, width), 0) // head
    column = lax.broadcasted_iota(jnp.int32, (width, width), 1) // head
    return jnp.where(row == column, 1.0 / head, 0.0).astype(BF)


def head_mean(values, matrix):
    high = values.astype(BF)
    low = (values - high.astype(F32)).astype(BF)
    return dot(high, matrix) + dot(low, matrix)


def head_parts(values, matrix):
    centred = values - head_mean(values, matrix)
    scale = lax.rsqrt(head_mean(centred * centred, matrix) + HEAD_EPS)
    return centred * scale, scale


def project(normed, weight, gains, matrix, put, rows=256, lanes=256):
    width = gains.shape[1]
    total = normed.shape[0]
    factor = HEAD_SCALE

    for part in range(3):
        for start in range(0, width, lanes):
            columns = part * width + start

            @pl.loop(0, total // rows)
            def _(i):
                r = pl.ds(pl.multiple_of(i * rows, rows), rows)
                values = dot(normed[r, :], weight[:, columns : columns + lanes])
                if part < 2:
                    unit, _ = head_parts(values, matrix)
                    values = unit * gains[part : part + 1, start : start + lanes]
                values = values.astype(BF)
                if part == 0:
                    values = (values.astype(F32) * factor).astype(BF)
                put(part, r, start, lanes, values)


HEAD_SCALE = 0.125


def only_first(values):
    lane = lax.broadcasted_iota(jnp.int32, values.shape, 1)
    return jnp.where(lane < values.shape[1] // 2, values, jnp.zeros_like(values))


def only_second(values):
    lane = lax.broadcasted_iota(jnp.int32, values.shape, 1)
    return jnp.where(lane < values.shape[1] // 2, jnp.zeros_like(values), values)


def pick(first, second):
    lane = lax.broadcasted_iota(jnp.int32, first.shape, 1)
    return jnp.where(lane < first.shape[1] // 2, first, second)


def gelu_parts(v):
    size = jnp.abs(v)
    bell = jnp.exp(v * v * -0.5)
    t = 1.0 / (1.0 + size * 0.23164189)
    tail = t * (0.127414796 + t * (-0.142248368 + t * (0.7107068705 + t * (-0.7265760135 + t * 0.5307027145))))
    tail = tail * bell
    phi = jnp.where(v >= 0.0, 1.0 - tail, tail)
    return v * phi, phi + v * bell * 0.3989422804014327


def attention_frame_kernel(frame, head, meta, rows_ref, near, far, norms, gains, normed, qkv, attended, part, weight, sems):
    copies = fetch(meta, PIECES, near, far, weight, sems)
    total, model = rows_ref.shape
    width = gains.shape[1]

    @pl.loop(0, total // 64)
    def _(i):
        r = pl.ds(pl.multiple_of(i * 64, 64), 64)
        unit, _ = norm_parts(rows_ref[r, :].astype(F32))
        normed[r, :] = (unit * norms[0:1, :] + norms[1:2, :]).astype(BF)

    finish(copies)
    matrix = head_matrix(256, head)

    def put(part, r, start, lanes, values):
        qkv[part, r, start : start + lanes] = values

    project(normed, weight, gains, matrix, put)
    pairs = width // 128

    @pl.loop(0, (total // frame) * pairs)
    def _(i):
        r = pl.ds(pl.multiple_of((i // pairs) * frame, frame), frame)
        lanes = pl.ds(pl.multiple_of((i % pairs) * 128, 128), 128)
        q, k, v = qkv[0, r, lanes], qkv[1, r, lanes], qkv[2, r, lanes]
        found = []
        for mask in (only_first, only_second):
            weights = jnp.exp(dot(mask(q), k, NT))
            found.append(dot(weights.astype(BF), v) / jnp.sum(weights, axis=-1, keepdims=True))
        attended[r, lanes] = pick(found[0], found[1]).astype(BF)

    for start in range(0, model, 256):
        part[:, start : start + 256] = dot(
            attended[...], weight[start : start + 256, 3 * width : 4 * width], NT
        ).astype(BF)


def attention_frame(meta, rows, near, far, norms, gains, frame, head):
    total, model = rows.shape
    width = gains.shape[1]
    return call(
        functools.partial(attention_frame_kernel, frame, head),
        (
            jax.ShapeDtypeStruct((total, model), BF),
            jax.ShapeDtypeStruct((3, total, width), BF),
            jax.ShapeDtypeStruct((total, width), BF),
            jax.ShapeDtypeStruct((total, model), BF),
        ),
        [SM, VM, ANY, ANY, VM, VM],
        (VM, VM, VM, VM),
        [pltpu.VMEM((model, 4 * width), BF), pltpu.SemaphoreType.DMA((PIECES,))],
        8 * total * model * width,
        2 * 4 * model * width,
        "attention_frame",
    )(meta, rows, near, far, norms, gains)


def feed_up_kernel(meta, x, one, two, un, uf, norms, mid, normed, active, slope, up, sems):
    copies = fetch(meta, PIECES, un, uf, up, sems)
    total, model = x.shape
    hidden = up.shape[1]

    @pl.loop(0, total // 64)
    def _(i):
        r = pl.ds(pl.multiple_of(i * 64, 64), 64)
        branch = one[r, :].astype(F32) + two[r, :].astype(F32)
        values = x[r, :].astype(F32) + norms[2:3, :] * branch
        mid[r, :] = values
        unit, _ = norm_parts(values)
        normed[r, :] = (unit * norms[3:4, :] + norms[4:5, :]).astype(BF)

    finish(copies)
    step, rows = 512, 256
    for start in range(0, hidden, step):

        @pl.loop(0, total // rows)
        def _(i):
            r = pl.ds(pl.multiple_of(i * rows, rows), rows)
            before = dot(normed[r, :], up[:, start : start + step])
            after_, rise = gelu_parts(before)
            active[r, start : start + step] = after_.astype(BF)
            slope[r, start : start + step] = rise.astype(BF)


def feed_up(meta, x, one, two, up, norms):
    total, model = x.shape
    hidden = up[0].shape[2]
    return call(
        feed_up_kernel,
        (
            jax.ShapeDtypeStruct((total, model), F32),
            jax.ShapeDtypeStruct((total, model), BF),
            jax.ShapeDtypeStruct((total, hidden), BF),
            jax.ShapeDtypeStruct((total, hidden), BF),
        ),
        [SM, VM, VM, VM, ANY, ANY, VM],
        (VM,) * 4,
        [pltpu.VMEM((model, hidden), BF), pltpu.SemaphoreType.DMA((PIECES,))],
        2 * total * model * hidden,
        2 * model * hidden,
        "feed_up",
    )(meta, x, one, two, *up, norms)


def feed_down_kernel(meta, active, dn, df, part, down, sems):
    model = part.shape[1]
    finish(fetch(meta, 0, dn, df, down, sems))
    for start in range(0, model, 256):
        part[:, start : start + 256] = dot(active[...], down[start : start + 256, :], NT).astype(BF)


def feed_down(meta, active, down):
    total, hidden = active.shape
    model = down[0].shape[1] * PIECES
    return call(
        feed_down_kernel,
        jax.ShapeDtypeStruct((total, model), BF),
        [SM, VM, ANY, ANY],
        VM,
        [pltpu.VMEM((model, hidden), BF), pltpu.SemaphoreType.DMA((PIECES,))],
        2 * total * model * hidden,
        2 * model * hidden,
        "feed_down",
    )(meta, active, *down)


def queries_kernel(head, meta, mid, one, two, near, far, before, norms, gains, x, normed, s0, s1, s2, s3, weight, held, sems):
    copies = fetch(meta, PIECES, near, far, weight, sems)
    total, model = mid.shape
    width = gains.shape[1]
    me = meta[META_ME]

    @pl.loop(0, total // 64)
    def _(i):
        r = pl.ds(pl.multiple_of(i * 64, 64), 64)
        values = mid[r, :] + before[5:6, :] * (one[r, :].astype(F32) + two[r, :].astype(F32))
        x[r, :] = values
        unit, _ = norm_parts(values)
        normed[r, :] = (unit * norms[0:1, :] + norms[1:2, :]).astype(BF)

    finish(copies)

    def put(part, r, start, lanes, values):
        held[part, r, start : start + lanes] = values

    project(normed, weight, gains, head_matrix(256, head), put)
    for d, slot in enumerate((s0, s1, s2, s3)):
        lanes = pl.ds(pl.multiple_of((me ^ d) * 128, 128), 128)
        for part in range(3):
            slot[part] = held[part, :, lanes]


def queries(meta, mid, one, two, near, far, before, norms, gains, head):
    total, model = mid.shape
    width = gains.shape[1]
    slot = jax.ShapeDtypeStruct((3, total, 128), BF)
    return call(
        functools.partial(queries_kernel, head),
        (jax.ShapeDtypeStruct((total, model), F32), jax.ShapeDtypeStruct((total, model), BF)) + (slot,) * 4,
        [SM, VM, VM, VM, ANY, ANY, VM, VM, VM],
        (VM,) * 6,
        [
            pltpu.VMEM((model, 4 * width), BF),
            pltpu.VMEM((3, total, width), BF),
            pltpu.SemaphoreType.DMA((PIECES,)),
        ],
        6 * total * model * width,
        8 * model * width,
        "queries",
    )(meta, mid, one, two, near, far, before, norms, gains)


def edge_kernel(meta, s0, s1, s2, s3, rise, fall):
    me = meta[META_ME]
    for d, slot in enumerate((s0, s1, s2, s3)):
        j = me ^ d

        @pl.when(j >= 1)
        def _():
            rise[jnp.maximum(j - 1, 0)] = slot[1:3]

        @pl.when(j <= REACH - 1)
        def _():
            fall[jnp.minimum(j, REACH - 1)] = slot[1:3]


def edges(meta, slots):
    total = slots[0].shape[1]
    out = jax.ShapeDtypeStruct((REACH, 2, total, 128), BF)
    return call(edge_kernel, (out, out), [SM] + [VM] * 4, (VM, VM), [], 0, 4 * REACH * 2 * total * 128 * 2, "edges")(
        meta, *slots
    )


def load_window(meta, slots, below, above, own, window, sems):
    me = meta[META_ME]
    copies = []
    for d, slot in enumerate(slots):
        j = me ^ d
        copies.append(pltpu.make_async_copy(slot.at[0], own.at[j], sems.at[0, d]))
        copies.append(pltpu.make_async_copy(slot.at[pl.ds(1, 2)], window.at[REACH + j], sems.at[1, d]))
    for k in range(REACH):
        copies.append(pltpu.make_async_copy(below.at[k], window.at[k], sems.at[2, k]))
        copies.append(pltpu.make_async_copy(above.at[k], window.at[REACH + PLANE + k], sems.at[3, k]))
    for copy in copies:
        copy.start()
    return copies


def scene_kernel(frame, meta, s0, s1, s2, s3, below, above, o0, o1, o2, o3, sums, found, own, window, held, sems):
    finish(load_window(meta, (s0, s1, s2, s3), below, above, own, window, sems))
    me = meta[META_ME]
    total = own.shape[1]
    parts = total // frame

    @pl.loop(0, parts * PLANE)
    def _(i):
        m, j = i // PLANE, i % PLANE
        r = pl.ds(pl.multiple_of(m * frame, frame), frame)
        q = own[j, r, :]
        first, second = only_first(q), only_second(q)
        held[...] = jnp.zeros_like(held)

        @pl.loop(meta[META_SCENES + i * 2], meta[META_SCENES + i * 2 + 1])
        def _(w):
            k, v = window[w, 0, r, :], window[w, 1, r, :]
            one = jnp.exp(dot(first, k, NT))
            two = jnp.exp(dot(second, k, NT))
            held[0] += pick(dot(one.astype(BF), v), dot(two.astype(BF), v))
            for h, weights in ((1, one), (2, two)):
                tally = weights[:, 0:128]
                for start in range(128, frame, 128):
                    tally = tally + weights[:, start : start + 128]
                held[h] += tally

        lane = pick(
            jnp.broadcast_to(jnp.sum(held[1], axis=-1, keepdims=True), (frame, 128)),
            jnp.broadcast_to(jnp.sum(held[2], axis=-1, keepdims=True), (frame, 128)),
        )
        inverse = 1.0 / lane
        sums[j, r, :] = inverse
        found[j, r, :] = held[0] * inverse

    for d, out in enumerate((o0, o1, o2, o3)):
        out[...] = found[me ^ d].astype(BF)


def scene(meta, slots, below, above, frame):
    total = slots[0].shape[1]
    out = jax.ShapeDtypeStruct((total, 128), BF)
    wide = 2 * REACH + PLANE
    return call(
        functools.partial(scene_kernel, frame),
        (out,) * 4 + (jax.ShapeDtypeStruct((PLANE, total, 128), F32),) * 2,
        [SM] + [ANY] * 6,
        (VM,) * 6,
        [
            pltpu.VMEM((PLANE, total, 128), BF),
            pltpu.VMEM((wide, 2, total, 128), BF),
            pltpu.VMEM((3, frame, 128), F32),
            pltpu.SemaphoreType.DMA((4, PLANE)),
        ],
        4 * PLANE * total * PLANE * frame * 128 * 2,
        4 * wide * total * 128,
        "scene",
    )(meta, *slots, below, above)


def output_kernel(meta, o0, o1, o2, o3, near, far, attended, part, weight, sems):
    copies = fetch(meta, PIECES, near, far, weight, sems)
    me = meta[META_ME]
    width = attended.shape[1]
    model = part.shape[1]
    for d, slot in enumerate((o0, o1, o2, o3)):
        attended[:, pl.ds(pl.multiple_of((me ^ d) * 128, 128), 128)] = slot[...]
    finish(copies)
    for start in range(0, model, 256):
        part[:, start : start + 256] = dot(attended[...], weight[start : start + 256, :], NT).astype(BF)


def outputs(meta, slots, near, far, width):
    total = slots[0].shape[0]
    model = near.shape[1] * PIECES
    return call(
        output_kernel_narrow(width),
        (jax.ShapeDtypeStruct((total, width), BF), jax.ShapeDtypeStruct((total, model), BF)),
        [SM] + [VM] * 4 + [ANY, ANY],
        (VM, VM),
        [pltpu.VMEM((model, width), BF), pltpu.SemaphoreType.DMA((PIECES,))],
        2 * total * model * width,
        2 * model * width,
        "outputs",
    )(meta, *slots, near, far)


def output_kernel_narrow(width):
    def body(meta, o0, o1, o2, o3, near, far, *rest):
        columns = pl.ds(3 * width, width)
        output_kernel(meta, o0, o1, o2, o3, near.at[:, :, columns], far.at[:, :, columns], *rest)

    return body


def feed_back_kernel(meta, g, slope, un, uf, dn, df, norms, d_mlp, d_hidden, part, up, down, sems):
    copies = fetch(meta, 0, dn, df, down, sems.at[0])
    later = fetch(meta, PIECES, un, uf, up, sems.at[1])
    total, model = g.shape
    hidden = up.shape[1]

    @pl.loop(0, total // 64)
    def _(i):
        r = pl.ds(pl.multiple_of(i * 64, 64), 64)
        d_mlp[r, :] = (g[r, :].astype(F32) * norms[5:6, :]).astype(BF)

    finish(copies)
    step = 256
    for start in range(0, hidden, step):
        d_active = dot(d_mlp[...], down[:, start : start + step])
        d_hidden[:, start : start + step] = (d_active * slope[:, start : start + step].astype(F32)).astype(BF)
    finish(later)
    for start in range(0, model, 256):
        part[:, start : start + 256] = dot(d_hidden[...], up[start : start + 256, :], NT).astype(BF)


def feed_back(meta, g, slope, up, down, norms):
    total, model = g.shape
    hidden = slope.shape[1]
    return call(
        feed_back_kernel,
        (
            jax.ShapeDtypeStruct((total, model), BF),
            jax.ShapeDtypeStruct((total, hidden), BF),
            jax.ShapeDtypeStruct((total, model), BF),
        ),
        [SM, VM, VM, ANY, ANY, ANY, ANY, VM],
        (VM,) * 3,
        [
            pltpu.VMEM((model, hidden), BF),
            pltpu.VMEM((model, hidden), BF),
            pltpu.SemaphoreType.DMA((2, PIECES)),
        ],
        4 * total * model * hidden,
        8 * model * hidden,
        "feed_back",
    )(meta, g, slope, *up, *down, norms)


def weight_grad_kernel(base, widths, meta, *refs):
    count = len(widths)
    lefts, rights = refs[:count], refs[count : 2 * count]
    keep, give, staged, sems = refs[2 * count :]
    half, rows = keep.shape[0], keep.shape[1]
    model = lefts[0].shape[1]
    block = 256
    per = block // rows

    def copy_out(b, act):
        slot = b % 2
        for s in range(per):
            place = meta[base + b * per + s]
            source = staged.at[slot, pl.ds(s * rows, rows), :]

            @pl.when(place < half)
            def _():
                getattr(pltpu.make_async_copy(source, keep.at[jnp.minimum(place, half - 1)], sems.at[slot, s]), act)()

            @pl.when(place >= half)
            def _():
                getattr(pltpu.make_async_copy(source, give.at[jnp.maximum(place - half, 0)], sems.at[slot, s]), act)()

    for b in range(model // block):
        if b >= 2:
            copy_out(b - 2, "wait")
        start = 0
        for left, right, width in zip(lefts, rights, widths):
            staged[b % 2, :, start : start + width] = dot(
                left[:, b * block : (b + 1) * block], right[...], TN
            ).astype(BF)
            start += width
        copy_out(b, "start")
    for b in range(max(0, model // block - 2), model // block):
        copy_out(b, "wait")


def weight_grad(meta, base, lefts, rights, name):
    widths = [right.shape[1] for right in rights]
    total, model = lefts[0].shape
    rows = model // PIECES
    wide = sum(widths)
    out = jax.ShapeDtypeStruct((PIECES // 2, rows, wide), BF)
    return call(
        functools.partial(weight_grad_kernel, base, widths),
        (out, out),
        [SM] + [VM] * (2 * len(widths)),
        (ANY, ANY),
        [pltpu.VMEM((2, 256, wide), BF), pltpu.SemaphoreType.DMA((2, 256 // rows))],
        2 * total * model * wide,
        2 * model * wide + 2 * total * (model + wide),
        name,
    )(meta, *lefts, *rights)


def norm_back_kernel(frame, count, meta, *refs):
    inner = count > 2
    g, x, one, two, norms = refs[:5]
    if inner:
        pa, pb = refs[5:7]
        ma, mb = refs[7:9] if count > 3 else (None, None)
        out, d_branch, sums, tally = refs[-4:]
        gain = norms[3:4, :]
    else:
        out, sums, tally = refs[-3:]
        gain = norms[0:1, :]
    total, model = x.shape
    core = meta[META_CORE]
    rows = 64
    tally[...] = jnp.zeros_like(tally)

    @pl.loop(0, total // rows)
    def _(i):
        r = pl.ds(pl.multiple_of(i * rows, rows), rows)
        unit, scale = norm_parts(x[r, :].astype(F32))
        d = one[r, :].astype(F32) + two[r, :].astype(F32)
        dg = d * gain
        mean = jnp.mean(dg, axis=-1, keepdims=True)
        slant = jnp.mean(dg * unit, axis=-1, keepdims=True)
        before = g[r, :].astype(F32)
        after = before + scale * (dg - mean - unit * slant)
        out[r, :] = after
        if inner:
            d_branch[r, :] = (after * norms[2:3, :]).astype(BF)

        @pl.when((i // (frame // 2 // rows)) % 2 == core)
        def _():
            def add(k, values):
                tally[k] += jnp.sum(values.reshape(rows // 8, 8, model), axis=0)

            add(0, d * unit)
            add(1, d)
            if inner:
                add(2, after * (pa[r, :].astype(F32) + pb[r, :].astype(F32)))
            if count > 3:
                add(3, before * (ma[r, :].astype(F32) + mb[r, :].astype(F32)))

    sums[...] = jnp.sum(tally[...], axis=1)


def norm_back(meta, g, x, one, two, norms, frame, extra=None):
    total, model = x.shape
    inner = extra is not None
    count = 2 + len(extra) // 2 if inner else 2
    outs = [jax.ShapeDtypeStruct((total, model), F32)]
    if inner:
        outs.append(jax.ShapeDtypeStruct((total, model), BF))
    outs.append(jax.ShapeDtypeStruct((count, model), F32))
    return call(
        functools.partial(norm_back_kernel, frame, count),
        tuple(outs),
        [SM] + [VM] * (5 + len(extra or ())),
        (VM,) * len(outs),
        [pltpu.VMEM((count, 8, model), F32)],
        20 * total * model,
        16 * total * model,
        "norm_back_inner" if inner else "norm_back",
    )(meta, g, x, one, two, norms, *(extra or ()))


def project_back(normed, weight, gains, matrix, take, d_projected, sums):
    width = gains.shape[1]
    total = normed.shape[0]
    rows, lanes = 256, 256
    sums[...] = jnp.zeros_like(sums)
    for part in range(2):
        for start in range(0, width, lanes):
            columns = part * width + start

            @pl.loop(0, total // rows)
            def _(i):
                r = pl.ds(pl.multiple_of(i * rows, rows), rows)
                unit, scale = head_parts(dot(normed[r, :], weight[:, columns : columns + lanes]), matrix)
                d = take(part, r, start, lanes)
                dg = d * gains[part : part + 1, start : start + lanes]
                mean = head_mean(dg, matrix)
                slant = head_mean(dg * unit, matrix)
                d_projected[r, columns : columns + lanes] = (scale * (dg - mean - unit * slant)).astype(BF)
                tally = jnp.sum((d * unit).reshape(rows // 8, 8, lanes), axis=0)
                sums[part * 8 : part * 8 + 8, start : start + lanes] += tally


def frame_back_kernel(frame, head, meta, d_branch, normed, qkv, near, far, gains, d_projected, part, sums, weight, d_att, dq, dk, sems):
    copies = fetch(meta, PIECES, near, far, weight, sems)
    total, model = normed.shape
    width = gains.shape[1]
    finish(copies)
    for start in range(0, width, 256):
        d_att[:, start : start + 256] = dot(
            d_branch[...], weight[:, 3 * width + start : 3 * width + start + 256]
        ).astype(BF)
    pairs = width // 128

    @pl.loop(0, (total // frame) * pairs)
    def _(i):
        r = pl.ds(pl.multiple_of((i // pairs) * frame, frame), frame)
        column = pl.multiple_of((i % pairs) * 128, 128)
        lanes = pl.ds(column, 128)
        q, k, v = qkv[0, r, lanes], qkv[1, r, lanes], qkv[2, r, lanes]
        d_out = d_att[r, lanes]
        found = []
        for mask in (only_first, only_second):
            weights = jnp.exp(dot(mask(q), k, NT))
            probs = weights / jnp.sum(weights, axis=-1, keepdims=True)
            d_probs = dot(mask(d_out), v, NT)
            delta = jnp.sum(probs * d_probs, axis=-1, keepdims=True)
            d_scores = (probs * (d_probs - delta)).astype(BF)
            found.append((dot(d_scores, k), dot(d_scores, q, TN), dot(probs.astype(BF), d_out, TN)))
        dq[r, lanes] = pick(found[0][0], found[1][0]) * HEAD_SCALE
        dk[r, lanes] = pick(found[0][1], found[1][1])
        d_projected[r, pl.ds(pl.multiple_of(2 * width + column, 128), 128)] = pick(found[0][2], found[1][2]).astype(BF)

    def take(which, r, start, lanes):
        return (dq, dk)[which][r, start : start + lanes]

    project_back(normed, weight, gains, head_matrix(256, head), take, d_projected, sums)
    for start in range(0, model, 256):
        part[:, start : start + 256] = dot(d_projected[...], weight[start : start + 256, 0 : 3 * width], NT).astype(BF)


def frame_back(meta, d_branch, normed, qkv, near, far, gains, frame, head):
    total, model = normed.shape
    width = gains.shape[1]
    return call(
        functools.partial(frame_back_kernel, frame, head),
        (
            jax.ShapeDtypeStruct((total, 3 * width), BF),
            jax.ShapeDtypeStruct((total, model), BF),
            jax.ShapeDtypeStruct((16, width), F32),
        ),
        [SM, VM, VM, VM, ANY, ANY, VM],
        (VM,) * 3,
        [
            pltpu.VMEM((model, 4 * width), BF),
            pltpu.VMEM((total, width), BF),
            pltpu.VMEM((total, width), F32),
            pltpu.VMEM((total, width), F32),
            pltpu.SemaphoreType.DMA((PIECES,)),
        ],
        12 * total * model * width,
        8 * model * width,
        "frame_back",
    )(meta, d_branch, normed, qkv, near, far, gains)


def attended_back_kernel(meta, d_branch, near, far, s0, s1, s2, s3, weight, held, sems):
    finish(fetch(meta, PIECES, near, far, weight, sems))
    me = meta[META_ME]
    width = weight.shape[1]
    for start in range(0, width, 256):
        held[:, start : start + 256] = dot(d_branch[...], weight[:, start : start + 256]).astype(BF)
    for d, slot in enumerate((s0, s1, s2, s3)):
        slot[...] = held[:, pl.ds(pl.multiple_of((me ^ d) * 128, 128), 128)]


def attended_back(meta, d_branch, near, far, width):
    total, model = d_branch.shape

    def body(meta, d_branch, near, far, *rest):
        columns = pl.ds(3 * width, width)
        attended_back_kernel(meta, d_branch, near.at[:, :, columns], far.at[:, :, columns], *rest)

    return call(
        body,
        (jax.ShapeDtypeStruct((total, 128), BF),) * 4,
        [SM, VM, ANY, ANY],
        (VM,) * 4,
        [
            pltpu.VMEM((model, width), BF),
            pltpu.VMEM((total, width), BF),
            pltpu.SemaphoreType.DMA((PIECES,)),
        ],
        2 * total * model * width,
        2 * model * width,
        "attended_back",
    )(meta, d_branch, near, far)


def scene_back_kernel(frame, meta, s0, s1, s2, s3, below, above, sums, whole, g0, g1, g2, g3, q0, q1, q2, q3, d_own, d_below, d_above, own, window, d_out, delta, dq, d_window, sems, more):
    copies = load_window(meta, (s0, s1, s2, s3), below, above, own, window, sems)
    me = meta[META_ME]
    for d, slot in enumerate((g0, g1, g2, g3)):
        copies.append(pltpu.make_async_copy(slot, d_out.at[me ^ d], more.at[d]))
        copies[-1].start()
    d_window[...] = jnp.zeros_like(d_window)
    finish(copies)
    total = own.shape[1]
    parts = total // frame

    @pl.loop(0, parts * PLANE)
    def _(i):
        m, j = i // PLANE, i % PLANE
        r = pl.ds(pl.multiple_of(m * frame, frame), frame)
        q, go = own[j, r, :], d_out[j, r, :]
        product = go.astype(F32) * whole[j, r, :]
        inverse = sums[j, r, :]
        heads = []
        for mask, lane in ((only_first, 0), (only_second, 64)):
            heads.append(
                (mask(q), mask(go), inverse[:, lane : lane + 1], jnp.sum(mask(product), axis=-1, keepdims=True))
            )
        dq[...] = jnp.zeros_like(dq)

        @pl.loop(meta[META_SCENES + i * 2], meta[META_SCENES + i * 2 + 1])
        def _(w):
            k, v = window[w, 0, r, :], window[w, 1, r, :]
            found = []
            for head_q, head_go, scale, shift in heads:
                probs = jnp.exp(dot(head_q, k, NT)) * scale
                d_scores = (probs * (dot(head_go, v, NT) - shift)).astype(BF)
                found.append((dot(d_scores, k), dot(d_scores, q, TN), dot(probs.astype(BF), go, TN)))
            dq[...] += pick(found[0][0], found[1][0])
            d_window[w, 0, r, :] += pick(found[0][1], found[1][1])
            d_window[w, 1, r, :] += pick(found[0][2], found[1][2])

        delta[j, r, :] = dq[...] * HEAD_SCALE

    for d, out in enumerate((q0, q1, q2, q3)):
        out[...] = delta[me ^ d].astype(BF)
    for k in range(PLANE):
        d_own[k] = d_window[REACH + k]
    for k in range(REACH):
        d_below[k] = d_window[k].astype(BF)
        d_above[k] = d_window[REACH + PLANE + k].astype(BF)


def scene_back(meta, slots, below, above, sums, found, d_found, frame):
    total = slots[0].shape[1]
    wide = 2 * REACH + PLANE
    out = jax.ShapeDtypeStruct((total, 128), BF)
    edge = jax.ShapeDtypeStruct((REACH, 2, total, 128), BF)
    return call(
        functools.partial(scene_back_kernel, frame),
        (out,) * 4 + (jax.ShapeDtypeStruct((PLANE, 2, total, 128), F32), edge, edge),
        [SM] + [ANY] * 6 + [VM] * 2 + [ANY] * 4,
        (VM,) * 7,
        [
            pltpu.VMEM((PLANE, total, 128), BF),
            pltpu.VMEM((wide, 2, total, 128), BF),
            pltpu.VMEM((PLANE, total, 128), BF),
            pltpu.VMEM((PLANE, total, 128), F32),
            pltpu.VMEM((frame, 128), F32),
            pltpu.VMEM((wide, 2, total, 128), F32),
            pltpu.SemaphoreType.DMA((4, PLANE)),
            pltpu.SemaphoreType.DMA((PLANE,)),
        ],
        10 * PLANE * total * PLANE * frame * 128 * 2,
        8 * wide * total * 128,
        "scene_back",
    )(meta, *slots, below, above, sums, found, *d_found)


def edge_sum_kernel(meta, d_own, from_below, from_above, t0, t1, t2, t3):
    me = meta[META_ME]
    for d, out in enumerate((t0, t1, t2, t3)):
        j = me ^ d
        low = jnp.where(j <= REACH - 1, 1.0, 0.0)
        high = jnp.where(j >= 1, 1.0, 0.0)
        at, top = jnp.minimum(j, REACH - 1), jnp.maximum(j - 1, 0)
        for part in range(2):
            values = d_own[j, part] + low * from_below[at, part].astype(F32)
            out[part] = (values + high * from_above[top, part].astype(F32)).astype(BF)


def edge_sum(meta, d_own, from_below, from_above):
    total = d_own.shape[2]
    out = jax.ShapeDtypeStruct((2, total, 128), BF)
    return call(
        edge_sum_kernel,
        (out,) * 4,
        [SM, VM, VM, VM],
        (VM,) * 4,
        [],
        8 * PLANE * total * 128,
        20 * PLANE * total * 128,
        "edge_sum",
    )(meta, d_own, from_below, from_above)


def queries_back_kernel(head, meta, q0, q1, q2, q3, t0, t1, t2, t3, normed, near, far, gains, d_projected, part, sums, weight, dq, dk, sems):
    copies = fetch(meta, PIECES, near, far, weight, sems)
    me = meta[META_ME]
    model = normed.shape[1]
    width = gains.shape[1]
    for d, (query, pair) in enumerate(zip((q0, q1, q2, q3), (t0, t1, t2, t3))):
        column = pl.multiple_of((me ^ d) * 128, 128)
        dq[:, pl.ds(column, 128)] = query[...].astype(F32)
        dk[:, pl.ds(column, 128)] = pair[0].astype(F32)
        d_projected[:, pl.ds(pl.multiple_of(2 * width + column, 128), 128)] = pair[1]
    finish(copies)

    def take(which, r, start, lanes):
        return (dq, dk)[which][r, start : start + lanes]

    project_back(normed, weight, gains, head_matrix(256, head), take, d_projected, sums)
    for start in range(0, model, 256):
        part[:, start : start + 256] = dot(d_projected[...], weight[start : start + 256, 0 : 3 * width], NT).astype(BF)


def queries_back(meta, d_queries, d_pairs, normed, near, far, gains, head):
    total, model = normed.shape
    width = gains.shape[1]
    return call(
        functools.partial(queries_back_kernel, head),
        (
            jax.ShapeDtypeStruct((total, 3 * width), BF),
            jax.ShapeDtypeStruct((total, model), BF),
            jax.ShapeDtypeStruct((16, width), F32),
        ),
        [SM] + [VM] * 9 + [ANY, ANY, VM],
        (VM,) * 3,
        [
            pltpu.VMEM((model, 4 * width), BF),
            pltpu.VMEM((total, width), F32),
            pltpu.VMEM((total, width), F32),
            pltpu.SemaphoreType.DMA((PIECES,)),
        ],
        10 * total * model * width,
        8 * model * width,
        "queries_back",
    )(meta, *d_queries, *d_pairs, normed, near, far, gains)


META_CORE = 4 * PIECES
META_ME = META_CORE + 1
META_SCENES = META_ME + 1


def body(tokens, cotangent, scene_ids, input_weight, output_weight, up_weight, down_weight, norm_params, head_gains):
    portions, _, share, model = tokens.shape
    frame = 2 * share
    total = portions * frame
    head = head_gains.shape[2]
    width = input_weight.shape[3]
    routes = Routes(lax.axis_size("frames"))
    n = routes.n
    index, core = lax.axis_index("frames"), lax.axis_index("mp")
    plain = n != PIECES

    identity = jnp.arange(PIECES, dtype=jnp.int32)
    tables = [identity] * 4 if plain else routes.tables()
    scene_here = scene_ids[:, (index // PLANE) * PLANE + jnp.arange(PLANE)]
    before = jnp.sum(scene_ids[:, None, :] < scene_here[:, :, None], axis=-1)
    until = jnp.sum(scene_ids[:, None, :] <= scene_here[:, :, None], axis=-1)
    spans = jnp.stack([before, until], axis=-1) - (index // PLANE) * PLANE + REACH
    meta = jnp.concatenate(
        [*tables, core[None], (index % PLANE)[None], spans.reshape(-1)]
    ).astype(jnp.int32)

    def all_rows(block):
        own = block[:, 0]
        other = routes.swap(own)
        both = jnp.where(core == 0, jnp.stack([own, other], 1), jnp.stack([other, own], 1))
        return both.reshape(total, model)

    def own_rows(values):
        return lax.dynamic_index_in_dim(values.reshape(portions, 2, share, -1), core, 1, keepdims=True)

    shards = []
    for layer in range(2):
        joined = jnp.concatenate(
            [input_weight[layer].reshape(-1, 3 * width), output_weight[layer]], axis=1
        )
        shards.append((joined, up_weight[layer], down_weight[layer]))
    gains = [jnp.tile(head_gains[layer], (1, width // head)) for layer in range(2)]

    def whole(shard):
        gathered = lax.all_gather(shard, "frames", axis=0, tiled=True).reshape(PIECES, -1, shard.shape[1])
        return gathered[: PIECES // 2], gathered[PIECES // 2 :]

    clock = Clock(False)
    names = ("input", "up", "down")
    kinds = (True, True, False)
    if not plain:
        (ga0, gu0, gd0), (ga1, gu1, gd1) = [
            [Gather(routes, clock, shard, kinds[at], names[at] + str(layer)) for at, shard in enumerate(shards[layer])]
            for layer in range(2)
        ]
    else:
        (ga0, gu0, gd0), (ga1, gu1, gd1) = [[Whole(whole(shard)) for shard in layer] for layer in shards]

    def scatter(pair, line_last, name):
        if plain:
            rows_ = jnp.concatenate(pair).reshape(model, -1).astype(F32)
            return Whole(lax.psum_scatter(rows_, "frames", scatter_dimension=0, tiled=True))
        return Scatter(routes, clock, pair, line_last, name)

    late, wait = clock.late, clock.wait

    ga0.line()
    gd0.one()
    gd1.one()
    rows = all_rows(tokens)
    d_result = all_rows(cotangent)
    ga0.wait()
    gd0.wait()
    gd1.wait()
    wait(rows, d_result)
    ga0.one()
    gu0.line()
    ga0.wait()
    ga0.two()
    gu0.wait()
    gd0.line()
    w0 = ga0.end()
    gu0.one()
    normed0, qkv0, attended0, a0 = attention_frame(
        meta, late(rows), *w0, norm_params[0], gains[0], frame, head
    )
    wait(a0)
    b0 = routes.swap_parts(a0)
    gu0.wait()
    gu0.two()
    gd0.wait()
    wait(b0)
    ga1.line()
    up0 = gu0.end()
    gd0.two()
    mid0, normed_mid0, active0, slope0 = feed_up(meta, rows, a0, late(b0), up0, norm_params[0])
    wait(active0)
    ga1.wait()
    gu1.line()
    down0 = gd0.end()
    ga1.one()
    m0 = feed_down(meta, late(active0), down0)
    wait(m0)
    n0 = routes.swap_parts(m0)
    wait(n0)
    ga1.wait()
    ga1.two()
    gu1.wait()
    gd1.line()
    w1 = ga1.end()
    gu1.one()
    x1, normed1, *slots = queries(
        meta, mid0, m0, late(n0), *w1, norm_params[0], norm_params[1], gains[1], head
    )
    wait(slots[0])
    gu1.wait()
    slots = routes.members(slots)
    wait(*slots[1:])
    rise, fall = edges(meta, slots)
    below, above = routes.up(rise), routes.down(fall)
    gu1.two()
    wait(below, above)
    gd1.wait()
    *found, sums, whole_found = scene(meta, slots, late(below), above, frame)
    home = routes.members(found)
    up1 = gu1.end()
    gd1.two()
    wait(*home[1:])
    attended1, a1 = outputs(meta, late(home), *w1, width)
    b1 = routes.swap_parts(a1)
    mid1, normed_mid1, active1, slope1 = feed_up(meta, x1, a1, b1, up1, norm_params[1])
    wait(active1)
    down1 = gd1.end()

    d_mlp, d_hidden, p = feed_back(meta, late(d_result), slope1, up1, down1, norm_params[1])
    wait(p)
    q = routes.swap_parts(p)
    sd1 = scatter(weight_grad(meta, 3 * PIECES, [late(d_mlp)], [active1], "down_grad"), True, "down_grad1")
    sd1.two()
    wait(q)
    g, d_branch, inner1 = norm_back(meta, d_result, mid1, p, late(q), norm_params[1], frame, (a1, b1))
    d_home = attended_back(meta, d_branch, *w1, width)
    wait(d_home[0])
    d_found = routes.members(d_home)
    su1 = scatter(weight_grad(meta, 2 * PIECES, [normed_mid1], [late(d_hidden)], "up_grad"), False, "up_grad1")
    wait(su1.give, *d_found[1:])
    sd1.wait()
    sd1.one()
    su1.two()
    *d_queries, d_own, d_below, d_above = scene_back(
        meta, slots, late(below), above, sums, whole_found, d_found, frame
    )
    wait(d_own)
    from_above, from_below = routes.down(d_below), routes.up(d_above)
    sd1.wait()
    su1.wait()
    sd1.line()
    d_queries = routes.members(d_queries)
    m1 = feed_down(meta, late(active1), down1)
    n1 = routes.swap_parts(m1)
    own_mlp = own_rows(m1).astype(F32) + own_rows(n1).astype(F32)
    result = own_rows(mid1) + norm_params[1, 5] * own_mlp
    scale1 = jnp.sum(cotangent.astype(F32).reshape(-1, model) * own_mlp.reshape(-1, model), axis=0)
    wait(m1, from_below, from_above)
    pairs = routes.members(edge_sum(meta, d_own, late(from_below), from_above))
    wait(*pairs[1:])
    wait(*d_queries[1:])
    su1.line()
    sd1.wait()
    d_projected, p, gain1 = queries_back(meta, d_queries, late(pairs), normed1, *w1, gains[1], head)
    wait(p)
    q = routes.swap_parts(p)
    sa1 = scatter(
        weight_grad(meta, 2 * PIECES, [normed1, d_branch], [late(d_projected), attended1], "input_grad"),
        False,
        "input_grad1",
    )
    sa1.two()
    wait(q)
    g, outer1 = norm_back(meta, g, x1, p, late(q), norm_params[1], frame)

    d_mlp, d_hidden, p = feed_back(meta, g, slope0, up0, down0, norm_params[0])
    wait(p)
    q = routes.swap_parts(p)
    sd0 = scatter(weight_grad(meta, 3 * PIECES, [late(d_mlp)], [active0], "down_grad"), True, "down_grad0")
    wait(sd0.give, q)
    sa1.wait()
    su1.wait()
    sd0.two()
    sa1.line()
    su1.one()
    su0 = scatter(weight_grad(meta, 3 * PIECES, [normed_mid0], [late(d_hidden)], "up_grad"), True, "up_grad0")
    g, d_branch, inner0 = norm_back(meta, g, mid0, p, q, norm_params[0], frame, (a0, b0, m0, n0))
    wait(d_branch, su0.give)
    sd0.wait()
    sd0.one()
    su0.two()
    d_projected, p, gain0 = frame_back(
        meta, late(d_branch), normed0, qkv0, *w0, gains[0], frame, head
    )
    wait(p)
    q = routes.swap_parts(p)
    sd0.wait()
    su0.wait()
    sa1.wait()
    su0.one()
    sa1.one()
    sd0.line()
    sa0 = scatter(
        weight_grad(meta, 3 * PIECES, [normed0, d_branch], [late(d_projected), attended0], "input_grad"),
        True,
        "input_grad0",
    )
    wait(sa0.give, q)
    su0.wait()
    sa0.two()
    g, outer0 = norm_back(meta, g, rows, p, late(q), norm_params[0], frame)
    token_grad = own_rows(g)
    wait(g)
    sd0.wait()
    su0.line()

    norm_rows = [
        jnp.stack([outer[0], outer[1], inner[2], inner[0], inner[1], scale])
        for outer, inner, scale in ((outer0, inner0, inner0[3]), (outer1, inner1, scale1))
    ]
    gain_rows = [
        jnp.sum(gain.reshape(2, 8, width // head, head), axis=(1, 2)).reshape(1, -1)
        for gain in (gain0, gain1)
    ]
    gain_rows = jnp.pad(jnp.concatenate(gain_rows, axis=1), ((0, 0), (0, model - 4 * head)))
    small = routes.total(jnp.concatenate([*norm_rows, gain_rows]))
    norm_grad = small[: 2 * 6].reshape(2, 6, model)
    gain_grad = small[2 * 6, : 4 * head].reshape(2, 2, head)
    wait(small)
    sa0.wait()
    sa0.one()
    su0.wait()
    sa0.wait()
    sa0.line()
    scattered = [[step.run for step in layer] for layer in ((sa0, su0, sd0), (sa1, su1, sd1))]
    return (
        result.astype(BF),
        token_grad,
        jnp.stack([scattered[layer][0][:, : 3 * width].reshape(-1, 3, width) for layer in range(2)]),
        jnp.stack([scattered[layer][0][:, 3 * width :] for layer in range(2)]),
        jnp.stack([scattered[layer][1] for layer in range(2)]),
        jnp.stack([scattered[layer][2] for layer in range(2)]),
        norm_grad,
        gain_grad,
    )


def solution(mesh):
    rows = P(None, "frames", "mp", None)
    shard = P(None, "frames", "mp")
    wide = P(None, "frames", None, "mp")
    return jax.shard_map(
        body,
        mesh=mesh,
        in_specs=(rows, rows, P(), wide, shard, shard, shard, P(), P()),
        out_specs=(rows, rows, wide, shard, shard, shard, P(), P()),
        check_vma=False,
    )
```

time: 2050 us -> 746 us (0.36)
  the two profiles are of different devices: /device:TPU:4 before, /device:TPU:1 now
where the time goes in v1:
time: 746 us; the launch traced here: 736 us
  waiting for transfers between devices  287 us (38%)
  Pallas kernels  258 us (35%)
  starting transfers between devices  80.2 us (11%)
  other arithmetic  61.1 us (8%)
  local copies, waits for them, and re-layouts  47.3 us (6%)
    ppermute x60, waiting for transfers between devices, send(): return lax.ppermute(block, AXES, route)  151 us
    ppermute x19, waiting for transfers between devices, member(): lax.ppermute(block, 'frames', [(f, f ^ distance) for f in range(self.n)])  106 us
    ppermute x60, starting transfers between devices, send(): return lax.ppermute(block, AXES, route)  49.8 us
    pallas_call x6, Pallas kernels, weight_grad(): call(functools.partial(weight_grad_kernel, base, widths), (out, out), [SM...  37.6 us
    pallas_call x4, Pallas kernels, norm_back(): call(functools.partial(norm_back_kernel, frame, count), tuple(outs), [SM]...  29.9 us
    pallas_call x1, Pallas kernels, scene_back(): call(functools.partial(scene_back_kernel, frame), (out,) * 4 + (jax.Shape...  28.2 us
    unnamed x133, local copies, waits for them, and re-layouts  26.8 us
    pallas_call x2, Pallas kernels, feed_up(): call(feed_up_kernel, (jax.ShapeDtypeStruct((total, model), F32), jax.Shap...  26 us
  transfers between devices with their start and end apart: 94, of which 40 were waited for; matrix products, arithmetic and copies ran while one was open for 12% of the time, Pallas kernels for 34%

profile of v1, /device:TPU:1, one launch (start us, length us, event | category | flops | bytes accessed | tf_op | source)
XLA Modules:
  0.0 736.1 jit_solution(11699443671662365278)
XLA Ops:
  30.9 15.5 %collective-permute-done.2 = bf16[64,2048]{1,0:T(8,128)(2,1)S(1)} collective-permute-done((bf16[64,2048]{1,0:T(8,128)(2,1)S(1)}, bf16[64,2048]{1,0:T(8,128)(2,1)S(1)}, u32[]{:S(2)}, u32[]{:S(2)}) %collective-permute-start.2) | collective-permute-done | bytes 262176 | tf_op jit(solution)/shard_map/input0_line/ppermute | solution.py:64
  47.0 5.0 collective-permute-done.8
  52.6 5.0 collective-permute-done.19
  58.3 5.0 collective-permute-done.3
  71.0 6.4 collective-permute-done.4
  88.1 4.5 collective-permute-done.10
  104.6 21.6 %collective-permute-done.5.far = bf16[8,64,2048]{2,1,0:T(8,128)(2,1)S(1)} collective-permute-done((bf16[8,64,2048]{2,1,0:T(8,128)(2,1)S(1)}, bf16[8,64,2048]{2,1,0:T(8,128)(2,1)S(1)}, u32[]{:S(2)}, u32[]{:S(2)}) %collective-permute-start.5) | collective-permute-done | bytes 2097184 | tf_op jit(solution)/shard_map/input0_two/ppermute | solution.py:64
  127.5 17.5 %attention_frame.1 = (bf16[512,1024]{1,0:T(8,128)(2,1)}, bf16[3,512,512]{2,1,0:T(8,128)(2,1)}, bf16[512,512]{1,0:T(8,128)(2,1)}, bf16[512,1024]{1,0:T(8,128)(2,1)}) custom-call(s32[82]{0:T(128)} %concatenate.40.meta, bf16[512,1024]{1,0:T(8,128)(2,1)} %bitcast.233, bf16[8,64,2048]{2,1,0:T(8,128)(2,1)} %copy-done.37, bf16[8,64,2048]{2,1,0:T(8,128)(2,1)} %copy-done.43, ...), custom_call_target="tpu_custom_call" | custom-call | flops 2147483648 | bytes 4194304 | tf_op jit(solution)/shard_map/attention_frame/pallas_call | solution.py:344
  148.5 5.0 collective-permute-done.33
  156.8 12.9 %feed_up.2 = (f32[512,1024]{1,0:T(8,128)}, bf16[512,1024]{1,0:T(8,128)(2,1)}, bf16[512,2048]{1,0:T(8,128)(2,1)}, bf16[512,2048]{1,0:T(8,128)(2,1)}) custom-call(s32[82]{0:T(128)} %concatenate.40.meta, bf16[512,1024]{1,0:T(8,128)(2,1)} %bitcast.234, bf16[512,1024]{1,0:T(8,128)(2,1)} %get-tuple-element.85.one.refs_5_, ...), custom_call_target="tpu_custom_call" | custom-call | flops 2147483648 | bytes 4194304 | tf_op jit(solution)/shard_map/feed_up/pallas_call | solution.py:391
  173.7 7.2 feed_down.2.one.refs_7_
  186.0 10.0 %collective-permute-done.39 = bf16[2,64,2048]{2,1,0:T(8,128)(2,1)} collective-permute-done((bf16[2,64,2048]{2,1,0:T(8,128)(2,1)}, bf16[2,64,2048]{2,1,0:T(8,128)(2,1)}, u32[]{:S(2)}, u32[]{:S(2)}) %collective-permute-start.39) | collective-permute-done | bytes 524320 | tf_op jit(solution)/shard_map/down1_line/ppermute | solution.py:64
  196.2 7.8 %collective-permute-done.22.far = bf16[8,64,2048]{2,1,0:T(8,128)(2,1)} collective-permute-done((bf16[8,64,2048]{2,1,0:T(8,128)(2,1)S(1)}, bf16[8,64,2048]{2,1,0:T(8,128)(2,1)}, u32[]{:S(2)}, u32[]{:S(2)}) %collective-permute-start.22) | collective-permute-done | bytes 2097184 | tf_op jit(solution)/shard_map/input1_two/ppermute | solution.py:64
  205.0 14.5 %queries.1 = (f32[512,1024]{1,0:T(8,128)}, bf16[512,1024]{1,0:T(8,128)(2,1)}, bf16[3,512,128]{2,1,0:T(8,128)(2,1)}, bf16[3,512,128]{2,1,0:T(8,128)(2,1)}, bf16[3...) custom-call(s32[82]{0:T(128)} %concatenate.40.meta, f32[512,1024]{1,0:T(8,128)} %get-tuple-element.86.mid.refs_1_, ...), custom_call_target="tpu_custom_call" | custom-call | flops 1610612736 | bytes 4194304 | tf_op jit(solution)/shard_map/queries/pallas_call | solution.py:460
  226.0 5.0 collective-permute-done.23.s1
  231.0 6.7 collective-permute-done.24.s2
  248.4 10.9 %collective-permute-done.26.below = bf16[3,2,512,128]{3,2,1,0:T(8,128)(2,1)S(1)} collective-permute-done((bf16[3,2,512,128]{3,2,1,0:T(8,128)(2,1)}, bf16[3,2,512,128]{3,2,1,0:T(8,128)(2,1)S(1)}, u32[]{:S(2)}, u32[]{:S(2)}) %collective-permute-start.26) | collective-permute-done | bytes 786464 | tf_op jit(solution)/shard_map/ppermute | solution.py:80
  263.7 15.1 %scene.1 = (bf16[512,128]{1,0:T(8,128)(2,1)}, bf16[512,128]{1,0:T(8,128)(2,1)}, bf16[512,128]{1,0:T(8,128)(2,1)}, bf16[512,128]{1,0:T(8,128)(2,1)}, f32[4,512,128]{2,1,0:T(8,128)}, /*index=5*/f32[4,512,128]{2,1,0:T(8,128)}) custom-call(s32[82]{0:T(128)} %concatenate.40.meta, bf16[3,512,128]{2,1,0:T(8,128)(2,1)} %get-tuple-element.89.s0, ...), custom_call_target="tpu_custom_call" | custom-call | flops 2147483648 | bytes 2621440 | tf_op jit(solution)/shard_map/scene/pallas_call | solution.py:555
  281.6 16.2 %collective-permute-done.28.o1 = bf16[512,128]{1,0:T(8,128)(2,1)S(1)} collective-permute-done((bf16[512,128]{1,0:T(8,128)(2,1)}, bf16[512,128]{1,0:T(8,128)(2,1)S(1)}, u32[]{:S(2)}, u32[]{:S(2)}) %collective-permute-start.28) | collective-permute-done | bytes 131104 | tf_op jit(solution)/shard_map/ppermute | solution.py:74
  311.3 13.1 %feed_up.3 = (f32[512,1024]{1,0:T(8,128)}, bf16[512,1024]{1,0:T(8,128)(2,1)}, bf16[512,2048]{1,0:T(8,128)(2,1)}, bf16[512,2048]{1,0:T(8,128)(2,1)}) custom-call(s32[82]{0:T(128)} %concatenate.40.meta, f32[512,1024]{1,0:T(8,128)} %get-tuple-element.88.x.refs_1_, bf16[512,1024]{1,0:T(8,128)(2,1)} %get-tuple-element.99.one.refs_5_, ...), custom_call_target="tpu_custom_call" | custom-call | flops 2147483648 | bytes 4194304 | tf_op jit(solution)/shard_map/feed_up/pallas_call | solution.py:391
  324.4 10.0 %feed_back.2 = (bf16[512,1024]{1,0:T(8,128)(2,1)}, bf16[512,2048]{1,0:T(8,128)(2,1)}, bf16[512,1024]{1,0:T(8,128)(2,1)}) custom-call(s32[82]{0:T(128)} %concatenate.40.meta, bf16[512,1024]{1,0:T(8,128)(2,1)} %bitcast.236, bf16[512,2048]{1,0:T(8,128)(2,1)} %get-tuple-element.102.slope, bf16[8,64,2048]{2,1,0:T(8,128)(2,1)} %copy-done.5, ...), custom_call_target="tpu_custom_call" | custom-call | flops 4294967296 | bytes 16777216 | tf_op jit(solution)/shard_map/feed_back/pallas_call | solution.py:631
  334.8 6.2 up_grad.3
  341.9 6.2 down_grad.3
  349.8 7.8 %norm_back_inner.2 = (f32[512,1024]{1,0:T(8,128)}, bf16[512,1024]{1,0:T(8,128)(2,1)}, f32[3,1024]{1,0:T(4,128)}) custom-call(s32[82]{0:T(128)} %concatenate.40.meta, bf16[512,1024]{1,0:T(8,128)(2,1)} %bitcast.237, f32[512,1024]{1,0:T(8,128)} %get-tuple-element.100.refs_1_, bf16[512,1024]{1,0:T(8,128)(2,1)} %get-tuple-element.103.refs_2_, ...), custom_call_target="tpu_custom_call" | custom-call | flops 10485760 | bytes 8388608 | tf_op jit(solution)/shard_map/norm_back_inner/pallas_call | solution.py:759
  364.5 28.7 %collective-permute-done.45.g1 = bf16[512,128]{1,0:T(8,128)(2,1)S(1)} collective-permute-done((bf16[512,128]{1,0:T(8,128)(2,1)}, bf16[512,128]{1,0:T(8,128)(2,1)S(1)}, u32[]{:S(2)}, u32[]{:S(2)}) %collective-permute-start.45) | collective-permute-done | bytes 131104 | tf_op jit(solution)/shard_map/ppermute | solution.py:74
  395.9 28.2 %scene_back.1 = (bf16[512,128]{1,0:T(8,128)(2,1)}, bf16[512,128]{1,0:T(8,128)(2,1)}, bf16[512,128]{1,0:T(8,128)(2,1)}, bf16[512,128]{1,0:T(8,128)(2,1)}, f32[4,2...) custom-call(s32[82]{0:T(128)} %concatenate.40.meta, ...), custom_call_target="tpu_custom_call" | custom-call | flops 5368709120 | bytes 5242880 | tf_op jit(solution)/shard_map/scene_back/pallas_call | solution.py:942
  428.3 7.2 feed_down.3
  436.3 7.9 %collective-permute-done.51.from_below = bf16[3,2,512,128]{3,2,1,0:T(8,128)(2,1)S(1)} collective-permute-done((bf16[3,2,512,128]{3,2,1,0:T(8,128)(2,1)}, bf16[3,2,512,128]{3,2,1,0:T(8,128)(2,1)S(1)}, u32[]{:S(2)}, u32[]{:S(2)}) %collective-permute-start.51) | collective-permute-done | bytes 786464 | tf_op jit(solution)/shard_map/ppermute | solution.py:80
  463.4 6.0 collective-permute-done.55.t3
  469.4 15.1 %queries_back.1 = (bf16[512,1536]{1,0:T(8,128)(2,1)}, bf16[512,1024]{1,0:T(8,128)(2,1)}, f32[16,512]{1,0:T(8,128)}) custom-call(s32[82]{0:T(128)} %concatenate.40.meta, bf16[512,128]{1,0:T(8,128)(2,1)} %get-tuple-element.112.q0, bf16[512,128]{1,0:T(8,128)(2,1)} %copy-done.48, bf16[512,128]{1,0:T(8,128)(2,1)} %collective-permute-done.49.q2, ...), custom_call_target="tpu_custom_call" | custom-call | flops 2684354560 | bytes 4194304 | tf_op jit(solution)/shard_map/queries_back/pallas_call | solution.py:1013
  490.7 6.4 input_grad.3
  499.2 6.0 collective-permute-done.76
  508.8 6.8 norm_back.2
  515.6 10.4 %feed_back.3 = (bf16[512,1024]{1,0:T(8,128)(2,1)}, bf16[512,2048]{1,0:T(8,128)(2,1)}, bf16[512,1024]{1,0:T(8,128)(2,1)}) custom-call(s32[82]{0:T(128)} %concatenate.40.meta, f32[512,1024]{1,0:T(8,128)} %get-tuple-element.125.g.refs_0_, bf16[512,2048]{1,0:T(8,128)(2,1)} %get-tuple-element.126.slope, ...), custom_call_target="tpu_custom_call" | custom-call | flops 4294967296 | bytes 16777216 | tf_op jit(solution)/shard_map/feed_back/pallas_call | solution.py:631
  528.8 6.2 down_grad.2
  535.1 6.2 up_grad.2
  547.9 4.8 collective-permute-done.88
  555.4 8.8 %norm_back_inner.3 = (f32[512,1024]{1,0:T(8,128)}, bf16[512,1024]{1,0:T(8,128)(2,1)}, f32[4,1024]{1,0:T(4,128)}) custom-call(s32[82]{0:T(128)} %concatenate.40.meta, f32[512,1024]{1,0:T(8,128)} %get-tuple-element.125.g.refs_0_, f32[512,1024]{1,0:T(8,128)} %get-tuple-element.86.mid.refs_1_, bf16[512,1024]{1,0:T(8,128)(2,1)} %get-tuple-element.127.refs_2_, ...), custom_call_target="tpu_custom_call" | custom-call | flops 10485760 | bytes 8388608 | tf_op jit(solution)/shard_map/norm_back_inner/pallas_call | solution.py:759
  566.6 25.0 %frame_back.1 = (bf16[512,1536]{1,0:T(8,128)(2,1)}, bf16[512,1024]{1,0:T(8,128)(2,1)}, f32[16,512]{1,0:T(8,128)}) custom-call(s32[82]{0:T(128)} %concatenate.40.meta, bf16[512,1024]{1,0:T(8,128)(2,1)} %get-tuple-element.129.d_branch.refs_1_, bf16[512,1024]{1,0:T(8,128)(2,1)} %get-tuple-element.130.normed.refs_0_, ...), custom_call_target="tpu_custom_call" | custom-call | flops 3221225472 | bytes 4194304 | tf_op jit(solution)/shard_map/frame_back/pallas_call | solution.py:834
  600.2 6.5 norm_back.3
  607.8 6.4 input_grad.2
  617.5 36.7 %collective-permute-done.90 = f32[13,1024]{1,0:T(8,128)S(1)} collective-permute-done((f32[13,1024]{1,0:T(8,128)S(1)}, f32[13,1024]{1,0:T(8,128)S(1)}, u32[]{:S(2)}, u32[]{:S(2)}) %collective-permute-start.90) | collective-permute-done | bytes 53280 | tf_op jit(solution)/shard_map/ppermute | solution.py:74
  670.3 4.5 collective-permute-done.68
  678.4 7.5 %collective-permute-done.70 = bf16[4,64,2048]{2,1,0:T(8,128)(2,1)} collective-permute-done((bf16[4,64,2048]{2,1,0:T(8,128)(2,1)}, bf16[4,64,2048]{2,1,0:T(8,128)(2,1)}, u32[]{:S(2)}, u32[]{:S(2)}) %collective-permute-start.70) | collective-permute-done | bytes 1048608 | tf_op jit(solution)/shard_map/up_grad0_one/ppermute | solution.py:64
  691.2 5.3 collective-permute-done.71
  707.2 4.7 collective-permute-done.83
  713.1 4.8 collective-permute-done.61
  720.3 4.9 collective-permute-done.62
  (416 shorter events, 243.9 us)
Async XLA Ops:
  3.6 19.6 %collective-permute-start.1 = (bf16[64,2048]{1,0:T(8,128)(2,1)}, bf16[64,2048]{1,0:T(8,128)(2,1)S(1)}, u32[]{:S(2)}, u32[]{:S(2)}) collective-permute-start(bf16[64,2048]{1,0:T(8,128)(2,1)} %get-tuple-element.207), channel_id=1, source_target_pairs={{0,8},{1,9},{2,10},{3,11},{4,12},{5,13},{6,14},{7,15},{8,24},{9,25... | collective-permute-start | bytes 786440 | tf_op jit(solution)/shard_map/input0_line/ppermute | solution.py:64
  5.8 95.2 %collective-permute-start = (bf16[2,128,1024]{2,1,0:T(8,128)(2,1)}, bf16[2,128,1024]{2,1,0:T(8,128)(2,1)}, u32[]{:S(2)}, u32[]{:S(2)}) collective-permute-start(bf16[2,128,1024]{2,1,0:T(8,128)(2,1)} %bitcast.8), channel_id=1, source_target_pairs={{0,1},{1,0},{2,3},{3,2},{4,5},{5,4},{6,7},{7,6},{8,9},{9,8},{10,11... | collective-permute-start | bytes 1572872 | tf_op jit(solution)/shard_map/ppermute | solution.py:67
  23.2 46.9 %collective-permute-start.13 = (bf16[2,64,2048]{2,1,0:T(8,128)(2,1)S(1)}, bf16[2,64,2048]{2,1,0:T(8,128)(2,1)S(1)}, u32[]{:S(2)}, u32[]{:S(2)}) collective-permute-start(bf16[2,64,2048]{2,1,0:T(8,128)(2,1)S(1)} %pad_maximum_fusion.7), channel_id=1, source_target_pairs={{0,8},{1,9},{2,10},{3,11},{4,12},{5,13},{6,14},{7,15},{8,24},{9,25... | collective-permute-start | bytes 1572872 | tf_op jit(solution)/shard_map/down0_line/ppermute | solution.py:64
  24.6 21.8 %collective-permute-start.2 = (bf16[64,2048]{1,0:T(8,128)(2,1)S(1)}, bf16[64,2048]{1,0:T(8,128)(2,1)S(1)}, u32[]{:S(2)}, u32[]{:S(2)}) collective-permute-start(bf16[64,2048]{1,0:T(8,128)(2,1)S(1)} %collective-permute-done.1), channel_id=1, source_target_pairs={{0,8},{1,9},{2,10},{3,11},{4,12},{5,13},{6,14},{7,15},{8,24},{9,25... | collective-permute-start | bytes 786440 | tf_op jit(solution)/shard_map/input0_line/ppermute | solution.py:64
  27.7 24.3 %collective-permute-start.8 = (bf16[64,2048]{1,0:T(8,128)(2,1)S(1)}, bf16[64,2048]{1,0:T(8,128)(2,1)S(1)}, u32[]{:S(2)}, u32[]{:S(2)}) collective-permute-start(bf16[64,2048]{1,0:T(8,128)(2,1)S(1)} %collective-permute-done.7), channel_id=1, source_target_pairs={{0,8},{1,9},{2,10},{3,11},{4,12},{5,13},{6,14},{7,15},{8,24},{9,25... | collective-permute-start | bytes 786440 | tf_op jit(solution)/shard_map/up0_line/ppermute | solution.py:64
  29.6 28.1 %collective-permute-start.19 = (bf16[64,2048]{1,0:T(8,128)(2,1)S(1)}, bf16[64,2048]{1,0:T(8,128)(2,1)S(1)}, u32[]{:S(2)}, u32[]{:S(2)}) collective-permute-start(bf16[64,2048]{1,0:T(8,128)(2,1)S(1)} %collective-permute-done.18), channel_id=1, source_target_pairs={{0,8},{1,9},{2,10},{3,11},{4,12},{5,13},{6,14},{7,15},{8,24},{9,25... | collective-permute-start | bytes 786440 | tf_op jit(solution)/shard_map/input1_line/ppermute | solution.py:64
  57.7 22.2 %collective-permute-start.20 = (bf16[64,2048]{1,0:T(8,128)(2,1)S(1)}, bf16[64,2048]{1,0:T(8,128)(2,1)S(1)}, u32[]{:S(2)}, u32[]{:S(2)}) collective-permute-start(bf16[64,2048]{1,0:T(8,128)(2,1)S(1)} %collective-permute-done.19), channel_id=1, source_target_pairs={{0,8},{1,9},{2,10},{3,11},{4,12},{5,13},{6,14},{7,15},{8,24},{9,25... | collective-permute-start | bytes 786440 | tf_op jit(solution)/shard_map/input1_line/ppermute | solution.py:64
  69.0 23.6 %collective-permute-start.10 = (bf16[4,64,2048]{2,1,0:T(8,128)(2,1)S(1)}, bf16[4,64,2048]{2,1,0:T(8,128)(2,1)S(1)}, u32[]{:S(2)}, u32[]{:S(2)}) collective-permute-start(bf16[4,64,2048]{2,1,0:T(8,128)(2,1)S(1)} %pad_maximum_fusion.1), channel_id=1, source_target_pairs={{0,2},{1,5},{2,0},{3,7},{4,6},{5,1},{6,4},{7,3},{8,10},{9,13},{10,... | collective-permute-start | bytes 3145736 | tf_op jit(solution)/shard_map/up0_one/ppermute | solution.py:64
  77.5 48.6 %collective-permute-start.5 = (bf16[8,64,2048]{2,1,0:T(8,128)(2,1)S(1)}, bf16[8,64,2048]{2,1,0:T(8,128)(2,1)S(1)}, u32[]{:S(2)}, u32[]{:S(2)}) collective-permute-start(bf16[8,64,2048]{2,1,0:T(8,128)(2,1)S(1)} %constant_dynamic-update-slice_fusion.near), channel_id=1, source_target_pairs={{0,4},{1,3},{2,6},{3,1},{4,0},{5,7},{6,2},{7,5},{8,12},{9,11},{10,... | collective-permute-start | bytes 6291464 | tf_op jit(solution)/shard_map/input0_two/ppermute | solution.py:64
  81.7 63.5 %collective-permute-start.21 = (bf16[4,64,2048]{2,1,0:T(8,128)(2,1)}, bf16[4,64,2048]{2,1,0:T(8,128)(2,1)S(1)}, u32[]{:S(2)}, u32[]{:S(2)}) collective-permute-start(bf16[4,64,2048]{2,1,0:T(8,128)(2,1)} %pad_maximum_fusion.2), channel_id=1, source_target_pairs={{0,2},{1,5},{2,0},{3,7},{4,6},{5,1},{6,4},{7,3},{8,10},{9,13},{10,... | collective-permute-start | bytes 3145736 | tf_op jit(solution)/shard_map/input1_one/ppermute | solution.py:64
  93.7 59.9 %collective-permute-start.11 = (bf16[8,64,2048]{2,1,0:T(8,128)(2,1)}, bf16[8,64,2048]{2,1,0:T(8,128)(2,1)}, u32[]{:S(2)}, u32[]{:S(2)}) collective-permute-start(bf16[8,64,2048]{2,1,0:T(8,128)(2,1)} %constant_dynamic-update-slice_fusion.5.un), channel_id=1, source_target_pairs={{0,4},{1,3},{2,6},{3,1},{4,0},{5,7},{6,2},{7,5},{8,12},{9,11},{10,... | collective-permute-start | bytes 6291464 | tf_op jit(solution)/shard_map/up0_two/ppermute | solution.py:64
  99.2 74.5 %collective-permute-start.16 = (bf16[8,64,2048]{2,1,0:T(8,128)(2,1)}, bf16[8,64,2048]{2,1,0:T(8,128)(2,1)}, u32[]{:S(2)}, u32[]{:S(2)}) collective-permute-start(bf16[8,64,2048]{2,1,0:T(8,128)(2,1)} %constant_dynamic-update-slice_fusion.10.dn), channel_id=1, source_target_pairs={{0,4},{1,3},{2,6},{3,1},{4,0},{5,7},{6,2},{7,5},{8,12},{9,11},{10,... | collective-permute-start | bytes 6291464 | tf_op jit(solution)/shard_map/down0_two/ppermute | solution.py:64
  101.0 44.3 %collective-permute-start.37 = (bf16[64,2048]{1,0:T(8,128)(2,1)}, bf16[64,2048]{1,0:T(8,128)(2,1)S(1)}, u32[]{:S(2)}, u32[]{:S(2)}) collective-permute-start(bf16[64,2048]{1,0:T(8,128)(2,1)} %get-tuple-element.193), channel_id=1, source_target_pairs={{0,2},{1,5},{2,0},{3,7},{4,6},{5,1},{6,4},{7,3},{8,10},{9,13},{10,... | collective-permute-start | bytes 786440 | tf_op jit(solution)/shard_map/down1_one/ppermute | solution.py:64
  145.4 58.6 %collective-permute-start.22 = (bf16[8,64,2048]{2,1,0:T(8,128)(2,1)S(1)}, bf16[8,64,2048]{2,1,0:T(8,128)(2,1)}, u32[]{:S(2)}, u32[]{:S(2)}) collective-permute-start(bf16[8,64,2048]{2,1,0:T(8,128)(2,1)S(1)} %constant_dynamic-update-slice_fusion.15.near), channel_id=1, source_target_pairs={{0,4},{1,3},{2,6},{3,1},{4,0},{5,7},{6,2},{7,5},{8,12},{9,11},{10,... | collective-permute-start | bytes 6291464 | tf_op jit(solution)/shard_map/input1_two/ppermute | solution.py:64
  153.5 28.2 %collective-permute-start.38 = (bf16[2,64,2048]{2,1,0:T(8,128)(2,1)}, bf16[2,64,2048]{2,1,0:T(8,128)(2,1)}, u32[]{:S(2)}, u32[]{:S(2)}) collective-permute-start(bf16[2,64,2048]{2,1,0:T(8,128)(2,1)} %pad_maximum_fusion.8), channel_id=1, source_target_pairs={{0,8},{1,9},{2,10},{3,11},{4,12},{5,13},{6,14},{7,15},{8,24},{9,25... | collective-permute-start | bytes 1572872 | tf_op jit(solution)/shard_map/down1_line/ppermute | solution.py:64
  153.5 28.4 %collective-permute-start.34 = (bf16[64,2048]{1,0:T(8,128)(2,1)S(1)}, bf16[64,2048]{1,0:T(8,128)(2,1)S(1)}, u32[]{:S(2)}, u32[]{:S(2)}) collective-permute-start(bf16[64,2048]{1,0:T(8,128)(2,1)S(1)} %collective-permute-done.33), channel_id=1, source_target_pairs={{0,8},{1,9},{2,10},{3,11},{4,12},{5,13},{6,14},{7,15},{8,24},{9,25... | collective-permute-start | bytes 786440 | tf_op jit(solution)/shard_map/up1_line/ppermute | solution.py:64
  180.9 23.1 %collective-permute-start.17 = (bf16[512,1024]{1,0:T(8,128)(2,1)}, bf16[512,1024]{1,0:T(8,128)(2,1)S(1)}, u32[]{:S(2)}, u32[]{:S(2)}) collective-permute-start(bf16[512,1024]{1,0:T(8,128)(2,1)} %feed_down.2.one.refs_7_), channel_id=1, source_target_pairs={{0,1},{1,0},{2,3},{3,2},{4,5},{5,4},{6,7},{7,6},{8,9},{9,8},{10,11... | collective-permute-start | bytes 3145736 | tf_op jit(solution)/shard_map/ppermute | solution.py:67
  184.0 60.3 %collective-permute-start.35 = (bf16[4,64,2048]{2,1,0:T(8,128)(2,1)}, bf16[4,64,2048]{2,1,0:T(8,128)(2,1)}, u32[]{:S(2)}, u32[]{:S(2)}) collective-permute-start(bf16[4,64,2048]{2,1,0:T(8,128)(2,1)} %pad_maximum_fusion.3), channel_id=1, source_target_pairs={{0,2},{1,5},{2,0},{3,7},{4,6},{5,1},{6,4},{7,3},{8,10},{9,13},{10,... | collective-permute-start | bytes 3145736 | tf_op jit(solution)/shard_map/up1_one/ppermute | solution.py:64
  196.0 51.0 %collective-permute-start.40 = (bf16[2,64,2048]{2,1,0:T(8,128)(2,1)}, bf16[2,64,2048]{2,1,0:T(8,128)(2,1)S(1)}, u32[]{:S(2)}, u32[]{:S(2)}) collective-permute-start(bf16[2,64,2048]{2,1,0:T(8,128)(2,1)} %collective-permute-done.39), channel_id=1, source_target_pairs={{0,8},{1,9},{2,10},{3,11},{4,12},{5,13},{6,14},{7,15},{8,24},{9,25... | collective-permute-start | bytes 1572872 | tf_op jit(solution)/shard_map/down1_line/ppermute | solution.py:64
  243.0 20.7 %collective-permute-start.27 = (bf16[3,2,512,128]{3,2,1,0:T(8,128)(2,1)}, bf16[3,2,512,128]{3,2,1,0:T(8,128)(2,1)}, u32[]{:S(2)}, u32[]{:S(2)}) collective-permute-start(bf16[3,2,512,128]{3,2,1,0:T(8,128)(2,1)} %get-tuple-element.94), channel_id=1, source_target_pairs={{8,0},{10,2},{12,4},{14,6},{16,8},{18,10},{20,12},{22,14},{24,16},... | collective-permute-start | bytes 2359304 | tf_op jit(solution)/shard_map/ppermute | solution.py:83
  245.7 64.5 %collective-permute-start.36 = (bf16[8,64,2048]{2,1,0:T(8,128)(2,1)S(1)}, bf16[8,64,2048]{2,1,0:T(8,128)(2,1)}, u32[]{:S(2)}, u32[]{:S(2)}) collective-permute-start(bf16[8,64,2048]{2,1,0:T(8,128)(2,1)S(1)} %constant_dynamic-update-slice_fusion.20.un), channel_id=1, source_target_pairs={{0,4},{1,3},{2,6},{3,1},{4,0},{5,7},{6,2},{7,5},{8,12},{9,11},{10,... | collective-permute-start | bytes 6291464 | tf_op jit(solution)/shard_map/up1_two/ppermute | solution.py:64
  247.8 76.6 %collective-permute-start.41 = (bf16[8,64,2048]{2,1,0:T(8,128)(2,1)}, bf16[8,64,2048]{2,1,0:T(8,128)(2,1)}, u32[]{:S(2)}, u32[]{:S(2)}) collective-permute-start(bf16[8,64,2048]{2,1,0:T(8,128)(2,1)} %constant_dynamic-update-slice_fusion.25.dn), channel_id=1, source_target_pairs={{0,4},{1,3},{2,6},{3,1},{4,0},{5,7},{6,2},{7,5},{8,12},{9,11},{10,... | collective-permute-start | bytes 6291464 | tf_op jit(solution)/shard_map/down1_two/ppermute | solution.py:64
  278.9 18.9 %collective-permute-start.28 = (bf16[512,128]{1,0:T(8,128)(2,1)}, bf16[512,128]{1,0:T(8,128)(2,1)S(1)}, u32[]{:S(2)}, u32[]{:S(2)}) collective-permute-start(bf16[512,128]{1,0:T(8,128)(2,1)} %get-tuple-element.96), channel_id=1, source_target_pairs={{0,2},{2,0},{4,6},{6,4},{8,10},{10,8},{12,14},{14,12},{16,18},{18,... | collective-permute-start | bytes 393224 | tf_op jit(solution)/shard_map/ppermute | solution.py:74
  280.0 19.9 %collective-permute-start.30 = (bf16[512,128]{1,0:T(8,128)(2,1)}, bf16[512,128]{1,0:T(8,128)(2,1)S(1)}, u32[]{:S(2)}, u32[]{:S(2)}) collective-permute-start(bf16[512,128]{1,0:T(8,128)(2,1)} %get-tuple-element.98), channel_id=1, source_target_pairs={{0,6},{2,4},{4,2},{6,0},{8,14},{10,12},{12,10},{14,8},{16,22},{18,... | collective-permute-start | bytes 393224 | tf_op jit(solution)/shard_map/ppermute | solution.py:74
  341.0 111.5 %collective-permute-start.74 = (bf16[8,64,2048]{2,1,0:T(8,128)(2,1)}, bf16[8,64,2048]{2,1,0:T(8,128)(2,1)}, u32[]{:S(2)}, u32[]{:S(2)}) collective-permute-start(bf16[8,64,2048]{2,1,0:T(8,128)(2,1)} %get-tuple-element.149), channel_id=1, source_target_pairs={{0,4},{1,3},{2,6},{3,1},{4,0},{5,7},{6,2},{7,5},{8,12},{9,11},{10,... | collective-permute-start | bytes 6291464 | tf_op jit(solution)/shard_map/up_grad1_two/ppermute | solution.py:64
  348.1 109.7 %collective-permute-start.84 = (bf16[8,64,2048]{2,1,0:T(8,128)(2,1)}, bf16[8,64,2048]{2,1,0:T(8,128)(2,1)}, u32[]{:S(2)}, u32[]{:S(2)}) collective-permute-start(bf16[8,64,2048]{2,1,0:T(8,128)(2,1)} %get-tuple-element.155), channel_id=1, source_target_pairs={{0,4},{1,3},{2,6},{3,1},{4,0},{5,7},{6,2},{7,5},{8,12},{9,11},{10,... | collective-permute-start | bytes 6291464 | tf_op jit(solution)/shard_map/down_grad1_two/ppermute | solution.py:64
  361.8 31.4 %collective-permute-start.45 = (bf16[512,128]{1,0:T(8,128)(2,1)}, bf16[512,128]{1,0:T(8,128)(2,1)S(1)}, u32[]{:S(2)}, u32[]{:S(2)}) collective-permute-start(bf16[512,128]{1,0:T(8,128)(2,1)} %get-tuple-element.109), channel_id=1, source_target_pairs={{0,2},{2,0},{4,6},{6,4},{8,10},{10,8},{12,14},{14,12},{16,18},{18,... | collective-permute-start | bytes 393224 | tf_op jit(solution)/shard_map/ppermute | solution.py:74
  362.7 30.5 %collective-permute-start.46 = (bf16[512,128]{1,0:T(8,128)(2,1)}, bf16[512,128]{1,0:T(8,128)(2,1)S(1)}, u32[]{:S(2)}, u32[]{:S(2)}) collective-permute-start(bf16[512,128]{1,0:T(8,128)(2,1)} %get-tuple-element.110), channel_id=1, source_target_pairs={{0,4},{2,6},{4,0},{6,2},{8,12},{10,14},{12,8},{14,10},{16,20},{18,... | collective-permute-start | bytes 393224 | tf_op jit(solution)/shard_map/ppermute | solution.py:74
  363.4 31.9 %collective-permute-start.47 = (bf16[512,128]{1,0:T(8,128)(2,1)}, bf16[512,128]{1,0:T(8,128)(2,1)S(1)}, u32[]{:S(2)}, u32[]{:S(2)}) collective-permute-start(bf16[512,128]{1,0:T(8,128)(2,1)} %get-tuple-element.111), channel_id=1, source_target_pairs={{0,6},{2,4},{4,2},{6,0},{8,14},{10,12},{12,10},{14,8},{16,22},{18,... | collective-permute-start | bytes 393224 | tf_op jit(solution)/shard_map/ppermute | solution.py:74
  424.1 20.2 %collective-permute-start.51 = (bf16[3,2,512,128]{3,2,1,0:T(8,128)(2,1)}, bf16[3,2,512,128]{3,2,1,0:T(8,128)(2,1)S(1)}, u32[]{:S(2)}, u32[]{:S(2)}) collective-permute-start(bf16[3,2,512,128]{3,2,1,0:T(8,128)(2,1)} %get-tuple-element.117), channel_id=1, source_target_pairs={{0,8},{2,10},{4,12},{6,14},{8,16},{10,18},{12,20},{14,22},{16,24},... | collective-permute-start | bytes 2359304 | tf_op jit(solution)/shard_map/ppermute | solution.py:80
  426.7 21.5 %collective-permute-start.52 = (bf16[3,2,512,128]{3,2,1,0:T(8,128)(2,1)}, bf16[3,2,512,128]{3,2,1,0:T(8,128)(2,1)S(1)}, u32[]{:S(2)}, u32[]{:S(2)}) collective-permute-start(bf16[3,2,512,128]{3,2,1,0:T(8,128)(2,1)} %get-tuple-element.118), channel_id=1, source_target_pairs={{8,0},{10,2},{12,4},{14,6},{16,8},{18,10},{20,12},{22,14},{24,16},... | collective-permute-start | bytes 2359304 | tf_op jit(solution)/shard_map/ppermute | solution.py:83
  435.6 19.5 %collective-permute-start.42 = (bf16[512,1024]{1,0:T(8,128)(2,1)}, bf16[512,1024]{1,0:T(8,128)(2,1)}, u32[]{:S(2)}, u32[]{:S(2)}) collective-permute-start(bf16[512,1024]{1,0:T(8,128)(2,1)} %feed_down.3), channel_id=1, source_target_pairs={{0,1},{1,0},{2,3},{3,2},{4,5},{5,4},{6,7},{7,6},{8,9},{9,8},{10,11... | collective-permute-start | bytes 3145736 | tf_op jit(solution)/shard_map/ppermute | solution.py:67
  457.8 30.3 %collective-permute-start.75 = (bf16[2,64,2048]{2,1,0:T(8,128)(2,1)S(1)}, bf16[2,64,2048]{2,1,0:T(8,128)(2,1)}, u32[]{:S(2)}, u32[]{:S(2)}) collective-permute-start(bf16[2,64,2048]{2,1,0:T(8,128)(2,1)S(1)} %add_convert_fusion.6), channel_id=1, source_target_pairs={{0,8},{1,9},{2,10},{3,11},{4,12},{5,13},{6,14},{7,15},{8,24},{9,25... | collective-permute-start | bytes 1572872 | tf_op jit(solution)/shard_map/up_grad1_line/ppermute | solution.py:64
  460.5 36.9 %collective-permute-start.85 = (bf16[4,64,2048]{2,1,0:T(8,128)(2,1)}, bf16[4,64,2048]{2,1,0:T(8,128)(2,1)}, u32[]{:S(2)}, u32[]{:S(2)}) collective-permute-start(bf16[4,64,2048]{2,1,0:T(8,128)(2,1)} %add_convert_fusion), channel_id=1, source_target_pairs={{0,2},{1,5},{2,0},{3,7},{4,6},{5,1},{6,4},{7,3},{8,10},{9,13},{10,... | collective-permute-start | bytes 3145736 | tf_op jit(solution)/shard_map/down_grad1_one/ppermute | solution.py:64
  484.5 23.3 %collective-permute-start.56 = (bf16[512,1024]{1,0:T(8,128)(2,1)}, bf16[512,1024]{1,0:T(8,128)(2,1)S(1)}, u32[]{:S(2)}, u32[]{:S(2)}) collective-permute-start(bf16[512,1024]{1,0:T(8,128)(2,1)} %get-tuple-element.124.refs_2_), channel_id=1, source_target_pairs={{0,1},{1,0},{2,3},{3,2},{4,5},{5,4},{6,7},{7,6},{8,9},{9,8},{10,11... | collective-permute-start | bytes 3145736 | tf_op jit(solution)/shard_map/ppermute | solution.py:67
  497.4 66.9 %collective-permute-start.64 = (bf16[8,64,2048]{2,1,0:T(8,128)(2,1)}, bf16[8,64,2048]{2,1,0:T(8,128)(2,1)}, u32[]{:S(2)}, u32[]{:S(2)}) collective-permute-start(bf16[8,64,2048]{2,1,0:T(8,128)(2,1)} %get-tuple-element.141), channel_id=1, source_target_pairs={{0,4},{1,3},{2,6},{3,1},{4,0},{5,7},{6,2},{7,5},{8,12},{9,11},{10,... | collective-permute-start | bytes 6291464 | tf_op jit(solution)/shard_map/input_grad1_two/ppermute | solution.py:64
  499.2 28.0 %collective-permute-start.86 = (bf16[64,2048]{1,0:T(8,128)(2,1)}, bf16[64,2048]{1,0:T(8,128)(2,1)S(1)}, u32[]{:S(2)}, u32[]{:S(2)}) collective-permute-start(bf16[64,2048]{1,0:T(8,128)(2,1)} %fusion.3), channel_id=1, source_target_pairs={{0,8},{1,9},{2,10},{3,11},{4,12},{5,13},{6,14},{7,15},{8,24},{9,25... | collective-permute-start | bytes 786440 | tf_op jit(solution)/shard_map/down_grad1_line/ppermute | solution.py:64
  507.6 36.4 %collective-permute-start.77 = (bf16[2,64,2048]{2,1,0:T(8,128)(2,1)}, bf16[2,64,2048]{2,1,0:T(8,128)(2,1)S(1)}, u32[]{:S(2)}, u32[]{:S(2)}) collective-permute-start(bf16[2,64,2048]{2,1,0:T(8,128)(2,1)} %add_convert_fusion.4), channel_id=1, source_target_pairs={{0,8},{1,9},{2,10},{3,11},{4,12},{5,13},{6,14},{7,15},{8,24},{9,25... | collective-permute-start | bytes 1572872 | tf_op jit(solution)/shard_map/up_grad1_line/ppermute | solution.py:64
  526.0 29.4 %collective-permute-start.57 = (bf16[512,1024]{1,0:T(8,128)(2,1)}, bf16[512,1024]{1,0:T(8,128)(2,1)}, u32[]{:S(2)}, u32[]{:S(2)}) collective-permute-start(bf16[512,1024]{1,0:T(8,128)(2,1)} %get-tuple-element.127.refs_2_), channel_id=1, source_target_pairs={{0,1},{1,0},{2,3},{3,2},{4,5},{5,4},{6,7},{7,6},{8,9},{9,8},{10,11... | collective-permute-start | bytes 3145736 | tf_op jit(solution)/shard_map/ppermute | solution.py:67
  535.0 120.1 %collective-permute-start.79 = (bf16[8,64,2048]{2,1,0:T(8,128)(2,1)}, bf16[8,64,2048]{2,1,0:T(8,128)(2,1)S(1)}, u32[]{:S(2)}, u32[]{:S(2)}) collective-permute-start(bf16[8,64,2048]{2,1,0:T(8,128)(2,1)} %get-tuple-element.152), channel_id=1, source_target_pairs={{0,4},{1,3},{2,6},{3,1},{4,0},{5,7},{6,2},{7,5},{8,12},{9,11},{10,... | collective-permute-start | bytes 6291464 | tf_op jit(solution)/shard_map/down_grad0_two/ppermute | solution.py:64
  541.3 120.3 %collective-permute-start.69 = (bf16[8,64,2048]{2,1,0:T(8,128)(2,1)}, bf16[8,64,2048]{2,1,0:T(8,128)(2,1)}, u32[]{:S(2)}, u32[]{:S(2)}) collective-permute-start(bf16[8,64,2048]{2,1,0:T(8,128)(2,1)} %get-tuple-element.145), channel_id=1, source_target_pairs={{0,4},{1,3},{2,6},{3,1},{4,0},{5,7},{6,2},{7,5},{8,12},{9,11},{10,... | collective-permute-start | bytes 6291464 | tf_op jit(solution)/shard_map/up_grad0_two/ppermute | solution.py:64
  552.7 40.8 %collective-permute-start.78 = (bf16[64,2048]{1,0:T(8,128)(2,1)}, bf16[64,2048]{1,0:T(8,128)(2,1)S(1)}, u32[]{:S(2)}, u32[]{:S(2)}) collective-permute-start(bf16[64,2048]{1,0:T(8,128)(2,1)} %fusion.31), channel_id=1, source_target_pairs={{0,2},{1,5},{2,0},{3,7},{4,6},{5,1},{6,4},{7,3},{8,10},{9,13},{10,... | collective-permute-start | bytes 786440 | tf_op jit(solution)/shard_map/up_grad1_one/ppermute | solution.py:64
  565.6 29.8 %collective-permute-start.65 = (bf16[2,64,2048]{2,1,0:T(8,128)(2,1)S(1)}, bf16[2,64,2048]{2,1,0:T(8,128)(2,1)}, u32[]{:S(2)}, u32[]{:S(2)}) collective-permute-start(bf16[2,64,2048]{2,1,0:T(8,128)(2,1)S(1)} %add_convert_fusion.9), channel_id=1, source_target_pairs={{0,8},{1,9},{2,10},{3,11},{4,12},{5,13},{6,14},{7,15},{8,24},{9,25... | collective-permute-start | bytes 1572872 | tf_op jit(solution)/shard_map/input_grad1_line/ppermute | solution.py:64
  614.2 73.0 %collective-permute-start.59 = (bf16[8,64,2048]{2,1,0:T(8,128)(2,1)}, bf16[8,64,2048]{2,1,0:T(8,128)(2,1)}, u32[]{:S(2)}, u32[]{:S(2)}) collective-permute-start(bf16[8,64,2048]{2,1,0:T(8,128)(2,1)} %get-tuple-element.137), channel_id=1, source_target_pairs={{0,4},{1,3},{2,6},{3,1},{4,0},{5,7},{6,2},{7,5},{8,12},{9,11},{10,... | collective-permute-start | bytes 6291464 | tf_op jit(solution)/shard_map/input_grad0_two/ppermute | solution.py:64
  615.7 38.6 %collective-permute-start.90 = (f32[13,1024]{1,0:T(8,128)S(1)}, f32[13,1024]{1,0:T(8,128)S(1)}, u32[]{:S(2)}, u32[]{:S(2)}) collective-permute-start(f32[13,1024]{1,0:T(8,128)S(1)} %add.526), channel_id=1, source_target_pairs={{0,2},{2,0},{4,6},{6,4},{8,10},{10,8},{12,14},{14,12},{16,18},{18,... | collective-permute-start | bytes 159752 | tf_op jit(solution)/shard_map/ppermute | solution.py:74
  617.4 41.2 %collective-permute-start.67 = (bf16[2,64,2048]{2,1,0:T(8,128)(2,1)S(1)}, bf16[2,64,2048]{2,1,0:T(8,128)(2,1)S(1)}, u32[]{:S(2)}, u32[]{:S(2)}) collective-permute-start(bf16[2,64,2048]{2,1,0:T(8,128)(2,1)S(1)} %add_convert_fusion.7), channel_id=1, source_target_pairs={{0,8},{1,9},{2,10},{3,11},{4,12},{5,13},{6,14},{7,15},{8,24},{9,25... | collective-permute-start | bytes 1572872 | tf_op jit(solution)/shard_map/input_grad1_line/ppermute | solution.py:64
  657.9 19.2 %collective-permute-start.80 = (bf16[4,64,2048]{2,1,0:T(8,128)(2,1)}, bf16[4,64,2048]{2,1,0:T(8,128)(2,1)}, u32[]{:S(2)}, u32[]{:S(2)}) collective-permute-start(bf16[4,64,2048]{2,1,0:T(8,128)(2,1)} %add_convert_fusion.1), channel_id=1, source_target_pairs={{0,2},{1,5},{2,0},{3,7},{4,6},{5,1},{6,4},{7,3},{8,10},{9,13},{10,... | collective-permute-start | bytes 3145736 | tf_op jit(solution)/shard_map/down_grad0_one/ppermute | solution.py:64
  664.2 21.7 %collective-permute-start.70 = (bf16[4,64,2048]{2,1,0:T(8,128)(2,1)}, bf16[4,64,2048]{2,1,0:T(8,128)(2,1)}, u32[]{:S(2)}, u32[]{:S(2)}) collective-permute-start(bf16[4,64,2048]{2,1,0:T(8,128)(2,1)} %add_convert_fusion.2), channel_id=1, source_target_pairs={{0,2},{1,5},{2,0},{3,7},{4,6},{5,1},{6,4},{7,3},{8,10},{9,13},{10,... | collective-permute-start | bytes 3145736 | tf_op jit(solution)/shard_map/up_grad0_one/ppermute | solution.py:64
  (100 other events, 1035.7 us)

commit v2 on v1

--- a/solution.py
+++ b/solution.py
@@ -26,6 +26,7 @@
 VM = pl.BlockSpec(memory_space=pltpu.VMEM)
 SM = pl.BlockSpec(memory_space=pltpu.SMEM)
 ANY = pl.BlockSpec(memory_space=pl.ANY)
+HBM = pl.BlockSpec(memory_space=pltpu.HBM)
 
 
 def dot(left, right, dims=NN):
@@ -39,7 +40,7 @@
         in_specs=in_specs,
         out_specs=out_specs,
         scratch_shapes=scratch,
-        compiler_params=pltpu.CompilerParams(vmem_limit_bytes=60 * 1024 * 1024),
+        compiler_params=pltpu.CompilerParams(vmem_limit_bytes=18 * 1024 * 1024),
         cost_estimate=pl.CostEstimate(flops=flops // COST, bytes_accessed=moved // COST, transcendentals=0),
         name=name,
     )
@@ -67,6 +68,8 @@
         return lax.ppermute(block, "mp", [(0, 1), (1, 0)])
 
     def swap_parts(self, block):
+        if SWAPS == 1:
+            return self.swap(block)
         rows = block.shape[0] // SWAPS
         return jnp.concatenate([self.swap(block[i * rows : (i + 1) * rows]) for i in range(SWAPS)])
 
@@ -87,10 +90,12 @@
         low, high = 1 + core, 2 - core
         bits = jnp.arange(2, dtype=jnp.int32)
         line = PLANE * jnp.asarray(self.back)[:, frame // PLANE]
+        straight = PLANE * (frame // PLANE ^ jnp.arange(self.lines, dtype=jnp.int32))
         near = ((frame // low) % 2 ^ bits) * low
         far = ((frame // high) % 2 ^ bits) * high
         middle = line[None, :, None] + near[None, None, :] + far[:, None, None]
         first = line[None, None, :] + near[None, :, None] + far[:, None, None]
+        direct = straight[None, None, :] + near[None, :, None] + far[:, None, None]
         every = jnp.arange(self.n, dtype=jnp.int32)
         k = jnp.repeat(jnp.asarray(self.steps)[frame // PLANE], PLANE)
         j = (every // low) % 2 ^ (frame // low) % 2
@@ -98,127 +103,172 @@
         half = self.n // 2
         place_middle = h * half + k * 2 + j
         place_first = h * half + j * self.lines + k
-        return [t.reshape(-1).astype(jnp.int32) for t in (middle, first, place_middle, place_first)]
-
-    def total(self, block):
-        block = block + self.swap(block)
-        distance = 1
-        while distance < self.n:
-            block = block + self.member(block, distance)
-            distance *= 2
-        return block
+        return [t.reshape(-1).astype(jnp.int32) for t in (middle, first, place_middle, place_first, direct)]
 
 
 class Clock:
     def __init__(self, active):
-        self.active, self.waited = active, []
-
-    def wait(self, *values):
-        self.waited = (self.waited + list(values))[-6:]
+        self.active, self.waited, self.pending = active, [], []
 
     def late(self, value):
         if not (self.active and self.waited):
             return value
         return lax.optimization_barrier((value, self.waited))[0]
 
+    def add(self, value):
+        self.pending.append(value)
+        return value
+
+    def close(self, *values):
+        self.waited, self.pending = self.pending + list(values), []
+
 
 class Gather:
     def __init__(self, routes, clock, shard, line_first, name):
-        self.routes, self.clock, self.near, self.line_first, self.name = routes, clock, shard, line_first, name
-
-    def line(self):
-        with jax.named_scope(self.name + "_line"):
-            source = self.clock.late(self.near)
-            pieces = [source]
-            for _ in range(1, self.routes.lines):
-                pieces.append(self.routes.send(pieces[-1], self.routes.ring))
-            self.near = jnp.stack(pieces) if self.line_first else jnp.concatenate(pieces)
+        self.routes, self.clock, self.line_first, self.name = routes, clock, line_first, name
+        self.shard, self.pieces, self.direct = shard, [shard], False
+
+    def send(self, block, route, step):
+        with jax.named_scope(self.name + step):
+            return self.clock.add(self.routes.send(self.clock.late(block), route))
+
+    def ring(self, steps=1):
+        for i in range(steps):
+            if i:
+                moved = self.routes.send(self.pieces[-1], self.routes.ring)
+                self.clock.pending[-1] = moved
+            else:
+                moved = self.send(self.pieces[-1], self.routes.ring, "_ring")
+            self.pieces.append(moved)
+        if self.line_first and len(self.pieces) == self.routes.lines:
+            self.line = jnp.stack(self.pieces)
+
+    def straight(self):
+        self.direct = True
+        for k in range(1, self.routes.lines):
+            with jax.named_scope(self.name + "_line"):
+                self.pieces.append(self.clock.add(self.routes.member(self.clock.late(self.shard), PLANE * k)))
+        self.line = jnp.stack(self.pieces)
 
     def one(self):
-        with jax.named_scope(self.name + "_one"):
-            source = self.clock.late(self.near)
-            got = self.routes.send(source, self.routes.one)
-            self.near = jnp.concatenate([source, got]) if self.line_first else jnp.stack([source, got])
-
-    def two(self):
-        with jax.named_scope(self.name + "_two"):
-            self.near = self.clock.late(self.near)
-            self.far = self.routes.send(self.near, self.routes.two)
-
-    def wait(self):
-        self.clock.wait(self.near)
-
-    def end(self):
-        self.clock.wait(self.far)
-        return self.near, self.far
+        if self.line_first:
+            self.got = self.send(self.line, self.routes.one, "_one")
+        else:
+            self.pieces = [jnp.stack([self.shard, self.send(self.shard, self.routes.one, "_one")])]
+
+    def near(self, half):
+        if self.line_first:
+            return (self.line, self.got)[half]
+        if not hasattr(self, "pairs"):
+            self.pairs = {}
+        if half not in self.pairs:
+            self.pairs[half] = jnp.concatenate(self.pieces[2 * half : 2 * half + 2])
+        return self.pairs[half]
+
+    def two(self, half):
+        far = self.send(self.near(half), self.routes.two, "_two")
+        self.far = (self.far if half else []) + [far]
+
+    def end(self, start=0, width=None):
+        sources = [self.near(0), self.near(1), *self.far]
+        base = (4 if self.direct else 1) * PIECES if self.line_first else 0
+        return Weight(sources, base, start, width)
 
 
 class Scatter:
-    def __init__(self, routes, clock, pair, line_last, name):
+    def __init__(self, routes, clock, parts, line_last, name):
         self.routes, self.clock, self.line_last, self.name = routes, clock, line_last, name
-        keep, give = pair
-        self.shape = ((2, routes.lines) if line_last else (routes.lines, 2)) + keep.shape[1:]
-        self.keep, self.give = keep.reshape(self.shape), give
-
-    def wait(self):
-        self.clock.wait(*self.last)
-
-    def two(self):
-        with jax.named_scope(self.name + "_two"):
-            give = self.clock.late(self.give)
-            got = self.routes.send(give, self.routes.two)
-            self.last = [got]
-            self.got = got.reshape(self.shape)
-
-    def pair(self, *index):
-        return self.keep[index].astype(F32) + self.got[index].astype(F32)
+        self.keep, self.give = parts[:2], parts[2:]
+        self.got, self.at, self.run = [None, None], 0, None
+
+    def send(self, block, route, step):
+        with jax.named_scope(self.name + step):
+            return self.clock.add(self.routes.send(self.clock.late(block), route))
+
+    def two(self, half):
+        self.got[half] = self.send(self.give[half], self.routes.two, "_two")
 
     def one(self):
-        with jax.named_scope(self.name + "_one"):
-            block = self.pair(1).astype(BF) if self.line_last else self.run[1].astype(BF)
-            self.more = self.routes.send(self.clock.late(block), self.routes.one)
-            self.last = [self.more]
-            if not self.line_last:
-                self.run = self.run[0] + self.more.astype(F32)
+        if self.line_last:
+            block = self.keep[1].astype(F32) + self.got[1].astype(F32)
+            self.more = self.send(block.astype(BF), self.routes.one, "_one")
+        else:
+            self.run = self.run[0] + self.send(self.run[1].astype(BF), self.routes.one, "_one").astype(F32)
 
     def local(self, k):
-        return self.pair(0, k) + self.more[k].astype(F32) if self.line_last else self.pair(k)
-
-    def line(self):
-        with jax.named_scope(self.name + "_line"):
-            lines = self.routes.lines
-            run = self.local(1 % lines)
-            for k in range(1, lines):
-                block = run.astype(BF)
-                got = self.routes.send(self.clock.late(block) if k == 1 else block, self.routes.ring)
-                run = self.local((k + 1) % lines) + got.astype(F32)
-            self.last = [got]
-            self.run = run
+        if self.line_last:
+            return self.keep[0][k].astype(F32) + self.got[0][k].astype(F32) + self.more[k].astype(F32)
+        half, rows = k // 2, slice(2 * (k % 2), 2 * (k % 2) + 2)
+        return self.keep[half][rows].astype(F32) + self.got[half][rows].astype(F32)
+
+    def ring(self):
+        if self.run is None:
+            self.at, self.run = 1, self.local(1)
+        moved = self.send(self.run.astype(BF), self.routes.ring, "_ring")
+        self.at = (self.at + 1) % self.routes.lines
+        self.run = self.local(self.at) + moved.astype(F32)
+
+
+class Weight:
+    def __init__(self, sources, base, start=0, width=None):
+        self.sources, self.count = tuple(sources), len(sources)
+        self.width = width or self.sources[0].shape[-1]
+        self.plan = (base, start, self.width)
 
 
 class Whole:
     def __init__(self, value):
-        self.run = self.give = value
-
-    def line(self):
+        self.run = value
+
+    def ring(self, steps=1):
         pass
 
-    one = two = wait = line
-
-    def end(self):
-        return self.run
-
-
-def fetch(meta, base, near, far, into, sems):
-    half, rows = near.shape[0], near.shape[1]
+    def one(self):
+        pass
+
+    def straight(self):
+        pass
+
+    def two(self, half):
+        pass
+
+    def end(self, start=0, width=None):
+        return Weight([self.run], None, start, width)
+
+
+def with_weights(kernel, before, weights):
+    def run(*refs):
+        at = before
+        given = []
+        for weight in weights:
+            given.append((weight.plan, refs[at : at + weight.count]))
+            at += weight.count
+        return kernel(*refs[:before], *given, *refs[at:])
+
+    return run
+
+
+def sources_of(weights):
+    return [source for weight in weights for source in weight.sources]
+
+
+def fetch(meta, plan, sources, into, sems):
+    base, start, width = plan
+    columns = pl.ds(start, width)
     copies = []
-    for side, source in ((0, near), (1, far)):
-        for p in range(half):
-            q = side * half + p
+    if base is None:
+        rows = into.shape[0] // 4
+        for q in range(4):
+            part = pl.ds(q * rows, rows)
+            copies.append(pltpu.make_async_copy(sources[0].at[part, columns], into.at[part, :], sems.at[q]))
+    else:
+        rows, quarter = into.shape[0] // PIECES, PIECES // 4
+        for q in range(PIECES):
+            source = sources[q // quarter].at[q % quarter, :, columns]
             row = pl.multiple_of(meta[base + q] * rows, rows)
-            copy = pltpu.make_async_copy(source.at[p], into.at[pl.ds(row, rows), :], sems.at[q])
-            copy.start()
-            copies.append(copy)
+            copies.append(pltpu.make_async_copy(source, into.at[pl.ds(row, rows), :], sems.at[q]))
+    for copy in copies:
+        copy.start()
     return copies
 
 
@@ -301,8 +351,9 @@
     return v * phi, phi + v * bell * 0.3989422804014327
 
 
-def attention_frame_kernel(frame, head, meta, rows_ref, near, far, norms, gains, normed, qkv, attended, part, weight, sems):
-    copies = fetch(meta, PIECES, near, far, weight, sems)
+def attention_frame_kernel(frame, head, meta, w_in, w_out, rows_ref, norms, gains, normed, qkv, attended, part, weight, out, sems):
+    copies = fetch(meta, *w_in, weight, sems.at[0])
+    later = fetch(meta, *w_out, out, sems.at[1])
     total, model = rows_ref.shape
     width = gains.shape[1]
 
@@ -332,34 +383,38 @@
             found.append(dot(weights.astype(BF), v) / jnp.sum(weights, axis=-1, keepdims=True))
         attended[r, lanes] = pick(found[0], found[1]).astype(BF)
 
+    finish(later)
     for start in range(0, model, 256):
-        part[:, start : start + 256] = dot(
-            attended[...], weight[start : start + 256, 3 * width : 4 * width], NT
-        ).astype(BF)
-
-
-def attention_frame(meta, rows, near, far, norms, gains, frame, head):
+        part[:, start : start + 256] = dot(attended[...], out[start : start + 256, :], NT).astype(BF)
+
+
+def attention_frame(meta, weights, rows, norms, gains, frame, head):
     total, model = rows.shape
     width = gains.shape[1]
+    sources = sources_of(weights)
     return call(
-        functools.partial(attention_frame_kernel, frame, head),
+        with_weights(functools.partial(attention_frame_kernel, frame, head), 1, weights),
         (
             jax.ShapeDtypeStruct((total, model), BF),
             jax.ShapeDtypeStruct((3, total, width), BF),
             jax.ShapeDtypeStruct((total, width), BF),
             jax.ShapeDtypeStruct((total, model), BF),
         ),
-        [SM, VM, ANY, ANY, VM, VM],
+        [SM] + [HBM] * len(sources) + [VM, VM, VM],
         (VM, VM, VM, VM),
-        [pltpu.VMEM((model, 4 * width), BF), pltpu.SemaphoreType.DMA((PIECES,))],
+        [
+            pltpu.VMEM((model, 3 * width), BF),
+            pltpu.VMEM((model, width), BF),
+            pltpu.SemaphoreType.DMA((2, PIECES)),
+        ],
         8 * total * model * width,
         2 * 4 * model * width,
         "attention_frame",
-    )(meta, rows, near, far, norms, gains)
-
-
-def feed_up_kernel(meta, x, one, two, un, uf, norms, mid, normed, active, slope, up, sems):
-    copies = fetch(meta, PIECES, un, uf, up, sems)
+    )(meta, *sources, rows, norms, gains)
+
+
+def feed_up_kernel(meta, w_up, x, one, two, norms, mid, normed, active, slope, up, sems):
+    copies = fetch(meta, *w_up, up, sems)
     total, model = x.shape
     hidden = up.shape[1]
 
@@ -385,50 +440,49 @@
             slope[r, start : start + step] = rise.astype(BF)
 
 
-def feed_up(meta, x, one, two, up, norms):
+def feed_up(meta, up, x, one, two, norms):
     total, model = x.shape
-    hidden = up[0].shape[2]
+    hidden = up.width
     return call(
-        feed_up_kernel,
+        with_weights(feed_up_kernel, 1, [up]),
         (
             jax.ShapeDtypeStruct((total, model), F32),
             jax.ShapeDtypeStruct((total, model), BF),
             jax.ShapeDtypeStruct((total, hidden), BF),
             jax.ShapeDtypeStruct((total, hidden), BF),
         ),
-        [SM, VM, VM, VM, ANY, ANY, VM],
+        [SM] + [HBM] * up.count + [VM] * 4,
         (VM,) * 4,
         [pltpu.VMEM((model, hidden), BF), pltpu.SemaphoreType.DMA((PIECES,))],
         2 * total * model * hidden,
         2 * model * hidden,
         "feed_up",
-    )(meta, x, one, two, *up, norms)
-
-
-def feed_down_kernel(meta, active, dn, df, part, down, sems):
+    )(meta, *up.sources, x, one, two, norms)
+
+
+def feed_down_kernel(meta, w_down, active, part, down, sems):
     model = part.shape[1]
-    finish(fetch(meta, 0, dn, df, down, sems))
+    finish(fetch(meta, *w_down, down, sems))
     for start in range(0, model, 256):
         part[:, start : start + 256] = dot(active[...], down[start : start + 256, :], NT).astype(BF)
 
 
-def feed_down(meta, active, down):
+def feed_down(meta, down, active, model):
     total, hidden = active.shape
-    model = down[0].shape[1] * PIECES
     return call(
-        feed_down_kernel,
+        with_weights(feed_down_kernel, 1, [down]),
         jax.ShapeDtypeStruct((total, model), BF),
-        [SM, VM, ANY, ANY],
+        [SM] + [HBM] * down.count + [VM],
         VM,
         [pltpu.VMEM((model, hidden), BF), pltpu.SemaphoreType.DMA((PIECES,))],
         2 * total * model * hidden,
         2 * model * hidden,
         "feed_down",
-    )(meta, active, *down)
-
-
-def queries_kernel(head, meta, mid, one, two, near, far, before, norms, gains, x, normed, s0, s1, s2, s3, weight, held, sems):
-    copies = fetch(meta, PIECES, near, far, weight, sems)
+    )(meta, *down.sources, active)
+
+
+def queries_kernel(head, meta, w_in, mid, one, two, before, norms, gains, x, normed, s0, s1, s2, s3, weight, held, sems):
+    copies = fetch(meta, *w_in, weight, sems)
     total, model = mid.shape
     width = gains.shape[1]
     me = meta[META_ME]
@@ -453,24 +507,24 @@
             slot[part] = held[part, :, lanes]
 
 
-def queries(meta, mid, one, two, near, far, before, norms, gains, head):
+def queries(meta, w_in, mid, one, two, before, norms, gains, head):
     total, model = mid.shape
     width = gains.shape[1]
     slot = jax.ShapeDtypeStruct((3, total, 128), BF)
     return call(
-        functools.partial(queries_kernel, head),
+        with_weights(functools.partial(queries_kernel, head), 1, [w_in]),
         (jax.ShapeDtypeStruct((total, model), F32), jax.ShapeDtypeStruct((total, model), BF)) + (slot,) * 4,
-        [SM, VM, VM, VM, ANY, ANY, VM, VM, VM],
+        [SM] + [HBM] * w_in.count + [VM] * 6,
         (VM,) * 6,
         [
-            pltpu.VMEM((model, 4 * width), BF),
+            pltpu.VMEM((model, 3 * width), BF),
             pltpu.VMEM((3, total, width), BF),
             pltpu.SemaphoreType.DMA((PIECES,)),
         ],
         6 * total * model * width,
         8 * model * width,
         "queries",
-    )(meta, mid, one, two, near, far, before, norms, gains)
+    )(meta, *w_in.sources, mid, one, two, before, norms, gains)
 
 
 def edge_kernel(meta, s0, s1, s2, s3, rise, fall):
@@ -569,10 +623,9 @@
     )(meta, *slots, below, above)
 
 
-def output_kernel(meta, o0, o1, o2, o3, near, far, attended, part, weight, sems):
-    copies = fetch(meta, PIECES, near, far, weight, sems)
+def output_kernel(meta, w_out, o0, o1, o2, o3, attended, part, weight, sems):
+    copies = fetch(meta, *w_out, weight, sems)
     me = meta[META_ME]
-    width = attended.shape[1]
     model = part.shape[1]
     for d, slot in enumerate((o0, o1, o2, o3)):
         attended[:, pl.ds(pl.multiple_of((me ^ d) * 128, 128), 128)] = slot[...]
@@ -581,32 +634,23 @@
         part[:, start : start + 256] = dot(attended[...], weight[start : start + 256, :], NT).astype(BF)
 
 
-def outputs(meta, slots, near, far, width):
+def outputs(meta, w_out, slots, width, model):
     total = slots[0].shape[0]
-    model = near.shape[1] * PIECES
     return call(
-        output_kernel_narrow(width),
+        with_weights(output_kernel, 1, [w_out]),
         (jax.ShapeDtypeStruct((total, width), BF), jax.ShapeDtypeStruct((total, model), BF)),
-        [SM] + [VM] * 4 + [ANY, ANY],
+        [SM] + [HBM] * w_out.count + [VM] * 4,
         (VM, VM),
         [pltpu.VMEM((model, width), BF), pltpu.SemaphoreType.DMA((PIECES,))],
         2 * total * model * width,
         2 * model * width,
         "outputs",
-    )(meta, *slots, near, far)
-
-
-def output_kernel_narrow(width):
-    def body(meta, o0, o1, o2, o3, near, far, *rest):
-        columns = pl.ds(3 * width, width)
-        output_kernel(meta, o0, o1, o2, o3, near.at[:, :, columns], far.at[:, :, columns], *rest)
-
-    return body
-
-
-def feed_back_kernel(meta, g, slope, un, uf, dn, df, norms, d_mlp, d_hidden, part, up, down, sems):
-    copies = fetch(meta, 0, dn, df, down, sems.at[0])
-    later = fetch(meta, PIECES, un, uf, up, sems.at[1])
+    )(meta, *w_out.sources, *slots)
+
+
+def feed_back_kernel(meta, w_down, w_up, g, slope, norms, d_mlp, d_hidden, part, up, down, sems):
+    copies = fetch(meta, *w_down, down, sems.at[0])
+    later = fetch(meta, *w_up, up, sems.at[1])
     total, model = g.shape
     hidden = up.shape[1]
 
@@ -625,17 +669,18 @@
         part[:, start : start + 256] = dot(d_hidden[...], up[start : start + 256, :], NT).astype(BF)
 
 
-def feed_back(meta, g, slope, up, down, norms):
+def feed_back(meta, weights, g, slope, norms):
     total, model = g.shape
     hidden = slope.shape[1]
+    sources = sources_of(weights)
     return call(
-        feed_back_kernel,
+        with_weights(feed_back_kernel, 1, weights),
         (
             jax.ShapeDtypeStruct((total, model), BF),
             jax.ShapeDtypeStruct((total, hidden), BF),
             jax.ShapeDtypeStruct((total, model), BF),
         ),
-        [SM, VM, VM, ANY, ANY, ANY, ANY, VM],
+        [SM] + [HBM] * len(sources) + [VM] * 3,
         (VM,) * 3,
         [
             pltpu.VMEM((model, hidden), BF),
@@ -645,15 +690,23 @@
         4 * total * model * hidden,
         8 * model * hidden,
         "feed_back",
-    )(meta, g, slope, *up, *down, norms)
+    )(meta, *sources, g, slope, norms)
 
 
 def weight_grad_kernel(base, widths, meta, *refs):
     count = len(widths)
     lefts, rights = refs[:count], refs[count : 2 * count]
-    keep, give, staged, sems = refs[2 * count :]
-    half, rows = keep.shape[0], keep.shape[1]
     model = lefts[0].shape[1]
+    if base is None:
+        whole = refs[2 * count]
+        for b in range(0, model, 256):
+            start = 0
+            for left, right, width in zip(lefts, rights, widths):
+                whole[b : b + 256, start : start + width] = dot(left[:, b : b + 256], right[...], TN).astype(BF)
+                start += width
+        return
+    parts, (staged, sems) = refs[2 * count : 2 * count + 4], refs[2 * count + 4 :]
+    quarter, rows = parts[0].shape[0], parts[0].shape[1]
     block = 256
     per = block // rows
 
@@ -662,14 +715,11 @@
         for s in range(per):
             place = meta[base + b * per + s]
             source = staged.at[slot, pl.ds(s * rows, rows), :]
-
-            @pl.when(place < half)
-            def _():
-                getattr(pltpu.make_async_copy(source, keep.at[jnp.minimum(place, half - 1)], sems.at[slot, s]), act)()
-
-            @pl.when(place >= half)
-            def _():
-                getattr(pltpu.make_async_copy(source, give.at[jnp.maximum(place - half, 0)], sems.at[slot, s]), act)()
+            for part, out in enumerate(parts):
+
+                @pl.when(place // quarter == part)
+                def _():
+                    getattr(pltpu.make_async_copy(source, out.at[lax.rem(place, quarter)], sems.at[slot, s]), act)()
 
     for b in range(model // block):
         if b >= 2:
@@ -690,13 +740,14 @@
     total, model = lefts[0].shape
     rows = model // PIECES
     wide = sum(widths)
-    out = jax.ShapeDtypeStruct((PIECES // 2, rows, wide), BF)
+    out = jax.ShapeDtypeStruct((PIECES // 4, rows, wide), BF)
+    whole = base is None
     return call(
         functools.partial(weight_grad_kernel, base, widths),
-        (out, out),
+        jax.ShapeDtypeStruct((model, wide), BF) if whole else (out,) * 4,
         [SM] + [VM] * (2 * len(widths)),
-        (ANY, ANY),
-        [pltpu.VMEM((2, 256, wide), BF), pltpu.SemaphoreType.DMA((2, 256 // rows))],
+        VM if whole else (ANY,) * 4,
+        [] if whole else [pltpu.VMEM((2, 256, wide), BF), pltpu.SemaphoreType.DMA((2, 256 // rows))],
         2 * total * model * wide,
         2 * model * wide + 2 * total * (model + wide),
         name,
@@ -790,15 +841,14 @@
                 sums[part * 8 : part * 8 + 8, start : start + lanes] += tally
 
 
-def frame_back_kernel(frame, head, meta, d_branch, normed, qkv, near, far, gains, d_projected, part, sums, weight, d_att, dq, dk, sems):
-    copies = fetch(meta, PIECES, near, far, weight, sems)
+def frame_back_kernel(frame, head, meta, w_in, w_out, d_branch, normed, qkv, gains, d_projected, part, sums, weight, out, d_att, dq, dk, sems):
+    copies = fetch(meta, *w_out, out, sems.at[1])
+    later = fetch(meta, *w_in, weight, sems.at[0])
     total, model = normed.shape
     width = gains.shape[1]
     finish(copies)
     for start in range(0, width, 256):
-        d_att[:, start : start + 256] = dot(
-            d_branch[...], weight[:, 3 * width + start : 3 * width + start + 256]
-        ).astype(BF)
+        d_att[:, start : start + 256] = dot(d_branch[...], out[:, start : start + 256]).astype(BF)
     pairs = width // 128
 
     @pl.loop(0, (total // frame) * pairs)
@@ -823,38 +873,41 @@
     def take(which, r, start, lanes):
         return (dq, dk)[which][r, start : start + lanes]
 
+    finish(later)
     project_back(normed, weight, gains, head_matrix(256, head), take, d_projected, sums)
     for start in range(0, model, 256):
-        part[:, start : start + 256] = dot(d_projected[...], weight[start : start + 256, 0 : 3 * width], NT).astype(BF)
-
-
-def frame_back(meta, d_branch, normed, qkv, near, far, gains, frame, head):
+        part[:, start : start + 256] = dot(d_projected[...], weight[start : start + 256, :], NT).astype(BF)
+
+
+def frame_back(meta, weights, d_branch, normed, qkv, gains, frame, head):
     total, model = normed.shape
     width = gains.shape[1]
+    sources = sources_of(weights)
     return call(
-        functools.partial(frame_back_kernel, frame, head),
+        with_weights(functools.partial(frame_back_kernel, frame, head), 1, weights),
         (
             jax.ShapeDtypeStruct((total, 3 * width), BF),
             jax.ShapeDtypeStruct((total, model), BF),
             jax.ShapeDtypeStruct((16, width), F32),
         ),
-        [SM, VM, VM, VM, ANY, ANY, VM],
+        [SM] + [HBM] * len(sources) + [VM] * 4,
         (VM,) * 3,
         [
-            pltpu.VMEM((model, 4 * width), BF),
+            pltpu.VMEM((model, 3 * width), BF),
+            pltpu.VMEM((model, width), BF),
             pltpu.VMEM((total, width), BF),
             pltpu.VMEM((total, width), F32),
             pltpu.VMEM((total, width), F32),
-            pltpu.SemaphoreType.DMA((PIECES,)),
+            pltpu.SemaphoreType.DMA((2, PIECES)),
         ],
         12 * total * model * width,
         8 * model * width,
         "frame_back",
-    )(meta, d_branch, normed, qkv, near, far, gains)
-
-
-def attended_back_kernel(meta, d_branch, near, far, s0, s1, s2, s3, weight, held, sems):
-    finish(fetch(meta, PIECES, near, far, weight, sems))
+    )(meta, *sources, d_branch, normed, qkv, gains)
+
+
+def attended_back_kernel(meta, w_out, d_branch, s0, s1, s2, s3, weight, held, sems):
+    finish(fetch(meta, *w_out, weight, sems))
     me = meta[META_ME]
     width = weight.shape[1]
     for start in range(0, width, 256):
@@ -863,17 +916,12 @@
         slot[...] = held[:, pl.ds(pl.multiple_of((me ^ d) * 128, 128), 128)]
 
 
-def attended_back(meta, d_branch, near, far, width):
+def attended_back(meta, w_out, d_branch, width):
     total, model = d_branch.shape
-
-    def body(meta, d_branch, near, far, *rest):
-        columns = pl.ds(3 * width, width)
-        attended_back_kernel(meta, d_branch, near.at[:, :, columns], far.at[:, :, columns], *rest)
-
     return call(
-        body,
+        with_weights(attended_back_kernel, 1, [w_out]),
         (jax.ShapeDtypeStruct((total, 128), BF),) * 4,
-        [SM, VM, ANY, ANY],
+        [SM] + [HBM] * w_out.count + [VM],
         (VM,) * 4,
         [
             pltpu.VMEM((model, width), BF),
@@ -883,7 +931,7 @@
         2 * total * model * width,
         2 * model * width,
         "attended_back",
-    )(meta, d_branch, near, far)
+    )(meta, *w_out.sources, d_branch)
 
 
 def scene_back_kernel(frame, meta, s0, s1, s2, s3, below, above, sums, whole, g0, g1, g2, g3, q0, q1, q2, q3, d_own, d_below, d_above, own, window, d_out, delta, dq, d_window, sems, more):
@@ -987,8 +1035,8 @@
     )(meta, d_own, from_below, from_above)
 
 
-def queries_back_kernel(head, meta, q0, q1, q2, q3, t0, t1, t2, t3, normed, near, far, gains, d_projected, part, sums, weight, dq, dk, sems):
-    copies = fetch(meta, PIECES, near, far, weight, sems)
+def queries_back_kernel(head, meta, w_in, q0, q1, q2, q3, t0, t1, t2, t3, normed, gains, d_projected, part, sums, weight, dq, dk, sems):
+    copies = fetch(meta, *w_in, weight, sems)
     me = meta[META_ME]
     model = normed.shape[1]
     width = gains.shape[1]
@@ -1004,23 +1052,23 @@
 
     project_back(normed, weight, gains, head_matrix(256, head), take, d_projected, sums)
     for start in range(0, model, 256):
-        part[:, start : start + 256] = dot(d_projected[...], weight[start : start + 256, 0 : 3 * width], NT).astype(BF)
-
-
-def queries_back(meta, d_queries, d_pairs, normed, near, far, gains, head):
+        part[:, start : start + 256] = dot(d_projected[...], weight[start : start + 256, :], NT).astype(BF)
+
+
+def queries_back(meta, w_in, d_queries, d_pairs, normed, gains, head):
     total, model = normed.shape
     width = gains.shape[1]
     return call(
-        functools.partial(queries_back_kernel, head),
+        with_weights(functools.partial(queries_back_kernel, head), 1, [w_in]),
         (
             jax.ShapeDtypeStruct((total, 3 * width), BF),
             jax.ShapeDtypeStruct((total, model), BF),
             jax.ShapeDtypeStruct((16, width), F32),
         ),
-        [SM] + [VM] * 9 + [ANY, ANY, VM],
+        [SM] + [HBM] * w_in.count + [VM] * 10,
         (VM,) * 3,
         [
-            pltpu.VMEM((model, 4 * width), BF),
+            pltpu.VMEM((model, 3 * width), BF),
             pltpu.VMEM((total, width), F32),
             pltpu.VMEM((total, width), F32),
             pltpu.SemaphoreType.DMA((PIECES,)),
@@ -1028,10 +1076,10 @@
         10 * total * model * width,
         8 * model * width,
         "queries_back",
-    )(meta, *d_queries, *d_pairs, normed, near, far, gains)
-
-
-META_CORE = 4 * PIECES
+    )(meta, *w_in.sources, *d_queries, *d_pairs, normed, gains)
+
+
+META_CORE = 5 * PIECES
 META_ME = META_CORE + 1
 META_SCENES = META_ME + 1
 
@@ -1048,7 +1096,7 @@
     plain = n != PIECES
 
     identity = jnp.arange(PIECES, dtype=jnp.int32)
-    tables = [identity] * 4 if plain else routes.tables()
+    tables = [identity] * 5 if plain else routes.tables()
     scene_here = scene_ids[:, (index // PLANE) * PLANE + jnp.arange(PLANE)]
     before = jnp.sum(scene_ids[:, None, :] < scene_here[:, :, None], axis=-1)
     until = jnp.sum(scene_ids[:, None, :] <= scene_here[:, :, None], axis=-1)
@@ -1066,192 +1114,188 @@
     def own_rows(values):
         return lax.dynamic_index_in_dim(values.reshape(portions, 2, share, -1), core, 1, keepdims=True)
 
-    shards = []
-    for layer in range(2):
-        joined = jnp.concatenate(
-            [input_weight[layer].reshape(-1, 3 * width), output_weight[layer]], axis=1
-        )
-        shards.append((joined, up_weight[layer], down_weight[layer]))
     gains = [jnp.tile(head_gains[layer], (1, width // head)) for layer in range(2)]
-
-    def whole(shard):
-        gathered = lax.all_gather(shard, "frames", axis=0, tiled=True).reshape(PIECES, -1, shard.shape[1])
-        return gathered[: PIECES // 2], gathered[PIECES // 2 :]
-
-    clock = Clock(False)
-    names = ("input", "up", "down")
-    kinds = (True, True, False)
-    if not plain:
-        (ga0, gu0, gd0), (ga1, gu1, gd1) = [
-            [Gather(routes, clock, shard, kinds[at], names[at] + str(layer)) for at, shard in enumerate(shards[layer])]
-            for layer in range(2)
-        ]
-    else:
-        (ga0, gu0, gd0), (ga1, gu1, gd1) = [[Whole(whole(shard)) for shard in layer] for layer in shards]
-
-    def scatter(pair, line_last, name):
-        if plain:
-            rows_ = jnp.concatenate(pair).reshape(model, -1).astype(F32)
-            return Whole(lax.psum_scatter(rows_, "frames", scatter_dimension=0, tiled=True))
-        return Scatter(routes, clock, pair, line_last, name)
-
-    late, wait = clock.late, clock.wait
-
-    ga0.line()
-    gd0.one()
-    gd1.one()
+    clock = Clock(not plain)
+    late, close = clock.late, clock.close
+    joined = [
+        jnp.concatenate([input_weight[layer].reshape(-1, 3 * width), output_weight[layer]], axis=1)
+        for layer in range(2)
+    ]
+
+    def gather(shard, line_first, name):
+        if plain or line_first is None:
+            return Whole(lax.all_gather(shard, "frames", axis=0, tiled=True))
+        return Gather(routes, clock, shard, line_first, name)
+
+    def scatter(line_last, name, lefts, rights):
+        if plain or line_last is None:
+            grad = weight_grad(meta, None, lefts, rights, name)
+            ready[name] = grad
+            summed = lax.psum_scatter(grad.astype(F32) if plain else grad, "frames", scatter_dimension=0, tiled=True)
+            return Whole(summed.astype(F32))
+        parts = weight_grad(meta, (3 if line_last else 2) * PIECES, lefts, rights, name)
+        ready[name] = parts[2]
+        return Scatter(routes, clock, parts, line_last, name)
+
+    ready = {}
+
+    ga0 = gather(joined[0], True, "input0")
+    gu0 = gather(up_weight[0], False, "up0")
+    gd0 = gather(down_weight[0], False, "down0")
+    ga1 = gather(joined[1], False, "input1")
+    gu1 = gather(up_weight[1], False, "up1")
+    gd1 = gather(down_weight[1], False, "down1")
+    ga0.ring(3)
+    for each in (gu0, gd0, ga1, gu1, gd1):
+        each.one()
     rows = all_rows(tokens)
     d_result = all_rows(cotangent)
-    ga0.wait()
-    gd0.wait()
-    gd1.wait()
-    wait(rows, d_result)
+    close(rows, d_result)
     ga0.one()
-    gu0.line()
-    ga0.wait()
-    ga0.two()
-    gu0.wait()
-    gd0.line()
-    w0 = ga0.end()
-    gu0.one()
+    ga0.two(0)
+    gu0.ring(2)
+    close()
+    ga0.two(1)
+    gu0.ring()
+    close()
+    in0, out0 = ga0.end(0, 3 * width), ga0.end(3 * width, width)
+    gu0.two(0)
+    gd0.ring()
     normed0, qkv0, attended0, a0 = attention_frame(
-        meta, late(rows), *w0, norm_params[0], gains[0], frame, head
+        meta, [in0, out0], late(rows), norm_params[0], gains[0], frame, head
     )
-    wait(a0)
-    b0 = routes.swap_parts(a0)
-    gu0.wait()
-    gu0.two()
-    gd0.wait()
-    wait(b0)
-    ga1.line()
+    close(a0)
+    b0 = clock.add(routes.swap(a0))
+    gu0.two(1)
+    gd0.ring()
+    close()
     up0 = gu0.end()
-    gd0.two()
-    mid0, normed_mid0, active0, slope0 = feed_up(meta, rows, a0, late(b0), up0, norm_params[0])
-    wait(active0)
-    ga1.wait()
-    gu1.line()
+    gd0.two(0)
+    gd0.ring()
+    mid0, normed_mid0, active0, slope0 = feed_up(meta, up0, rows, a0, late(b0), norm_params[0])
+    close(active0)
+    gd0.two(1)
+    ga1.ring()
+    close()
     down0 = gd0.end()
-    ga1.one()
-    m0 = feed_down(meta, late(active0), down0)
-    wait(m0)
-    n0 = routes.swap_parts(m0)
-    wait(n0)
-    ga1.wait()
-    ga1.two()
-    gu1.wait()
-    gd1.line()
-    w1 = ga1.end()
-    gu1.one()
+    ga1.two(0)
+    ga1.ring()
+    m0 = feed_down(meta, down0, late(active0), model)
+    close(m0)
+    n0 = clock.add(routes.swap(m0))
+    ga1.ring()
+    close()
+    ga1.two(1)
+    gu1.ring()
+    close()
+    in1, out1 = ga1.end(0, 3 * width), ga1.end(3 * width, width)
+    gu1.two(0)
+    gu1.ring()
     x1, normed1, *slots = queries(
-        meta, mid0, m0, late(n0), *w1, norm_params[0], norm_params[1], gains[1], head
+        meta, in1, mid0, m0, late(n0), norm_params[0], norm_params[1], gains[1], head
     )
-    wait(slots[0])
-    gu1.wait()
-    slots = routes.members(slots)
-    wait(*slots[1:])
-    rise, fall = edges(meta, slots)
+    close(slots[0])
+    slots = routes.members(late(slots))
+    gu1.ring()
+    close(*slots[1:])
+    rise, fall = edges(meta, late(slots))
     below, above = routes.up(rise), routes.down(fall)
-    gu1.two()
-    wait(below, above)
-    gd1.wait()
+    gu1.two(1)
+    close(below, above)
+    gd1.ring()
     *found, sums, whole_found = scene(meta, slots, late(below), above, frame)
-    home = routes.members(found)
+    close(found[0])
+    home = routes.members(late(found))
+    gd1.ring()
+    close(*home[1:])
+    gd1.two(0)
+    gd1.ring()
+    attended1, a1 = outputs(meta, out1, late(home), width, model)
+    b1 = routes.swap(a1)
+    close(b1)
     up1 = gu1.end()
-    gd1.two()
-    wait(*home[1:])
-    attended1, a1 = outputs(meta, late(home), *w1, width)
-    b1 = routes.swap_parts(a1)
-    mid1, normed_mid1, active1, slope1 = feed_up(meta, x1, a1, b1, up1, norm_params[1])
-    wait(active1)
+    gd1.two(1)
+    mid1, normed_mid1, active1, slope1 = feed_up(meta, up1, x1, a1, late(b1), norm_params[1])
+    close(active1)
+
     down1 = gd1.end()
-
-    d_mlp, d_hidden, p = feed_back(meta, late(d_result), slope1, up1, down1, norm_params[1])
-    wait(p)
-    q = routes.swap_parts(p)
-    sd1 = scatter(weight_grad(meta, 3 * PIECES, [late(d_mlp)], [active1], "down_grad"), True, "down_grad1")
-    sd1.two()
-    wait(q)
+    d_mlp, d_hidden, p = feed_back(meta, [down1, up1], late(d_result), slope1, norm_params[1])
+    close(p)
+    q = clock.add(routes.swap(p))
+    sd1 = scatter(True, "down_grad1", [late(d_mlp)], [active1])
+    close(ready["down_grad1"])
+    sd1.two(1)
     g, d_branch, inner1 = norm_back(meta, d_result, mid1, p, late(q), norm_params[1], frame, (a1, b1))
-    d_home = attended_back(meta, d_branch, *w1, width)
-    wait(d_home[0])
-    d_found = routes.members(d_home)
-    su1 = scatter(weight_grad(meta, 2 * PIECES, [normed_mid1], [late(d_hidden)], "up_grad"), False, "up_grad1")
-    wait(su1.give, *d_found[1:])
-    sd1.wait()
+    d_home = attended_back(meta, out1, d_branch, width)
+    su1 = scatter(True, "up_grad1", [late(normed_mid1)], [d_hidden])
+    close(d_home[0], ready["up_grad1"])
+    d_found = routes.members(late(d_home))
+    close(*d_found[1:])
     sd1.one()
-    su1.two()
+    sd1.two(0)
     *d_queries, d_own, d_below, d_above = scene_back(
         meta, slots, late(below), above, sums, whole_found, d_found, frame
     )
-    wait(d_own)
-    from_above, from_below = routes.down(d_below), routes.up(d_above)
-    sd1.wait()
-    su1.wait()
-    sd1.line()
-    d_queries = routes.members(d_queries)
-    m1 = feed_down(meta, late(active1), down1)
-    n1 = routes.swap_parts(m1)
+    close(d_own)
+    from_above, from_below = routes.down(late(d_below)), routes.up(late(d_above))
+    d_queries = routes.members(late(d_queries))
+    su1.two(1)
+    m1 = feed_down(meta, down1, late(active1), model)
+    close(m1, from_above, from_below, *d_queries[1:])
+    n1 = clock.add(routes.swap(m1))
+    sd1.ring()
+    pairs = routes.members(edge_sum(meta, d_own, late(from_below), from_above))
+    close(*pairs[1:])
+    su1.one()
+    sd1.ring()
+    d_projected, p, gain1 = queries_back(meta, in1, d_queries, late(pairs), normed1, gains[1], head)
+    close(p)
+    q = clock.add(routes.swap(p))
+    su1.two(0)
+    sd1.ring()
+    sa1 = scatter(False, "input_grad1", [normed1, d_branch], [late(d_projected), attended1])
+    close(ready["input_grad1"])
+    sa1.two(0)
+    su1.ring()
     own_mlp = own_rows(m1).astype(F32) + own_rows(n1).astype(F32)
     result = own_rows(mid1) + norm_params[1, 5] * own_mlp
     scale1 = jnp.sum(cotangent.astype(F32).reshape(-1, model) * own_mlp.reshape(-1, model), axis=0)
-    wait(m1, from_below, from_above)
-    pairs = routes.members(edge_sum(meta, d_own, late(from_below), from_above))
-    wait(*pairs[1:])
-    wait(*d_queries[1:])
-    su1.line()
-    sd1.wait()
-    d_projected, p, gain1 = queries_back(meta, d_queries, late(pairs), normed1, *w1, gains[1], head)
-    wait(p)
-    q = routes.swap_parts(p)
-    sa1 = scatter(
-        weight_grad(meta, 2 * PIECES, [normed1, d_branch], [late(d_projected), attended1], "input_grad"),
-        False,
-        "input_grad1",
+    g, outer1 = norm_back(meta, g, x1, p, late(q), norm_params[1], frame)
+
+    d_mlp, d_hidden, p = feed_back(meta, [down0, up0], g, slope0, norm_params[0])
+    close(p)
+    q = clock.add(routes.swap(p))
+    sa1.two(1)
+    sa1.ring()
+    su1.ring()
+    sd0 = scatter(False, "down_grad0", [late(d_mlp)], [active0])
+    close(ready["down_grad0"])
+    sd0.two(0)
+    sa1.ring()
+    su1.ring()
+    su0 = scatter(True, "up_grad0", [late(normed_mid0)], [d_hidden])
+    g, d_branch, inner0 = norm_back(meta, g, mid0, p, late(q), norm_params[0], frame, (a0, b0, m0, n0))
+    close(d_branch, ready["up_grad0"])
+    sd0.two(1)
+    su0.two(1)
+    sa1.ring()
+    sd0.ring()
+    d_projected, p, gain0 = frame_back(
+        meta, [in0, out0], late(d_branch), normed0, qkv0, gains[0], frame, head
     )
-    sa1.two()
-    wait(q)
-    g, outer1 = norm_back(meta, g, x1, p, late(q), norm_params[1], frame)
-
-    d_mlp, d_hidden, p = feed_back(meta, g, slope0, up0, down0, norm_params[0])
-    wait(p)
-    q = routes.swap_parts(p)
-    sd0 = scatter(weight_grad(meta, 3 * PIECES, [late(d_mlp)], [active0], "down_grad"), True, "down_grad0")
-    wait(sd0.give, q)
-    sa1.wait()
-    su1.wait()
-    sd0.two()
-    sa1.line()
-    su1.one()
-    su0 = scatter(weight_grad(meta, 3 * PIECES, [normed_mid0], [late(d_hidden)], "up_grad"), True, "up_grad0")
-    g, d_branch, inner0 = norm_back(meta, g, mid0, p, q, norm_params[0], frame, (a0, b0, m0, n0))
-    wait(d_branch, su0.give)
-    sd0.wait()
-    sd0.one()
-    su0.two()
-    d_projected, p, gain0 = frame_back(
-        meta, late(d_branch), normed0, qkv0, *w0, gains[0], frame, head
-    )
-    wait(p)
-    q = routes.swap_parts(p)
-    sd0.wait()
-    su0.wait()
-    sa1.wait()
+    close(p)
+    q = clock.add(routes.swap(late(p)))
+    su0.two(0)
+    sd0.ring()
+    sa1.one()
+    sa0 = scatter(False, "input_grad0", [normed0, d_branch], [late(d_projected), attended0])
+    close(ready["input_grad0"])
     su0.one()
-    sa1.one()
-    sd0.line()
-    sa0 = scatter(
-        weight_grad(meta, 3 * PIECES, [normed0, d_branch], [late(d_projected), attended0], "input_grad"),
-        True,
-        "input_grad0",
-    )
-    wait(sa0.give, q)
-    su0.wait()
-    sa0.two()
+    sa0.two(0)
+    sd0.ring()
     g, outer0 = norm_back(meta, g, rows, p, late(q), norm_params[0], frame)
     token_grad = own_rows(g)
-    wait(g)
-    sd0.wait()
-    su0.line()
+    close(g)
 
     norm_rows = [
         jnp.stack([outer[0], outer[1], inner[2], inner[0], inner[1], scale])
@@ -1262,23 +1306,37 @@
         for gain in (gain0, gain1)
     ]
     gain_rows = jnp.pad(jnp.concatenate(gain_rows, axis=1), ((0, 0), (0, model - 4 * head)))
-    small = routes.total(jnp.concatenate([*norm_rows, gain_rows]))
+    small = jnp.concatenate([*norm_rows, gain_rows])
+    small = small + routes.swap(small)
+    distances = [2**i for i in range(n.bit_length() - 1)]
+
+    def sum_step(block, distance):
+        return block + clock.add(routes.member(late(block), distance))
+
+    small = sum_step(small, distances[0])
+    sa0.two(1)
+    sa0.ring()
+    su0.ring()
+    close()
+    small = sum_step(small, distances[1])
+    sd0.one()
+    sa0.ring()
+    su0.ring()
+    close()
+    for distance in distances[2:]:
+        small = sum_step(small, distance)
+    sa0.ring()
+    su0.ring()
+    sa0.one()
     norm_grad = small[: 2 * 6].reshape(2, 6, model)
     gain_grad = small[2 * 6, : 4 * head].reshape(2, 2, head)
-    wait(small)
-    sa0.wait()
-    sa0.one()
-    su0.wait()
-    sa0.wait()
-    sa0.line()
-    scattered = [[step.run for step in layer] for layer in ((sa0, su0, sd0), (sa1, su1, sd1))]
     return (
         result.astype(BF),
         token_grad,
-        jnp.stack([scattered[layer][0][:, : 3 * width].reshape(-1, 3, width) for layer in range(2)]),
-        jnp.stack([scattered[layer][0][:, 3 * width :] for layer in range(2)]),
-        jnp.stack([scattered[layer][1] for layer in range(2)]),
-        jnp.stack([scattered[layer][2] for layer in range(2)]),
+        jnp.stack([step.run[:, : 3 * width].reshape(-1, 3, width) for step in (sa0, sa1)]),
+        jnp.stack([step.run[:, 3 * width :] for step in (sa0, sa1)]),
+        jnp.stack([step.run for step in (su0, su1)]),
+        jnp.stack([step.run for step in (sd0, sd1)]),
         norm_grad,
         gain_grad,
     )

time: 746 us -> 686 us (0.920)
  the two profiles are of different devices: /device:TPU:1 before, /device:TPU:4 now
where the time goes in v2:
time: 686 us; the launch traced here: 674 us
  waiting for transfers between devices  245 us (36%)
  Pallas kernels  186 us (27%)
  starting transfers between devices  124 us (18%)
  local copies, waits for them, and re-layouts  64.5 us (9%)
  other arithmetic  51.8 us (8%)
    ppermute x72, waiting for transfers between devices, send(): return lax.ppermute(block, AXES, route)  184 us
    ppermute x72, starting transfers between devices, send(): return lax.ppermute(block, AXES, route)  82.1 us
    unnamed x304, local copies, waits for them, and re-layouts  47.6 us
    ppermute x19, waiting for transfers between devices, member(): lax.ppermute(block, 'frames', [(f, f ^ distance) for f in range(self.n)])  42.2 us
    ppermute x19, starting transfers between devices, member(): lax.ppermute(block, 'frames', [(f, f ^ distance) for f in range(self.n)])  29.9 us
    pallas_call x6, Pallas kernels, weight_grad(): call(functools.partial(weight_grad_kernel, base, widths), jax.ShapeDtypeS...  28.3 us
    pallas_call x1, Pallas kernels, scene_back(): call(functools.partial(scene_back_kernel, frame), (out,) * 4 + (jax.Shape...  23.9 us
    pallas_call x1, Pallas kernels, frame_back(): call(with_weights(functools.partial(frame_back_kernel, frame, head), 1, w...  22.6 us
  transfers between devices with their start and end apart: 106, of which 48 were waited for; matrix products, arithmetic and copies ran while one was open for 10% of the time, Pallas kernels for 27%

profile of v2, /device:TPU:4, one launch (start us, length us, event | category | flops | bytes accessed | tf_op | source)
XLA Modules:
  0.0 674.3 jit_solution(7409940979576308551)
XLA Ops:
  16.4 4.3 collective-permute-done.3
  41.5 8.2 %collective-permute-done.12 = bf16[2,64,2048]{2,1,0:T(8,128)(2,1)} collective-permute-done((bf16[2,64,2048]{2,1,0:T(8,128)(2,1)}, bf16[2,64,2048]{2,1,0:T(8,128)(2,1)}, u32[]{:S(2)}, u32[]{:S(2)}) %collective-permute-start.12) | collective-permute-done | bytes 524320 | tf_op jit(solution)/shard_map/up0_ring/ppermute | solution.py:65
  51.2 7.0 %collective-permute-done.10.refs_2_.refs_6_ = bf16[4,64,2048]{2,1,0:T(8,128)(2,1)S(1)} collective-permute-done((bf16[4,64,2048]{2,1,0:T(8,128)(2,1)S(1)}, bf16[4,64,2048]{2,1,0:T(8,128)(2,1)S(1)}, u32[]{:S(2)}, u32[]{:S(2)}) %collective-permute-start.10) | collective-permute-done | bytes 1048608 | tf_op jit(solution)/shard_map/input0_one/ppermute | solution.py:65
  58.2 3.7 collective-permute-done.13
  70.5 5.5 collective-permute-done.15
  84.5 16.1 %attention_frame.1 = (bf16[512,1024]{1,0:T(8,128)(2,1)S(1)}, bf16[3,512,512]{2,1,0:T(8,128)(2,1)S(1)}, bf16[512,512]{1,0:T(8,128)(2,1)S(1)}, bf16[512,1024]{1,0:T(8,128)(2,1)S(1)}) custom-call(s32[98]{0:T(128)S(1)} %concatenate.51.refs_0_.meta, bf16[4,64,2048]{2,1,0:T(8,128)(2,1)S(1)} %pad_maximum_fusion.refs_1_.refs_5_, ...), custom_call_target="tpu_custom_call" | custom-call | flops 2147483648 | bytes 4194304 | tf_op jit(solution)/shard_map/attention_frame/pallas_call | solution.py:395
  106.1 11.6 %collective-permute-done.18 = bf16[2,64,2048]{2,1,0:T(8,128)(2,1)S(1)} collective-permute-done((bf16[2,64,2048]{2,1,0:T(8,128)(2,1)S(1)}, bf16[2,64,2048]{2,1,0:T(8,128)(2,1)S(1)}, u32[]{:S(2)}, u32[]{:S(2)}) %collective-permute-start.18) | collective-permute-done | bytes 524320 | tf_op jit(solution)/shard_map/down0_ring/ppermute | solution.py:65
  120.8 9.4 %feed_up.2 = (f32[512,1024]{1,0:T(8,128)S(1)}, bf16[512,1024]{1,0:T(8,128)(2,1)S(1)}, bf16[512,2048]{1,0:T(8,128)(2,1)S(1)}, bf16[512,2048]{1,0:T(8,128)(2,1)S(1)}) custom-call(s32[98]{0:T(128)S(1)} %concatenate.51.refs_0_.meta, bf16[4,64,2048]{2,1,0:T(8,128)(2,1)} %pad_maximum_fusion.2.refs_1_.refs_5_, ...), custom_call_target="tpu_custom_call" | custom-call | flops 2147483648 | bytes 4194304 | tf_op jit(solution)/shard_map/feed_up/pallas_call | solution.py:446
  136.1 12.8 %collective-permute-done.24 = bf16[2,64,2048]{2,1,0:T(8,128)(2,1)S(1)} collective-permute-done((bf16[2,64,2048]{2,1,0:T(8,128)(2,1)S(1)}, bf16[2,64,2048]{2,1,0:T(8,128)(2,1)S(1)}, u32[]{:S(2)}, u32[]{:S(2)}) %collective-permute-start.24) | collective-permute-done | bytes 524320 | tf_op jit(solution)/shard_map/input1_ring/ppermute | solution.py:65
  153.9 8.4 %collective-permute-done.26 = bf16[2,64,2048]{2,1,0:T(8,128)(2,1)S(1)} collective-permute-done((bf16[2,64,2048]{2,1,0:T(8,128)(2,1)S(1)}, bf16[2,64,2048]{2,1,0:T(8,128)(2,1)S(1)}, u32[]{:S(2)}, u32[]{:S(2)}) %collective-permute-start.26) | collective-permute-done | bytes 524320 | tf_op jit(solution)/shard_map/input1_ring/ppermute | solution.py:65
  165.2 10.4 %collective-permute-done.28 = bf16[2,64,2048]{2,1,0:T(8,128)(2,1)S(1)} collective-permute-done((bf16[2,64,2048]{2,1,0:T(8,128)(2,1)S(1)}, bf16[2,64,2048]{2,1,0:T(8,128)(2,1)S(1)}, u32[]{:S(2)}, u32[]{:S(2)}) %collective-permute-start.28) | collective-permute-done | bytes 524320 | tf_op jit(solution)/shard_map/input1_ring/ppermute | solution.py:65
  178.3 11.5 %collective-permute-done.29 = bf16[2,64,2048]{2,1,0:T(8,128)(2,1)} collective-permute-done((bf16[2,64,2048]{2,1,0:T(8,128)(2,1)S(1)}, bf16[2,64,2048]{2,1,0:T(8,128)(2,1)}, u32[]{:S(2)}, u32[]{:S(2)}) %collective-permute-start.29) | collective-permute-done | bytes 524320 | tf_op jit(solution)/shard_map/up1_ring/ppermute | solution.py:65
  200.8 11.3 %queries.1 = (f32[512,1024]{1,0:T(8,128)S(1)}, bf16[512,1024]{1,0:T(8,128)(2,1)S(1)}, bf16[3,512,128]{2,1,0:T(8,128)(2,1)S(1)}, bf16[3,512,128]{2,1,0:T(8,128)(2...) custom-call(s32[98]{0:T(128)S(1)} %concatenate.51.refs_0_.meta, ...), custom_call_target="tpu_custom_call" | custom-call | flops 1610612736 | bytes 4194304 | tf_op jit(solution)/shard_map/queries/pallas_call | solution.py:514
  221.3 3.9 collective-permute-done.33
  228.4 4.6 collective-permute-done.35.s2
  239.2 13.9 %collective-permute-done.38.below = bf16[3,2,512,128]{3,2,1,0:T(8,128)(2,1)S(1)} collective-permute-done((bf16[3,2,512,128]{3,2,1,0:T(8,128)(2,1)S(1)}, bf16[3,2,512,128]{3,2,1,0:T(8,128)(2,1)S(1)}, u32[]{:S(2)}, u32[]{:S(2)}) %collective-permute-start.38) | collective-permute-done | bytes 786464 | tf_op jit(solution)/shard_map/ppermute | solution.py:83
  253.1 4.2 collective-permute-done.39.above
  257.5 11.8 %scene.1 = (bf16[512,128]{1,0:T(8,128)(2,1)S(1)}, bf16[512,128]{1,0:T(8,128)(2,1)S(1)}, bf16[512,128]{1,0:T(8,128)(2,1)S(1)}, bf16[512,128]{1,0:T(8,128)(2,1)S(1...) custom-call(s32[98]{0:T(128)S(1)} %concatenate.51.refs_0_.meta, ...), custom_call_target="tpu_custom_call" | custom-call | flops 2147483648 | bytes 2621440 | tf_op jit(solution)/shard_map/scene/pallas_call | solution.py:609
  270.9 5.9 collective-permute-start.42
  280.5 3.7 collective-permute-done.43.refs_8_
  287.0 15.5 %collective-permute-done.47 = bf16[2,64,2048]{2,1,0:T(8,128)(2,1)S(1)} collective-permute-done((bf16[2,64,2048]{2,1,0:T(8,128)(2,1)S(1)}, bf16[2,64,2048]{2,1,0:T(8,128)(2,1)S(1)}, u32[]{:S(2)}, u32[]{:S(2)}) %collective-permute-start.47) | collective-permute-done | bytes 524320 | tf_op jit(solution)/shard_map/down1_ring/ppermute | solution.py:65
  304.6 9.4 %feed_up.3 = (f32[512,1024]{1,0:T(8,128)S(1)}, bf16[512,1024]{1,0:T(8,128)(2,1)S(1)}, bf16[512,2048]{1,0:T(8,128)(2,1)S(1)}, bf16[512,2048]{1,0:T(8,128)(2,1)S(1)}) custom-call(s32[98]{0:T(128)S(1)} %concatenate.51.refs_0_.meta, bf16[4,64,2048]{2,1,0:T(8,128)(2,1)} %pad_maximum_fusion.4.refs_1_.refs_5_, ...), custom_call_target="tpu_custom_call" | custom-call | flops 2147483648 | bytes 4194304 | tf_op jit(solution)/shard_map/feed_up/pallas_call | solution.py:446
  317.4 6.4 feed_back.2
  323.9 4.7 down_grad1.1
  336.1 4.8 up_grad1.1
  349.8 3.8 collective-permute-done.52.g2
  355.2 23.9 %scene_back.1 = (bf16[512,128]{1,0:T(8,128)(2,1)S(1)}, bf16[512,128]{1,0:T(8,128)(2,1)S(1)}, bf16[512,128]{1,0:T(8,128)(2,1)S(1)}, bf16[512,128]{1,0:T(8,128)(2,...) custom-call(s32[98]{0:T(128)S(1)} %concatenate.51.refs_0_.meta, ...), custom_call_target="tpu_custom_call" | custom-call | flops 5368709120 | bytes 5242880 | tf_op jit(solution)/shard_map/scene_back/pallas_call | solution.py:990
  390.4 4.3 collective-permute-start.56
  400.1 3.9 collective-permute-done.59.refs_8_
  413.5 3.6 collective-permute-done.64.refs_11_
  433.6 12.7 %queries_back.1 = (bf16[512,1536]{1,0:T(8,128)(2,1)S(1)}, bf16[512,1024]{1,0:T(8,128)(2,1)}, f32[16,512]{1,0:T(8,128)S(1)}) custom-call(s32[98]{0:T(128)S(1)} %concatenate.51.refs_0_.meta, bf16[4,64,2048]{2,1,0:T(8,128)(2,1)S(1)} %pad_maximum_fusion.3.refs_1_, bf16[4,64,2048]{2,1,0:T(8,128)(2,1)S(1)} %copy-done.5, bf16[4,64,2048]{2,1,0:T(8,128)(2,1)S(1)} %copy-done.11, ...), custom_call_target="tpu_custom_call" | custom-call | flops 2684354560 | bytes 4194304 | tf_op jit(solution)/shard_map/queries_back/pallas_call | solution.py:1061
  454.7 4.4 input_grad1.1
  467.1 4.3 norm_back.2
  471.6 6.3 feed_back.3
  482.2 4.9 down_grad0.1
  491.7 9.6 %collective-permute-done.76 = bf16[2,64,2048]{2,1,0:T(8,128)(2,1)S(1)} collective-permute-done((bf16[2,64,2048]{2,1,0:T(8,128)(2,1)S(1)}, bf16[2,64,2048]{2,1,0:T(8,128)(2,1)S(1)}, u32[]{:S(2)}, u32[]{:S(2)}) %collective-permute-start.76) | collective-permute-done | bytes 524320 | tf_op jit(solution)/shard_map/input_grad1_ring/ppermute | solution.py:65
  503.7 5.1 up_grad0.1
  510.8 3.8 norm_back_inner.3
  516.9 4.4 collective-permute-done.79
  528.1 22.6 %frame_back.1 = (bf16[512,1536]{1,0:T(8,128)(2,1)S(1)}, bf16[512,1024]{1,0:T(8,128)(2,1)}, f32[16,512]{1,0:T(8,128)S(1)}) custom-call(s32[98]{0:T(128)S(1)} %concatenate.51.refs_0_.meta, bf16[4,64,2048]{2,1,0:T(8,128)(2,1)S(1)} %pad_maximum_fusion.refs_1_.refs_5_, bf16[4,64,2048]{2,1,0:T(8,128)(2,1)S(1)} %collective-permute-done.10.refs_2_.refs_6_, ...), custom_call_target="tpu_custom_call" | custom-call | flops 3221225472 | bytes 4194304 | tf_op jit(solution)/shard_map/frame_back/pallas_call | solution.py:886
  556.2 4.5 input_grad0.1
  564.3 6.3 collective-permute-done.87
  581.5 3.9 norm_back.3
  591.0 8.6 %collective-permute-done.89 = bf16[4,64,2048]{2,1,0:T(8,128)(2,1)} collective-permute-done((bf16[4,64,2048]{2,1,0:T(8,128)(2,1)}, bf16[4,64,2048]{2,1,0:T(8,128)(2,1)}, u32[]{:S(2)}, u32[]{:S(2)}) %collective-permute-start.89) | collective-permute-done | bytes 1048608 | tf_op jit(solution)/shard_map/input_grad0_two/ppermute | solution.py:65
  606.7 10.1 %collective-permute-done.93 = bf16[2,64,2048]{2,1,0:T(8,128)(2,1)S(1)} collective-permute-done((bf16[2,64,2048]{2,1,0:T(8,128)(2,1)S(1)}, bf16[2,64,2048]{2,1,0:T(8,128)(2,1)S(1)}, u32[]{:S(2)}, u32[]{:S(2)}) %collective-permute-start.93) | collective-permute-done | bytes 524320 | tf_op jit(solution)/shard_map/input_grad0_ring/ppermute | solution.py:65
  617.0 4.3 collective-permute-done.96
  628.4 8.7 %collective-permute-done.97 = bf16[2,64,2048]{2,1,0:T(8,128)(2,1)S(1)} collective-permute-done((bf16[2,64,2048]{2,1,0:T(8,128)(2,1)S(1)}, bf16[2,64,2048]{2,1,0:T(8,128)(2,1)S(1)}, u32[]{:S(2)}, u32[]{:S(2)}) %collective-permute-start.97) | collective-permute-done | bytes 524320 | tf_op jit(solution)/shard_map/input_grad0_ring/ppermute | solution.py:65
  647.4 8.7 %collective-permute-done.104 = f32[13,1024]{1,0:T(8,128)S(1)} collective-permute-done((f32[13,1024]{1,0:T(8,128)S(1)}, f32[13,1024]{1,0:T(8,128)S(1)}, u32[]{:S(2)}, u32[]{:S(2)}) %collective-permute-start.104) | collective-permute-done | bytes 53280 | tf_op jit(solution)/shard_map/ppermute | solution.py:77
  (615 shorter events, 289.8 us)
Async XLA Ops:
  2.8 28.4 %collective-permute-start.7 = (bf16[64,2048]{1,0:T(8,128)(2,1)}, bf16[64,2048]{1,0:T(8,128)(2,1)S(1)}, u32[]{:S(2)}, u32[]{:S(2)}) collective-permute-start(bf16[64,2048]{1,0:T(8,128)(2,1)} %get-tuple-element.452), channel_id=1, source_target_pairs={{0,2},{1,5},{2,0},{3,7},{4,6},{5,1},{6,4},{7,3},{8,10},{9,13},{10,... | collective-permute-start | bytes 786440 | tf_op jit(solution)/shard_map/down1_one/ppermute | solution.py:65
  8.6 17.9 %collective-permute-start.9 = (bf16[2,128,1024]{2,1,0:T(8,128)(2,1)S(1)}, bf16[2,128,1024]{2,1,0:T(8,128)(2,1)S(1)}, u32[]{:S(2)}, u32[]{:S(2)}) collective-permute-start(bf16[2,128,1024]{2,1,0:T(8,128)(2,1)S(1)} %bitcast.157), channel_id=1, source_target_pairs={{0,1},{1,0},{2,3},{3,2},{4,5},{5,4},{6,7},{7,6},{8,9},{9,8},{10,11... | collective-permute-start | bytes 1572872 | tf_op jit(solution)/shard_map/ppermute | solution.py:68
  14.4 16.8 %collective-permute-start = (bf16[64,2048]{1,0:T(8,128)(2,1)}, bf16[64,2048]{1,0:T(8,128)(2,1)S(1)}, u32[]{:S(2)}, u32[]{:S(2)}) collective-permute-start(bf16[64,2048]{1,0:T(8,128)(2,1)} %get-tuple-element.455), channel_id=1, source_target_pairs={{0,2},{1,5},{2,0},{3,7},{4,6},{5,1},{6,4},{7,3},{8,10},{9,13},{10,... | collective-permute-start | bytes 786440 | tf_op jit(solution)/shard_map/up1_one/ppermute | solution.py:65
  33.7 24.4 %collective-permute-start.10 = (bf16[4,64,2048]{2,1,0:T(8,128)(2,1)S(1)}, bf16[4,64,2048]{2,1,0:T(8,128)(2,1)S(1)}, u32[]{:S(2)}, u32[]{:S(2)}) collective-permute-start(bf16[4,64,2048]{2,1,0:T(8,128)(2,1)S(1)} %pad_maximum_fusion.refs_1_.refs_5_), channel_id=1, source_target_pairs={{0,2},{1,5},{2,0},{3,7},{4,6},{5,1},{6,4},{7,3},{8,10},{9,13},{10,... | collective-permute-start | bytes 3145736 | tf_op jit(solution)/shard_map/input0_one/ppermute | solution.py:65
  34.3 23.9 %collective-permute-start.11 = (bf16[4,64,2048]{2,1,0:T(8,128)(2,1)S(1)}, bf16[4,64,2048]{2,1,0:T(8,128)(2,1)S(1)}, u32[]{:S(2)}, u32[]{:S(2)}) collective-permute-start(bf16[4,64,2048]{2,1,0:T(8,128)(2,1)S(1)} %pad_maximum_fusion.refs_1_.refs_5_), channel_id=1, source_target_pairs={{0,4},{1,3},{2,6},{3,1},{4,0},{5,7},{6,2},{7,5},{8,12},{9,11},{10,... | collective-permute-start | bytes 3145736 | tf_op jit(solution)/shard_map/input0_two/ppermute | solution.py:65
  61.9 16.4 %collective-permute-start.14 = (bf16[4,64,2048]{2,1,0:T(8,128)(2,1)S(1)}, bf16[4,64,2048]{2,1,0:T(8,128)(2,1)}, u32[]{:S(2)}, u32[]{:S(2)}) collective-permute-start(bf16[4,64,2048]{2,1,0:T(8,128)(2,1)S(1)} %collective-permute-done.10.refs_2_.refs_6_), channel_id=1, source_target_pairs={{0,4},{1,3},{2,6},{3,1},{4,0},{5,7},{6,2},{7,5},{8,12},{9,11},{10,... | collective-permute-start | bytes 3145736 | tf_op jit(solution)/shard_map/input0_two/ppermute | solution.py:65
  78.3 24.2 %collective-permute-start.17 = (bf16[4,64,2048]{2,1,0:T(8,128)(2,1)}, bf16[4,64,2048]{2,1,0:T(8,128)(2,1)}, u32[]{:S(2)}, u32[]{:S(2)}) collective-permute-start(bf16[4,64,2048]{2,1,0:T(8,128)(2,1)} %pad_maximum_fusion.2.refs_1_.refs_5_), channel_id=1, source_target_pairs={{0,4},{1,3},{2,6},{3,1},{4,0},{5,7},{6,2},{7,5},{8,12},{9,11},{10,... | collective-permute-start | bytes 3145736 | tf_op jit(solution)/shard_map/up0_two/ppermute | solution.py:65
  81.7 20.8 %collective-permute-start.16 = (bf16[2,64,2048]{2,1,0:T(8,128)(2,1)S(1)}, bf16[2,64,2048]{2,1,0:T(8,128)(2,1)S(1)}, u32[]{:S(2)}, u32[]{:S(2)}) collective-permute-start(bf16[2,64,2048]{2,1,0:T(8,128)(2,1)S(1)} %pad_maximum_fusion.10), channel_id=1, source_target_pairs={{0,8},{1,9},{2,10},{3,11},{4,12},{5,13},{6,14},{7,15},{8,24},{9,25... | collective-permute-start | bytes 1572872 | tf_op jit(solution)/shard_map/down0_ring/ppermute | solution.py:65
  132.8 16.2 %collective-permute-start.23 = (bf16[4,64,2048]{2,1,0:T(8,128)(2,1)S(1)}, bf16[4,64,2048]{2,1,0:T(8,128)(2,1)S(1)}, u32[]{:S(2)}, u32[]{:S(2)}) collective-permute-start(bf16[4,64,2048]{2,1,0:T(8,128)(2,1)S(1)} %constant_dynamic-update-slice_fusion.2.refs_2_), channel_id=1, source_target_pairs={{0,4},{1,3},{2,6},{3,1},{4,0},{5,7},{6,2},{7,5},{8,12},{9,11},{10,... | collective-permute-start | bytes 3145736 | tf_op jit(solution)/shard_map/down0_two/ppermute | solution.py:65
  153.8 21.8 %collective-permute-start.25 = (bf16[512,1024]{1,0:T(8,128)(2,1)S(1)}, bf16[512,1024]{1,0:T(8,128)(2,1)S(1)}, u32[]{:S(2)}, u32[]{:S(2)}) collective-permute-start(bf16[512,1024]{1,0:T(8,128)(2,1)S(1)} %feed_down.2.refs_6_.refs_7_), channel_id=1, source_target_pairs={{0,1},{1,0},{2,3},{3,2},{4,5},{5,4},{6,7},{7,6},{8,9},{9,8},{10,11... | collective-permute-start | bytes 3145736 | tf_op jit(solution)/shard_map/ppermute | solution.py:68
  176.6 15.3 %collective-permute-start.30 = (bf16[4,64,2048]{2,1,0:T(8,128)(2,1)S(1)}, bf16[4,64,2048]{2,1,0:T(8,128)(2,1)S(1)}, u32[]{:S(2)}, u32[]{:S(2)}) collective-permute-start(bf16[4,64,2048]{2,1,0:T(8,128)(2,1)S(1)} %constant_dynamic-update-slice_fusion.4.refs_2_), channel_id=1, source_target_pairs={{0,4},{1,3},{2,6},{3,1},{4,0},{5,7},{6,2},{7,5},{8,12},{9,11},{10,... | collective-permute-start | bytes 3145736 | tf_op jit(solution)/shard_map/input1_two/ppermute | solution.py:65
  192.9 20.3 %collective-permute-start.32 = (bf16[4,64,2048]{2,1,0:T(8,128)(2,1)}, bf16[4,64,2048]{2,1,0:T(8,128)(2,1)}, u32[]{:S(2)}, u32[]{:S(2)}) collective-permute-start(bf16[4,64,2048]{2,1,0:T(8,128)(2,1)} %pad_maximum_fusion.4.refs_1_.refs_5_), channel_id=1, source_target_pairs={{0,4},{1,3},{2,6},{3,1},{4,0},{5,7},{6,2},{7,5},{8,12},{9,11},{10,... | collective-permute-start | bytes 3145736 | tf_op jit(solution)/shard_map/up1_two/ppermute | solution.py:65
  193.0 20.2 %collective-permute-start.31 = (bf16[2,64,2048]{2,1,0:T(8,128)(2,1)}, bf16[2,64,2048]{2,1,0:T(8,128)(2,1)}, u32[]{:S(2)}, u32[]{:S(2)}) collective-permute-start(bf16[2,64,2048]{2,1,0:T(8,128)(2,1)} %collective-permute-done.29), channel_id=1, source_target_pairs={{0,8},{1,9},{2,10},{3,11},{4,12},{5,13},{6,14},{7,15},{8,24},{9,25... | collective-permute-start | bytes 1572872 | tf_op jit(solution)/shard_map/up1_ring/ppermute | solution.py:65
  217.5 15.5 %collective-permute-start.35 = (bf16[3,512,128]{2,1,0:T(8,128)(2,1)S(1)}, bf16[3,512,128]{2,1,0:T(8,128)(2,1)S(1)}, u32[]{:S(2)}, u32[]{:S(2)}) collective-permute-start(bf16[3,512,128]{2,1,0:T(8,128)(2,1)S(1)} %get-tuple-element.247), channel_id=1, source_target_pairs={{0,4},{2,6},{4,0},{6,2},{8,12},{10,14},{12,8},{14,10},{16,20},{18,... | collective-permute-start | bytes 1179656 | tf_op jit(solution)/shard_map/ppermute | solution.py:77
  233.0 24.3 %collective-permute-start.37 = (bf16[4,64,2048]{2,1,0:T(8,128)(2,1)S(1)}, bf16[4,64,2048]{2,1,0:T(8,128)(2,1)S(1)}, u32[]{:S(2)}, u32[]{:S(2)}) collective-permute-start(bf16[4,64,2048]{2,1,0:T(8,128)(2,1)S(1)} %constant_dynamic-update-slice_fusion.6.refs_2_.refs_6_), channel_id=1, source_target_pairs={{0,4},{1,3},{2,6},{3,1},{4,0},{5,7},{6,2},{7,5},{8,12},{9,11},{10,... | collective-permute-start | bytes 3145736 | tf_op jit(solution)/shard_map/up1_two/ppermute | solution.py:65
  235.5 17.6 %collective-permute-start.38 = (bf16[3,2,512,128]{3,2,1,0:T(8,128)(2,1)S(1)}, bf16[3,2,512,128]{3,2,1,0:T(8,128)(2,1)S(1)}, u32[]{:S(2)}, u32[]{:S(2)}) collective-permute-start(bf16[3,2,512,128]{3,2,1,0:T(8,128)(2,1)S(1)} %get-tuple-element.256), channel_id=1, source_target_pairs={{0,8},{2,10},{4,12},{6,14},{8,16},{10,18},{12,20},{14,22},{16,24},... | collective-permute-start | bytes 2359304 | tf_op jit(solution)/shard_map/ppermute | solution.py:83
  237.8 19.5 %collective-permute-start.39 = (bf16[3,2,512,128]{3,2,1,0:T(8,128)(2,1)S(1)}, bf16[3,2,512,128]{3,2,1,0:T(8,128)(2,1)S(1)}, u32[]{:S(2)}, u32[]{:S(2)}) collective-permute-start(bf16[3,2,512,128]{3,2,1,0:T(8,128)(2,1)S(1)} %get-tuple-element.257), channel_id=1, source_target_pairs={{8,0},{10,2},{12,4},{14,6},{16,8},{18,10},{20,12},{22,14},{24,16},... | collective-permute-start | bytes 2359304 | tf_op jit(solution)/shard_map/ppermute | solution.py:86
  284.2 18.3 %collective-permute-start.46 = (bf16[4,64,2048]{2,1,0:T(8,128)(2,1)S(1)}, bf16[4,64,2048]{2,1,0:T(8,128)(2,1)S(1)}, u32[]{:S(2)}, u32[]{:S(2)}) collective-permute-start(bf16[4,64,2048]{2,1,0:T(8,128)(2,1)S(1)} %pad_maximum_fusion.5.refs_1_), channel_id=1, source_target_pairs={{0,4},{1,3},{2,6},{3,1},{4,0},{5,7},{6,2},{7,5},{8,12},{9,11},{10,... | collective-permute-start | bytes 3145736 | tf_op jit(solution)/shard_map/down1_two/ppermute | solution.py:65
  286.8 15.7 %collective-permute-start.45 = (bf16[512,1024]{1,0:T(8,128)(2,1)S(1)}, bf16[512,1024]{1,0:T(8,128)(2,1)S(1)}, u32[]{:S(2)}, u32[]{:S(2)}) collective-permute-start(bf16[512,1024]{1,0:T(8,128)(2,1)S(1)} %get-tuple-element.273.refs_6_.refs_5_), channel_id=1, source_target_pairs={{0,1},{1,0},{2,3},{3,2},{4,5},{5,4},{6,7},{7,6},{8,9},{9,8},{10,11... | collective-permute-start | bytes 3145736 | tf_op jit(solution)/shard_map/ppermute | solution.py:68
  286.8 15.7 %collective-permute-start.47 = (bf16[2,64,2048]{2,1,0:T(8,128)(2,1)S(1)}, bf16[2,64,2048]{2,1,0:T(8,128)(2,1)S(1)}, u32[]{:S(2)}, u32[]{:S(2)}) collective-permute-start(bf16[2,64,2048]{2,1,0:T(8,128)(2,1)S(1)} %collective-permute-done.44), channel_id=1, source_target_pairs={{0,8},{1,9},{2,10},{3,11},{4,12},{5,13},{6,14},{7,15},{8,24},{9,25... | collective-permute-start | bytes 1572872 | tf_op jit(solution)/shard_map/down1_ring/ppermute | solution.py:65
  353.6 26.2 %collective-permute-start.54 = (bf16[4,64,2048]{2,1,0:T(8,128)(2,1)S(1)}, bf16[4,64,2048]{2,1,0:T(8,128)(2,1)S(1)}, u32[]{:S(2)}, u32[]{:S(2)}) collective-permute-start(bf16[4,64,2048]{2,1,0:T(8,128)(2,1)S(1)} %add_convert_fusion.2), channel_id=1, source_target_pairs={{0,2},{1,5},{2,0},{3,7},{4,6},{5,1},{6,4},{7,3},{8,10},{9,13},{10,... | collective-permute-start | bytes 3145736 | tf_op jit(solution)/shard_map/down_grad1_one/ppermute | solution.py:65
  354.1 25.7 %collective-permute-start.55 = (bf16[4,64,2048]{2,1,0:T(8,128)(2,1)S(1)}, bf16[4,64,2048]{2,1,0:T(8,128)(2,1)S(1)}, u32[]{:S(2)}, u32[]{:S(2)}) collective-permute-start(bf16[4,64,2048]{2,1,0:T(8,128)(2,1)S(1)} %get-tuple-element.303), channel_id=1, source_target_pairs={{0,4},{1,3},{2,6},{3,1},{4,0},{5,7},{6,2},{7,5},{8,12},{9,11},{10,... | collective-permute-start | bytes 3145736 | tf_op jit(solution)/shard_map/down_grad1_two/ppermute | solution.py:65
  379.8 24.9 %collective-permute-start.61 = (bf16[4,64,2048]{2,1,0:T(8,128)(2,1)S(1)}, bf16[4,64,2048]{2,1,0:T(8,128)(2,1)S(1)}, u32[]{:S(2)}, u32[]{:S(2)}) collective-permute-start(bf16[4,64,2048]{2,1,0:T(8,128)(2,1)S(1)} %get-tuple-element.322), channel_id=1, source_target_pairs={{0,4},{1,3},{2,6},{3,1},{4,0},{5,7},{6,2},{7,5},{8,12},{9,11},{10,... | collective-permute-start | bytes 3145736 | tf_op jit(solution)/shard_map/up_grad1_two/ppermute | solution.py:65
  380.7 23.9 %collective-permute-start.60 = (bf16[3,2,512,128]{3,2,1,0:T(8,128)(2,1)S(1)}, bf16[3,2,512,128]{3,2,1,0:T(8,128)(2,1)S(1)}, u32[]{:S(2)}, u32[]{:S(2)}) collective-permute-start(bf16[3,2,512,128]{3,2,1,0:T(8,128)(2,1)S(1)} %get-tuple-element.320), channel_id=1, source_target_pairs={{0,8},{2,10},{4,12},{6,14},{8,16},{10,18},{12,20},{14,22},{16,24},... | collective-permute-start | bytes 2359304 | tf_op jit(solution)/shard_map/ppermute | solution.py:83
  382.6 22.0 %collective-permute-start.62 = (bf16[3,2,512,128]{3,2,1,0:T(8,128)(2,1)S(1)}, bf16[3,2,512,128]{3,2,1,0:T(8,128)(2,1)S(1)}, u32[]{:S(2)}, u32[]{:S(2)}) collective-permute-start(bf16[3,2,512,128]{3,2,1,0:T(8,128)(2,1)S(1)} %get-tuple-element.324), channel_id=1, source_target_pairs={{8,0},{10,2},{12,4},{14,6},{16,8},{18,10},{20,12},{22,14},{24,16},... | collective-permute-start | bytes 2359304 | tf_op jit(solution)/shard_map/ppermute | solution.py:86
  390.4 21.4 %collective-permute-start.56 = (bf16[512,1024]{1,0:T(8,128)(2,1)S(1)}, bf16[512,1024]{1,0:T(8,128)(2,1)S(1)}, u32[]{:S(2)}, u32[]{:S(2)}) collective-permute-start(bf16[512,1024]{1,0:T(8,128)(2,1)S(1)} %feed_down.3), channel_id=1, source_target_pairs={{0,1},{1,0},{2,3},{3,2},{4,5},{5,4},{6,7},{7,6},{8,9},{9,8},{10,11... | collective-permute-start | bytes 3145736 | tf_op jit(solution)/shard_map/ppermute | solution.py:68
  417.1 29.2 %collective-permute-start.68 = (bf16[4,64,2048]{2,1,0:T(8,128)(2,1)}, bf16[4,64,2048]{2,1,0:T(8,128)(2,1)}, u32[]{:S(2)}, u32[]{:S(2)}) collective-permute-start(bf16[4,64,2048]{2,1,0:T(8,128)(2,1)} %add_convert_fusion.1), channel_id=1, source_target_pairs={{0,2},{1,5},{2,0},{3,7},{4,6},{5,1},{6,4},{7,3},{8,10},{9,13},{10,... | collective-permute-start | bytes 3145736 | tf_op jit(solution)/shard_map/up_grad1_one/ppermute | solution.py:65
  419.6 26.8 %collective-permute-start.69 = (bf16[64,2048]{1,0:T(8,128)(2,1)}, bf16[64,2048]{1,0:T(8,128)(2,1)}, u32[]{:S(2)}, u32[]{:S(2)}) collective-permute-start(bf16[64,2048]{1,0:T(8,128)(2,1)} %fusion.12), channel_id=1, source_target_pairs={{0,8},{1,9},{2,10},{3,11},{4,12},{5,13},{6,14},{7,15},{8,24},{9,25... | collective-permute-start | bytes 786440 | tf_op jit(solution)/shard_map/down_grad1_ring/ppermute | solution.py:65
  461.6 17.7 %collective-permute-start.73 = (bf16[4,64,2048]{2,1,0:T(8,128)(2,1)S(1)}, bf16[4,64,2048]{2,1,0:T(8,128)(2,1)S(1)}, u32[]{:S(2)}, u32[]{:S(2)}) collective-permute-start(bf16[4,64,2048]{2,1,0:T(8,128)(2,1)S(1)} %get-tuple-element.352), channel_id=1, source_target_pairs={{0,4},{1,3},{2,6},{3,1},{4,0},{5,7},{6,2},{7,5},{8,12},{9,11},{10,... | collective-permute-start | bytes 3145736 | tf_op jit(solution)/shard_map/input_grad1_two/ppermute | solution.py:65
  479.3 22.0 %collective-permute-start.75 = (bf16[4,64,2048]{2,1,0:T(8,128)(2,1)S(1)}, bf16[4,64,2048]{2,1,0:T(8,128)(2,1)S(1)}, u32[]{:S(2)}, u32[]{:S(2)}) collective-permute-start(bf16[4,64,2048]{2,1,0:T(8,128)(2,1)S(1)} %get-tuple-element.355), channel_id=1, source_target_pairs={{0,4},{1,3},{2,6},{3,1},{4,0},{5,7},{6,2},{7,5},{8,12},{9,11},{10,... | collective-permute-start | bytes 3145736 | tf_op jit(solution)/shard_map/input_grad1_two/ppermute | solution.py:65
  480.7 20.6 %collective-permute-start.76 = (bf16[2,64,2048]{2,1,0:T(8,128)(2,1)S(1)}, bf16[2,64,2048]{2,1,0:T(8,128)(2,1)S(1)}, u32[]{:S(2)}, u32[]{:S(2)}) collective-permute-start(bf16[2,64,2048]{2,1,0:T(8,128)(2,1)S(1)} %add_convert_fusion.11), channel_id=1, source_target_pairs={{0,8},{1,9},{2,10},{3,11},{4,12},{5,13},{6,14},{7,15},{8,24},{9,25... | collective-permute-start | bytes 1572872 | tf_op jit(solution)/shard_map/input_grad1_ring/ppermute | solution.py:65
  501.3 21.1 %collective-permute-start.78 = (bf16[4,64,2048]{2,1,0:T(8,128)(2,1)S(1)}, bf16[4,64,2048]{2,1,0:T(8,128)(2,1)S(1)}, u32[]{:S(2)}, u32[]{:S(2)}) collective-permute-start(bf16[4,64,2048]{2,1,0:T(8,128)(2,1)S(1)} %get-tuple-element.365), channel_id=1, source_target_pairs={{0,4},{1,3},{2,6},{3,1},{4,0},{5,7},{6,2},{7,5},{8,12},{9,11},{10,... | collective-permute-start | bytes 3145736 | tf_op jit(solution)/shard_map/down_grad0_two/ppermute | solution.py:65
  501.9 19.4 %collective-permute-start.79 = (bf16[2,64,2048]{2,1,0:T(8,128)(2,1)S(1)}, bf16[2,64,2048]{2,1,0:T(8,128)(2,1)S(1)}, u32[]{:S(2)}, u32[]{:S(2)}) collective-permute-start(bf16[2,64,2048]{2,1,0:T(8,128)(2,1)S(1)} %add_convert_fusion.10), channel_id=1, source_target_pairs={{0,8},{1,9},{2,10},{3,11},{4,12},{5,13},{6,14},{7,15},{8,24},{9,25... | collective-permute-start | bytes 1572872 | tf_op jit(solution)/shard_map/input_grad1_ring/ppermute | solution.py:65
  522.4 31.4 %collective-permute-start.81 = (bf16[4,64,2048]{2,1,0:T(8,128)(2,1)}, bf16[4,64,2048]{2,1,0:T(8,128)(2,1)}, u32[]{:S(2)}, u32[]{:S(2)}) collective-permute-start(bf16[4,64,2048]{2,1,0:T(8,128)(2,1)} %get-tuple-element.378), channel_id=1, source_target_pairs={{0,4},{1,3},{2,6},{3,1},{4,0},{5,7},{6,2},{7,5},{8,12},{9,11},{10,... | collective-permute-start | bytes 3145736 | tf_op jit(solution)/shard_map/down_grad0_two/ppermute | solution.py:65
  522.9 30.9 %collective-permute-start.82 = (bf16[4,64,2048]{2,1,0:T(8,128)(2,1)}, bf16[4,64,2048]{2,1,0:T(8,128)(2,1)}, u32[]{:S(2)}, u32[]{:S(2)}) collective-permute-start(bf16[4,64,2048]{2,1,0:T(8,128)(2,1)} %get-tuple-element.380), channel_id=1, source_target_pairs={{0,4},{1,3},{2,6},{3,1},{4,0},{5,7},{6,2},{7,5},{8,12},{9,11},{10,... | collective-permute-start | bytes 3145736 | tf_op jit(solution)/shard_map/up_grad0_two/ppermute | solution.py:65
  524.5 27.7 %collective-permute-start.83 = (bf16[2,64,2048]{2,1,0:T(8,128)(2,1)}, bf16[2,64,2048]{2,1,0:T(8,128)(2,1)}, u32[]{:S(2)}, u32[]{:S(2)}) collective-permute-start(bf16[2,64,2048]{2,1,0:T(8,128)(2,1)} %add_convert_fusion.9), channel_id=1, source_target_pairs={{0,8},{1,9},{2,10},{3,11},{4,12},{5,13},{6,14},{7,15},{8,24},{9,25... | collective-permute-start | bytes 1572872 | tf_op jit(solution)/shard_map/input_grad1_ring/ppermute | solution.py:65
  525.4 28.4 %collective-permute-start.84 = (bf16[2,64,2048]{2,1,0:T(8,128)(2,1)}, bf16[2,64,2048]{2,1,0:T(8,128)(2,1)}, u32[]{:S(2)}, u32[]{:S(2)}) collective-permute-start(bf16[2,64,2048]{2,1,0:T(8,128)(2,1)} %add_convert_fusion.8), channel_id=1, source_target_pairs={{0,8},{1,9},{2,10},{3,11},{4,12},{5,13},{6,14},{7,15},{8,24},{9,25... | collective-permute-start | bytes 1572872 | tf_op jit(solution)/shard_map/down_grad0_ring/ppermute | solution.py:65
  553.8 18.9 %collective-permute-start.85 = (bf16[512,1024]{1,0:T(8,128)(2,1)}, bf16[512,1024]{1,0:T(8,128)(2,1)S(1)}, u32[]{:S(2)}, u32[]{:S(2)}) collective-permute-start(bf16[512,1024]{1,0:T(8,128)(2,1)} %get-tuple-element.384.refs_2_), channel_id=1, source_target_pairs={{0,1},{1,0},{2,3},{3,2},{4,5},{5,4},{6,7},{7,6},{8,9},{9,8},{10,11... | collective-permute-start | bytes 3145736 | tf_op jit(solution)/shard_map/ppermute | solution.py:68
  553.9 19.8 %collective-permute-start.86 = (bf16[4,64,2048]{2,1,0:T(8,128)(2,1)}, bf16[4,64,2048]{2,1,0:T(8,128)(2,1)S(1)}, u32[]{:S(2)}, u32[]{:S(2)}) collective-permute-start(bf16[4,64,2048]{2,1,0:T(8,128)(2,1)} %copy-done.85), channel_id=1, source_target_pairs={{0,4},{1,3},{2,6},{3,1},{4,0},{5,7},{6,2},{7,5},{8,12},{9,11},{10,... | collective-permute-start | bytes 3145736 | tf_op jit(solution)/shard_map/up_grad0_two/ppermute | solution.py:65
  555.6 17.2 %collective-permute-start.88 = (bf16[64,2048]{1,0:T(8,128)(2,1)S(1)}, bf16[64,2048]{1,0:T(8,128)(2,1)S(1)}, u32[]{:S(2)}, u32[]{:S(2)}) collective-permute-start(bf16[64,2048]{1,0:T(8,128)(2,1)S(1)} %fusion.16), channel_id=1, source_target_pairs={{0,2},{1,5},{2,0},{3,7},{4,6},{5,1},{6,4},{7,3},{8,10},{9,13},{10,... | collective-permute-start | bytes 786440 | tf_op jit(solution)/shard_map/input_grad1_one/ppermute | solution.py:65
  573.7 25.8 %collective-permute-start.89 = (bf16[4,64,2048]{2,1,0:T(8,128)(2,1)}, bf16[4,64,2048]{2,1,0:T(8,128)(2,1)}, u32[]{:S(2)}, u32[]{:S(2)}) collective-permute-start(bf16[4,64,2048]{2,1,0:T(8,128)(2,1)} %get-tuple-element.396), channel_id=1, source_target_pairs={{0,4},{1,3},{2,6},{3,1},{4,0},{5,7},{6,2},{7,5},{8,12},{9,11},{10,... | collective-permute-start | bytes 3145736 | tf_op jit(solution)/shard_map/input_grad0_two/ppermute | solution.py:65
  573.8 25.7 %collective-permute-start.90 = (bf16[4,64,2048]{2,1,0:T(8,128)(2,1)}, bf16[4,64,2048]{2,1,0:T(8,128)(2,1)}, u32[]{:S(2)}, u32[]{:S(2)}) collective-permute-start(bf16[4,64,2048]{2,1,0:T(8,128)(2,1)} %add_convert_fusion), channel_id=1, source_target_pairs={{0,2},{1,5},{2,0},{3,7},{4,6},{5,1},{6,4},{7,3},{8,10},{9,13},{10,... | collective-permute-start | bytes 3145736 | tf_op jit(solution)/shard_map/up_grad0_one/ppermute | solution.py:65
  599.6 17.2 %collective-permute-start.92 = (bf16[4,64,2048]{2,1,0:T(8,128)(2,1)S(1)}, bf16[4,64,2048]{2,1,0:T(8,128)(2,1)S(1)}, u32[]{:S(2)}, u32[]{:S(2)}) collective-permute-start(bf16[4,64,2048]{2,1,0:T(8,128)(2,1)S(1)} %copy-done.87), channel_id=1, source_target_pairs={{0,4},{1,3},{2,6},{3,1},{4,0},{5,7},{6,2},{7,5},{8,12},{9,11},{10,... | collective-permute-start | bytes 3145736 | tf_op jit(solution)/shard_map/input_grad0_two/ppermute | solution.py:65
  601.0 15.8 %collective-permute-start.93 = (bf16[2,64,2048]{2,1,0:T(8,128)(2,1)S(1)}, bf16[2,64,2048]{2,1,0:T(8,128)(2,1)S(1)}, u32[]{:S(2)}, u32[]{:S(2)}) collective-permute-start(bf16[2,64,2048]{2,1,0:T(8,128)(2,1)S(1)} %add_convert_fusion.5), channel_id=1, source_target_pairs={{0,8},{1,9},{2,10},{3,11},{4,12},{5,13},{6,14},{7,15},{8,24},{9,25... | collective-permute-start | bytes 1572872 | tf_op jit(solution)/shard_map/input_grad0_ring/ppermute | solution.py:65
  603.6 17.7 %collective-permute-start.96 = (bf16[64,2048]{1,0:T(8,128)(2,1)S(1)}, bf16[64,2048]{1,0:T(8,128)(2,1)S(1)}, u32[]{:S(2)}, u32[]{:S(2)}) collective-permute-start(bf16[64,2048]{1,0:T(8,128)(2,1)S(1)} %fusion.15), channel_id=1, source_target_pairs={{0,8},{1,9},{2,10},{3,11},{4,12},{5,13},{6,14},{7,15},{8,24},{9,25... | collective-permute-start | bytes 786440 | tf_op jit(solution)/shard_map/up_grad0_ring/ppermute | solution.py:65
  621.3 15.8 %collective-permute-start.97 = (bf16[2,64,2048]{2,1,0:T(8,128)(2,1)S(1)}, bf16[2,64,2048]{2,1,0:T(8,128)(2,1)S(1)}, u32[]{:S(2)}, u32[]{:S(2)}) collective-permute-start(bf16[2,64,2048]{2,1,0:T(8,128)(2,1)S(1)} %add_convert_fusion.4), channel_id=1, source_target_pairs={{0,8},{1,9},{2,10},{3,11},{4,12},{5,13},{6,14},{7,15},{8,24},{9,25... | collective-permute-start | bytes 1572872 | tf_op jit(solution)/shard_map/input_grad0_ring/ppermute | solution.py:65
  624.0 16.6 %collective-permute-start.100 = (bf16[64,2048]{1,0:T(8,128)(2,1)S(1)}, bf16[64,2048]{1,0:T(8,128)(2,1)S(1)}, u32[]{:S(2)}, u32[]{:S(2)}) collective-permute-start(bf16[64,2048]{1,0:T(8,128)(2,1)S(1)} %fusion.8), channel_id=1, source_target_pairs={{0,8},{1,9},{2,10},{3,11},{4,12},{5,13},{6,14},{7,15},{8,24},{9,25... | collective-permute-start | bytes 786440 | tf_op jit(solution)/shard_map/up_grad0_ring/ppermute | solution.py:65
  640.7 22.9 %collective-permute-start.101 = (bf16[2,64,2048]{2,1,0:T(8,128)(2,1)S(1)}, bf16[2,64,2048]{2,1,0:T(8,128)(2,1)S(1)}, u32[]{:S(2)}, u32[]{:S(2)}) collective-permute-start(bf16[2,64,2048]{2,1,0:T(8,128)(2,1)S(1)} %add_convert_fusion.3), channel_id=1, source_target_pairs={{0,8},{1,9},{2,10},{3,11},{4,12},{5,13},{6,14},{7,15},{8,24},{9,25... | collective-permute-start | bytes 1572872 | tf_op jit(solution)/shard_map/input_grad0_ring/ppermute | solution.py:65
  (204 other events, 2222.6 us)

commit v3 on v2

--- a/solution.py
+++ b/solution.py
@@ -40,7 +40,7 @@
         in_specs=in_specs,
         out_specs=out_specs,
         scratch_shapes=scratch,
-        compiler_params=pltpu.CompilerParams(vmem_limit_bytes=18 * 1024 * 1024),
+        compiler_params=pltpu.CompilerParams(vmem_limit_bytes=(60 if name in ("queries", "queries_back") else 18) * 1024 * 1024),
         cost_estimate=pl.CostEstimate(flops=flops // COST, bytes_accessed=moved // COST, transcendentals=0),
         name=name,
     )
@@ -860,12 +860,12 @@
         d_out = d_att[r, lanes]
         found = []
         for mask in (only_first, only_second):
-            weights = jnp.exp(dot(mask(q), k, NT))
-            probs = weights / jnp.sum(weights, axis=-1, keepdims=True)
-            d_probs = dot(mask(d_out), v, NT)
-            delta = jnp.sum(probs * d_probs, axis=-1, keepdims=True)
+            weights = jnp.exp(dot(k, mask(q), NT))
+            probs = weights * (1.0 / jnp.sum(weights, axis=0, keepdims=True))
+            d_probs = dot(v, mask(d_out), NT)
+            delta = jnp.sum(probs * d_probs, axis=0, keepdims=True)
             d_scores = (probs * (d_probs - delta)).astype(BF)
-            found.append((dot(d_scores, k), dot(d_scores, q, TN), dot(probs.astype(BF), d_out, TN)))
+            found.append((dot(d_scores, k, TN), dot(d_scores, q), dot(probs.astype(BF), d_out)))
         dq[r, lanes] = pick(found[0][0], found[1][0]) * HEAD_SCALE
         dk[r, lanes] = pick(found[0][1], found[1][1])
         d_projected[r, pl.ds(pl.multiple_of(2 * width + column, 128), 128)] = pick(found[0][2], found[1][2]).astype(BF)
@@ -1140,38 +1140,40 @@
     ready = {}
 
     ga0 = gather(joined[0], True, "input0")
-    gu0 = gather(up_weight[0], False, "up0")
+    gu0 = gather(up_weight[0], True, "up0")
     gd0 = gather(down_weight[0], False, "down0")
     ga1 = gather(joined[1], False, "input1")
     gu1 = gather(up_weight[1], False, "up1")
     gd1 = gather(down_weight[1], False, "down1")
     ga0.ring(3)
-    for each in (gu0, gd0, ga1, gu1, gd1):
+    for each in (gd0, ga1, gu1, gd1):
         each.one()
     rows = all_rows(tokens)
     d_result = all_rows(cotangent)
     close(rows, d_result)
     ga0.one()
     ga0.two(0)
-    gu0.ring(2)
+    gu0.ring(3)
     close()
     ga0.two(1)
-    gu0.ring()
+    gd0.ring()
     close()
     in0, out0 = ga0.end(0, 3 * width), ga0.end(3 * width, width)
-    gu0.two(0)
+    gu0.one()
     gd0.ring()
     normed0, qkv0, attended0, a0 = attention_frame(
         meta, [in0, out0], late(rows), norm_params[0], gains[0], frame, head
     )
     close(a0)
     b0 = clock.add(routes.swap(a0))
+    gu0.two(0)
     gu0.two(1)
     gd0.ring()
+    ga1.ring()
     close()
     up0 = gu0.end()
     gd0.two(0)
-    gd0.ring()
+    ga1.ring()
     mid0, normed_mid0, active0, slope0 = feed_up(meta, up0, rows, a0, late(b0), norm_params[0])
     close(active0)
     gd0.two(1)
@@ -1179,15 +1181,11 @@
     close()
     down0 = gd0.end()
     ga1.two(0)
-    ga1.ring()
+    ga1.two(1)
+    gu1.ring(2)
     m0 = feed_down(meta, down0, late(active0), model)
+    n0 = clock.add(routes.swap(m0))
     close(m0)
-    n0 = clock.add(routes.swap(m0))
-    ga1.ring()
-    close()
-    ga1.two(1)
-    gu1.ring()
-    close()
     in1, out1 = ga1.end(0, 3 * width), ga1.end(3 * width, width)
     gu1.two(0)
     gu1.ring()
@@ -1196,20 +1194,19 @@
     )
     close(slots[0])
     slots = routes.members(late(slots))
-    gu1.ring()
+    gd1.ring()
     close(*slots[1:])
     rise, fall = edges(meta, late(slots))
     below, above = routes.up(rise), routes.down(fall)
     gu1.two(1)
     close(below, above)
     gd1.ring()
+    gd1.two(0)
     *found, sums, whole_found = scene(meta, slots, late(below), above, frame)
     close(found[0])
     home = routes.members(late(found))
     gd1.ring()
     close(*home[1:])
-    gd1.two(0)
-    gd1.ring()
     attended1, a1 = outputs(meta, out1, late(home), width, model)
     b1 = routes.swap(a1)
     close(b1)

time: 686 us -> 659 us (0.961)
  local copies, waits for them, and re-layouts: 64.5 us -> 47 us
  waiting for transfers between devices: 245 us -> 236 us
    unnamed x304 -> x293, local copies, waits for them, and re-layouts: 47.6 us -> 27.5 us
    ppermute x72, waiting for transfers between devices: 184 us -> 166 us  [send(): return lax.ppermute(block, AXES, route)]
    ppermute x19, starting transfers between devices: 29.9 us -> 20.5 us  [member(): lax.ppermute(block, 'frames', [(f, f ^ distance) for f in range(self.n)])]
    ppermute x19, waiting for transfers between devices: 42.2 us -> 51.1 us  [member(): lax.ppermute(block, 'frames', [(f, f ^ distance) for f in range(self.n)])]
  transfers between devices with their start and end apart: 106 -> 106, of which waited for: 48 -> 54; matrix products, arithmetic and copies ran while one was open for 10% -> 11% of each run, Pallas kernels for 27% -> 28%
where the time goes in v3:
time: 659 us; the launch traced here: 648 us
  waiting for transfers between devices  236 us (36%)
  Pallas kernels  188 us (29%)
  starting transfers between devices  120 us (18%)
  other arithmetic  52.9 us (8%)
  local copies, waits for them, and re-layouts  47 us (7%)
    ppermute x72, waiting for transfers between devices, send(): return lax.ppermute(block, AXES, route)  166 us
    ppermute x72, starting transfers between devices, send(): return lax.ppermute(block, AXES, route)  87.1 us
    ppermute x19, waiting for transfers between devices, member(): lax.ppermute(block, 'frames', [(f, f ^ distance) for f in range(self.n)])  51.1 us
    pallas_call x6, Pallas kernels, weight_grad(): call(functools.partial(weight_grad_kernel, base, widths), jax.ShapeDtypeS...  28 us
    unnamed x293, local copies, waits for them, and re-layouts  27.5 us
    pallas_call x1, Pallas kernels, scene_back(): call(functools.partial(scene_back_kernel, frame), (out,) * 4 + (jax.Shape...  23 us
    pallas_call x1, Pallas kernels, frame_back(): call(with_weights(functools.partial(frame_back_kernel, frame, head), 1, w...  21.8 us
    ppermute x19, starting transfers between devices, member(): lax.ppermute(block, 'frames', [(f, f ^ distance) for f in range(self.n)])  20.5 us
  transfers between devices with their start and end apart: 106, of which 54 were waited for; matrix products, arithmetic and copies ran while one was open for 11% of the time, Pallas kernels for 28%

profile of v3, /device:TPU:4, one launch (start us, length us, event | category | flops | bytes accessed | tf_op | source)
XLA Modules:
  0.0 647.8 jit_solution(12844354293292212781)
XLA Ops:
  7.7 4.3 collective-permute-done.2
  15.7 4.5 collective-permute-done.3
  37.9 4.4 collective-permute-done.11
  44.8 6.8 %collective-permute-done.12 = bf16[64,2048]{1,0:T(8,128)(2,1)} collective-permute-done((bf16[64,2048]{1,0:T(8,128)(2,1)}, bf16[64,2048]{1,0:T(8,128)(2,1)}, u32[]{:S(2)}, u32[]{:S(2)}) %collective-permute-start.12) | collective-permute-done | bytes 262176 | tf_op jit(solution)/shard_map/ppermute | solution.py:65
  53.4 5.7 collective-permute-done.13
  59.8 4.1 collective-permute-start.15
  73.5 5.5 collective-permute-done.14
  78.9 3.7 collective-permute-done.15.refs_4_.refs_8_
  82.7 3.6 collective-permute-start.17
  90.3 16.1 %attention_frame.1 = (bf16[512,1024]{1,0:T(8,128)(2,1)S(1)}, bf16[3,512,512]{2,1,0:T(8,128)(2,1)S(1)}, bf16[512,512]{1,0:T(8,128)(2,1)S(1)}, bf16[512,1024]{1,0:T(8,128)(2,1)S(1)}) custom-call(s32[98]{0:T(128)S(1)} %concatenate.44.refs_0_.meta, bf16[4,64,2048]{2,1,0:T(8,128)(2,1)S(1)} %pad_maximum_fusion.refs_1_.refs_5_, ...), custom_call_target="tpu_custom_call" | custom-call | flops 2147483648 | bytes 4194304 | tf_op jit(solution)/shard_map/attention_frame/pallas_call | solution.py:395
  113.4 13.2 %collective-permute-done.18 = bf16[2,64,2048]{2,1,0:T(8,128)(2,1)S(1)} collective-permute-done((bf16[2,64,2048]{2,1,0:T(8,128)(2,1)}, bf16[2,64,2048]{2,1,0:T(8,128)(2,1)S(1)}, u32[]{:S(2)}, u32[]{:S(2)}) %collective-permute-start.18) | collective-permute-done | bytes 524320 | tf_op jit(solution)/shard_map/down0_ring/ppermute | solution.py:65
  126.5 10.4 %collective-permute-done.22 = bf16[2,64,2048]{2,1,0:T(8,128)(2,1)S(1)} collective-permute-done((bf16[2,64,2048]{2,1,0:T(8,128)(2,1)S(1)}, bf16[2,64,2048]{2,1,0:T(8,128)(2,1)S(1)}, u32[]{:S(2)}, u32[]{:S(2)}) %collective-permute-start.22) | collective-permute-done | bytes 524320 | tf_op jit(solution)/shard_map/input1_ring/ppermute | solution.py:65
  140.2 9.4 %feed_up.2 = (f32[512,1024]{1,0:T(8,128)S(1)}, bf16[512,1024]{1,0:T(8,128)(2,1)S(1)}, bf16[512,2048]{1,0:T(8,128)(2,1)S(1)}, bf16[512,2048]{1,0:T(8,128)(2,1)S(1)}) custom-call(s32[98]{0:T(128)S(1)} %concatenate.44.refs_0_.meta, bf16[4,64,2048]{2,1,0:T(8,128)(2,1)} %pad_maximum_fusion.1.refs_1_.refs_5_, ...), custom_call_target="tpu_custom_call" | custom-call | flops 2147483648 | bytes 4194304 | tf_op jit(solution)/shard_map/feed_up/pallas_call | solution.py:446
  154.4 11.6 %collective-permute-done.26 = bf16[2,64,2048]{2,1,0:T(8,128)(2,1)S(1)} collective-permute-done((bf16[2,64,2048]{2,1,0:T(8,128)(2,1)S(1)}, bf16[2,64,2048]{2,1,0:T(8,128)(2,1)S(1)}, u32[]{:S(2)}, u32[]{:S(2)}) %collective-permute-start.26) | collective-permute-done | bytes 524320 | tf_op jit(solution)/shard_map/input1_ring/ppermute | solution.py:65
  173.6 5.3 collective-permute-done.27
  182.8 11.2 %collective-permute-done.30.refs_4_ = bf16[4,64,2048]{2,1,0:T(8,128)(2,1)S(1)} collective-permute-done((bf16[4,64,2048]{2,1,0:T(8,128)(2,1)S(1)}, bf16[4,64,2048]{2,1,0:T(8,128)(2,1)S(1)}, u32[]{:S(2)}, u32[]{:S(2)}) %collective-permute-start.30) | collective-permute-done | bytes 1048608 | tf_op jit(solution)/shard_map/input1_two/ppermute | solution.py:65
  200.1 14.0 %queries.1 = (f32[512,1024]{1,0:T(8,128)}, bf16[512,1024]{1,0:T(8,128)(2,1)}, bf16[3,512,128]{2,1,0:T(8,128)(2,1)}, bf16[3,512,128]{2,1,0:T(8,128)(2,1)}, bf16[3...) custom-call(s32[98]{0:T(128)} %copy-done.68, bf16[4,64,2048]{2,1,0:T(8,128)(2,1)} %copy-done, ...), custom_call_target="tpu_custom_call" | custom-call | flops 1610612736 | bytes 4194304 | tf_op jit(solution)/shard_map/queries/pallas_call | solution.py:514
  221.1 5.8 collective-permute-done.35.s1
  226.8 3.7 collective-permute-done.36.s2
  239.6 10.4 %collective-permute-done.39.below = bf16[3,2,512,128]{3,2,1,0:T(8,128)(2,1)S(1)} collective-permute-done((bf16[3,2,512,128]{3,2,1,0:T(8,128)(2,1)S(1)}, bf16[3,2,512,128]{3,2,1,0:T(8,128)(2,1)S(1)}, u32[]{:S(2)}, u32[]{:S(2)}) %collective-permute-start.39) | collective-permute-done | bytes 786464 | tf_op jit(solution)/shard_map/ppermute | solution.py:83
  250.0 5.9 collective-permute-done.40.above
  260.0 11.4 %scene.1 = (bf16[512,128]{1,0:T(8,128)(2,1)S(1)}, bf16[512,128]{1,0:T(8,128)(2,1)S(1)}, bf16[512,128]{1,0:T(8,128)(2,1)S(1)}, bf16[512,128]{1,0:T(8,128)(2,1)S(1...) custom-call(s32[98]{0:T(128)S(1)} %copy-done.69, bf16[3,512,128]{2,1,0:T(8,128)(2,1)S(1)} %copy-done.64, ...), custom_call_target="tpu_custom_call" | custom-call | flops 2147483648 | bytes 2621440 | tf_op jit(solution)/shard_map/scene/pallas_call | solution.py:609
  292.0 9.4 %feed_up.3 = (f32[512,1024]{1,0:T(8,128)S(1)}, bf16[512,1024]{1,0:T(8,128)(2,1)S(1)}, bf16[512,2048]{1,0:T(8,128)(2,1)S(1)}, bf16[512,2048]{1,0:T(8,128)(2,1)S(1)}) custom-call(s32[98]{0:T(128)S(1)} %copy-done.69, bf16[4,64,2048]{2,1,0:T(8,128)(2,1)S(1)} %pad_maximum_fusion.3.refs_1_.refs_5_, ...), custom_call_target="tpu_custom_call" | custom-call | flops 2147483648 | bytes 4194304 | tf_op jit(solution)/shard_map/feed_up/pallas_call | solution.py:446
  304.8 6.4 feed_back.2
  311.3 4.6 down_grad1.1
  323.4 4.4 up_grad1.1
  342.4 23.0 %scene_back.1 = (bf16[512,128]{1,0:T(8,128)(2,1)S(1)}, bf16[512,128]{1,0:T(8,128)(2,1)S(1)}, bf16[512,128]{1,0:T(8,128)(2,1)S(1)}, bf16[512,128]{1,0:T(8,128)(2,...) custom-call(s32[98]{0:T(128)S(1)} %copy-done.69, ...), custom_call_target="tpu_custom_call" | custom-call | flops 5368709120 | bytes 5242880 | tf_op jit(solution)/shard_map/scene_back/pallas_call | solution.py:990
  375.7 4.9 collective-permute-start.56
  384.4 4.6 collective-permute-done.59.refs_8_
  397.6 4.8 collective-permute-done.64.refs_11_
  403.7 15.0 %queries_back.1 = (bf16[512,1536]{1,0:T(8,128)(2,1)}, bf16[512,1024]{1,0:T(8,128)(2,1)}, f32[16,512]{1,0:T(8,128)}) custom-call(s32[98]{0:T(128)} %copy-done.68, bf16[4,64,2048]{2,1,0:T(8,128)(2,1)} %copy-done, bf16[4,64,2048]{2,1,0:T(8,128)(2,1)} %copy-done.4, bf16[4,64,2048]{2,1,0:T(8,128)(2,1)} %copy-done.9, bf16[4,64,2048]{2,1,0:T(8,128)(2,1)} %copy-done.11, ...), custom_call_target="tpu_custom_call" | custom-call | flops 2684354560 | bytes 4194304 | tf_op jit(solution)/shard_map/queries_back/pallas_call | solution.py:1061
  430.0 4.4 input_grad1.1
  440.6 4.0 norm_back.2
  444.7 6.3 feed_back.3
  457.2 4.9 down_grad0.1
  465.2 9.5 %collective-permute-done.76 = bf16[2,64,2048]{2,1,0:T(8,128)(2,1)S(1)} collective-permute-done((bf16[2,64,2048]{2,1,0:T(8,128)(2,1)S(1)}, bf16[2,64,2048]{2,1,0:T(8,128)(2,1)S(1)}, u32[]{:S(2)}, u32[]{:S(2)}) %collective-permute-start.76) | collective-permute-done | bytes 524320 | tf_op jit(solution)/shard_map/input_grad1_ring/ppermute | solution.py:65
  478.4 5.0 up_grad0.1
  485.5 3.8 norm_back_inner.3
  502.2 21.8 %frame_back.1 = (bf16[512,1536]{1,0:T(8,128)(2,1)S(1)}, bf16[512,1024]{1,0:T(8,128)(2,1)}, f32[16,512]{1,0:T(8,128)S(1)}) custom-call(s32[98]{0:T(128)S(1)} %copy-done.70, bf16[4,64,2048]{2,1,0:T(8,128)(2,1)S(1)} %pad_maximum_fusion.refs_1_.refs_5_, bf16[4,64,2048]{2,1,0:T(8,128)(2,1)S(1)} %collective-permute-done.9.refs_2_.refs_6_, ...), custom_call_target="tpu_custom_call" | custom-call | flops 3221225472 | bytes 4194304 | tf_op jit(solution)/shard_map/frame_back/pallas_call | solution.py:886
  530.7 4.5 input_grad0.1
  538.7 5.0 collective-permute-done.87
  554.7 3.9 norm_back.3
  564.7 8.2 %collective-permute-done.89 = bf16[4,64,2048]{2,1,0:T(8,128)(2,1)} collective-permute-done((bf16[4,64,2048]{2,1,0:T(8,128)(2,1)}, bf16[4,64,2048]{2,1,0:T(8,128)(2,1)}, u32[]{:S(2)}, u32[]{:S(2)}) %collective-permute-start.89) | collective-permute-done | bytes 1048608 | tf_op jit(solution)/shard_map/input_grad0_two/ppermute | solution.py:65
  580.1 10.5 %collective-permute-done.93 = bf16[2,64,2048]{2,1,0:T(8,128)(2,1)S(1)} collective-permute-done((bf16[2,64,2048]{2,1,0:T(8,128)(2,1)S(1)}, bf16[2,64,2048]{2,1,0:T(8,128)(2,1)S(1)}, u32[]{:S(2)}, u32[]{:S(2)}) %collective-permute-start.93) | collective-permute-done | bytes 524320 | tf_op jit(solution)/shard_map/input_grad0_ring/ppermute | solution.py:65
  590.9 4.7 collective-permute-done.96
  602.4 8.9 %collective-permute-done.97 = bf16[2,64,2048]{2,1,0:T(8,128)(2,1)S(1)} collective-permute-done((bf16[2,64,2048]{2,1,0:T(8,128)(2,1)S(1)}, bf16[2,64,2048]{2,1,0:T(8,128)(2,1)S(1)}, u32[]{:S(2)}, u32[]{:S(2)}) %collective-permute-start.97) | collective-permute-done | bytes 524320 | tf_op jit(solution)/shard_map/input_grad0_ring/ppermute | solution.py:65
  611.6 3.8 collective-permute-done.100
  619.1 10.2 %collective-permute-done.104 = f32[13,1024]{1,0:T(8,128)S(1)} collective-permute-done((f32[13,1024]{1,0:T(8,128)S(1)}, f32[13,1024]{1,0:T(8,128)S(1)}, u32[]{:S(2)}, u32[]{:S(2)}) %collective-permute-start.104) | collective-permute-done | bytes 53280 | tf_op jit(solution)/shard_map/ppermute | solution.py:77
  (602 shorter events, 276.8 us)
Async XLA Ops:
  5.7 24.3 %collective-permute-start.6 = (bf16[64,2048]{1,0:T(8,128)(2,1)}, bf16[64,2048]{1,0:T(8,128)(2,1)S(1)}, u32[]{:S(2)}, u32[]{:S(2)}) collective-permute-start(bf16[64,2048]{1,0:T(8,128)(2,1)} %get-tuple-element.450), channel_id=1, source_target_pairs={{0,2},{1,5},{2,0},{3,7},{4,6},{5,1},{6,4},{7,3},{8,10},{9,13},{10,... | collective-permute-start | bytes 786440 | tf_op jit(solution)/shard_map/down1_one/ppermute | solution.py:65
  7.2 18.3 %collective-permute-start.8 = (bf16[2,128,1024]{2,1,0:T(8,128)(2,1)S(1)}, bf16[2,128,1024]{2,1,0:T(8,128)(2,1)}, u32[]{:S(2)}, u32[]{:S(2)}) collective-permute-start(bf16[2,128,1024]{2,1,0:T(8,128)(2,1)S(1)} %bitcast.159), channel_id=1, source_target_pairs={{0,1},{1,0},{2,3},{3,2},{4,5},{5,4},{6,7},{7,6},{8,9},{9,8},{10,11... | collective-permute-start | bytes 1572872 | tf_op jit(solution)/shard_map/ppermute | solution.py:68
  13.9 16.1 %collective-permute-start = (bf16[64,2048]{1,0:T(8,128)(2,1)}, bf16[64,2048]{1,0:T(8,128)(2,1)S(1)}, u32[]{:S(2)}, u32[]{:S(2)}) collective-permute-start(bf16[64,2048]{1,0:T(8,128)(2,1)} %get-tuple-element.453), channel_id=1, source_target_pairs={{0,2},{1,5},{2,0},{3,7},{4,6},{5,1},{6,4},{7,3},{8,10},{9,13},{10,... | collective-permute-start | bytes 786440 | tf_op jit(solution)/shard_map/up1_one/ppermute | solution.py:65
  32.7 26.4 %collective-permute-start.9 = (bf16[4,64,2048]{2,1,0:T(8,128)(2,1)S(1)}, bf16[4,64,2048]{2,1,0:T(8,128)(2,1)S(1)}, u32[]{:S(2)}, u32[]{:S(2)}) collective-permute-start(bf16[4,64,2048]{2,1,0:T(8,128)(2,1)S(1)} %pad_maximum_fusion.refs_1_.refs_5_), channel_id=1, source_target_pairs={{0,2},{1,5},{2,0},{3,7},{4,6},{5,1},{6,4},{7,3},{8,10},{9,13},{10,... | collective-permute-start | bytes 3145736 | tf_op jit(solution)/shard_map/input0_one/ppermute | solution.py:65
  33.2 25.9 %collective-permute-start.10 = (bf16[4,64,2048]{2,1,0:T(8,128)(2,1)S(1)}, bf16[4,64,2048]{2,1,0:T(8,128)(2,1)S(1)}, u32[]{:S(2)}, u32[]{:S(2)}) collective-permute-start(bf16[4,64,2048]{2,1,0:T(8,128)(2,1)S(1)} %pad_maximum_fusion.refs_1_.refs_5_), channel_id=1, source_target_pairs={{0,4},{1,3},{2,6},{3,1},{4,0},{5,7},{6,2},{7,5},{8,12},{9,11},{10,... | collective-permute-start | bytes 3145736 | tf_op jit(solution)/shard_map/input0_two/ppermute | solution.py:65
  59.8 22.9 %collective-permute-start.15 = (bf16[4,64,2048]{2,1,0:T(8,128)(2,1)S(1)}, bf16[4,64,2048]{2,1,0:T(8,128)(2,1)}, u32[]{:S(2)}, u32[]{:S(2)}) collective-permute-start(bf16[4,64,2048]{2,1,0:T(8,128)(2,1)S(1)} %collective-permute-done.9.refs_2_.refs_6_), channel_id=1, source_target_pairs={{0,4},{1,3},{2,6},{3,1},{4,0},{5,7},{6,2},{7,5},{8,12},{9,11},{10,... | collective-permute-start | bytes 3145736 | tf_op jit(solution)/shard_map/input0_two/ppermute | solution.py:65
  82.7 25.7 %collective-permute-start.17 = (bf16[4,64,2048]{2,1,0:T(8,128)(2,1)}, bf16[4,64,2048]{2,1,0:T(8,128)(2,1)}, u32[]{:S(2)}, u32[]{:S(2)}) collective-permute-start(bf16[4,64,2048]{2,1,0:T(8,128)(2,1)} %pad_maximum_fusion.1.refs_1_.refs_5_), channel_id=1, source_target_pairs={{0,2},{1,5},{2,0},{3,7},{4,6},{5,1},{6,4},{7,3},{8,10},{9,13},{10,... | collective-permute-start | bytes 3145736 | tf_op jit(solution)/shard_map/up0_one/ppermute | solution.py:65
  86.6 21.9 %collective-permute-start.16 = (bf16[2,64,2048]{2,1,0:T(8,128)(2,1)}, bf16[2,64,2048]{2,1,0:T(8,128)(2,1)}, u32[]{:S(2)}, u32[]{:S(2)}) collective-permute-start(bf16[2,64,2048]{2,1,0:T(8,128)(2,1)} %collective-permute-done.14), channel_id=1, source_target_pairs={{0,8},{1,9},{2,10},{3,11},{4,12},{5,13},{6,14},{7,15},{8,24},{9,25... | collective-permute-start | bytes 1572872 | tf_op jit(solution)/shard_map/down0_ring/ppermute | solution.py:65
  108.4 28.5 %collective-permute-start.20 = (bf16[4,64,2048]{2,1,0:T(8,128)(2,1)}, bf16[4,64,2048]{2,1,0:T(8,128)(2,1)S(1)}, u32[]{:S(2)}, u32[]{:S(2)}) collective-permute-start(bf16[4,64,2048]{2,1,0:T(8,128)(2,1)} %pad_maximum_fusion.1.refs_1_.refs_5_), channel_id=1, source_target_pairs={{0,4},{1,3},{2,6},{3,1},{4,0},{5,7},{6,2},{7,5},{8,12},{9,11},{10,... | collective-permute-start | bytes 3145736 | tf_op jit(solution)/shard_map/up0_two/ppermute | solution.py:65
  109.2 27.7 %collective-permute-start.21 = (bf16[4,64,2048]{2,1,0:T(8,128)(2,1)}, bf16[4,64,2048]{2,1,0:T(8,128)(2,1)S(1)}, u32[]{:S(2)}, u32[]{:S(2)}) collective-permute-start(bf16[4,64,2048]{2,1,0:T(8,128)(2,1)} %collective-permute-done.17.refs_2_.refs_6_), channel_id=1, source_target_pairs={{0,4},{1,3},{2,6},{3,1},{4,0},{5,7},{6,2},{7,5},{8,12},{9,11},{10,... | collective-permute-start | bytes 3145736 | tf_op jit(solution)/shard_map/up0_two/ppermute | solution.py:65
  110.6 15.9 %collective-permute-start.18 = (bf16[2,64,2048]{2,1,0:T(8,128)(2,1)}, bf16[2,64,2048]{2,1,0:T(8,128)(2,1)S(1)}, u32[]{:S(2)}, u32[]{:S(2)}) collective-permute-start(bf16[2,64,2048]{2,1,0:T(8,128)(2,1)} %collective-permute-done.16), channel_id=1, source_target_pairs={{0,8},{1,9},{2,10},{3,11},{4,12},{5,13},{6,14},{7,15},{8,24},{9,25... | collective-permute-start | bytes 1572872 | tf_op jit(solution)/shard_map/down0_ring/ppermute | solution.py:65
  112.1 24.8 %collective-permute-start.22 = (bf16[2,64,2048]{2,1,0:T(8,128)(2,1)S(1)}, bf16[2,64,2048]{2,1,0:T(8,128)(2,1)S(1)}, u32[]{:S(2)}, u32[]{:S(2)}) collective-permute-start(bf16[2,64,2048]{2,1,0:T(8,128)(2,1)S(1)} %pad_maximum_fusion.11), channel_id=1, source_target_pairs={{0,8},{1,9},{2,10},{3,11},{4,12},{5,13},{6,14},{7,15},{8,24},{9,25... | collective-permute-start | bytes 1572872 | tf_op jit(solution)/shard_map/input1_ring/ppermute | solution.py:65
  168.6 25.5 %collective-permute-start.30 = (bf16[4,64,2048]{2,1,0:T(8,128)(2,1)S(1)}, bf16[4,64,2048]{2,1,0:T(8,128)(2,1)S(1)}, u32[]{:S(2)}, u32[]{:S(2)}) collective-permute-start(bf16[4,64,2048]{2,1,0:T(8,128)(2,1)S(1)} %constant_dynamic-update-slice_fusion.2.refs_2_), channel_id=1, source_target_pairs={{0,4},{1,3},{2,6},{3,1},{4,0},{5,7},{6,2},{7,5},{8,12},{9,11},{10,... | collective-permute-start | bytes 3145736 | tf_op jit(solution)/shard_map/input1_two/ppermute | solution.py:65
  173.5 20.5 %collective-permute-start.31 = (bf16[512,1024]{1,0:T(8,128)(2,1)S(1)}, bf16[512,1024]{1,0:T(8,128)(2,1)S(1)}, u32[]{:S(2)}, u32[]{:S(2)}) collective-permute-start(bf16[512,1024]{1,0:T(8,128)(2,1)S(1)} %feed_down.2.refs_6_.refs_7_), channel_id=1, source_target_pairs={{0,1},{1,0},{2,3},{3,2},{4,5},{5,4},{6,7},{7,6},{8,9},{9,8},{10,11... | collective-permute-start | bytes 3145736 | tf_op jit(solution)/shard_map/ppermute | solution.py:68
  178.9 16.1 %collective-permute-start.28 = (bf16[2,64,2048]{2,1,0:T(8,128)(2,1)S(1)}, bf16[2,64,2048]{2,1,0:T(8,128)(2,1)}, u32[]{:S(2)}, u32[]{:S(2)}) collective-permute-start(bf16[2,64,2048]{2,1,0:T(8,128)(2,1)S(1)} %collective-permute-done.27), channel_id=1, source_target_pairs={{0,8},{1,9},{2,10},{3,11},{4,12},{5,13},{6,14},{7,15},{8,24},{9,25... | collective-permute-start | bytes 1572872 | tf_op jit(solution)/shard_map/ppermute | solution.py:65
  195.1 19.1 %collective-permute-start.33 = (bf16[4,64,2048]{2,1,0:T(8,128)(2,1)S(1)}, bf16[4,64,2048]{2,1,0:T(8,128)(2,1)}, u32[]{:S(2)}, u32[]{:S(2)}) collective-permute-start(bf16[4,64,2048]{2,1,0:T(8,128)(2,1)S(1)} %pad_maximum_fusion.3.refs_1_.refs_5_), channel_id=1, source_target_pairs={{0,4},{1,3},{2,6},{3,1},{4,0},{5,7},{6,2},{7,5},{8,12},{9,11},{10,... | collective-permute-start | bytes 3145736 | tf_op jit(solution)/shard_map/up1_two/ppermute | solution.py:65
  196.0 18.1 %collective-permute-start.32 = (bf16[2,64,2048]{2,1,0:T(8,128)(2,1)}, bf16[2,64,2048]{2,1,0:T(8,128)(2,1)}, u32[]{:S(2)}, u32[]{:S(2)}) collective-permute-start(bf16[2,64,2048]{2,1,0:T(8,128)(2,1)} %collective-permute-done.28), channel_id=1, source_target_pairs={{0,8},{1,9},{2,10},{3,11},{4,12},{5,13},{6,14},{7,15},{8,24},{9,25... | collective-permute-start | bytes 1572872 | tf_op jit(solution)/shard_map/up1_ring/ppermute | solution.py:65
  214.2 19.2 %collective-permute-start.34 = (bf16[2,64,2048]{2,1,0:T(8,128)(2,1)S(1)}, bf16[2,64,2048]{2,1,0:T(8,128)(2,1)S(1)}, u32[]{:S(2)}, u32[]{:S(2)}) collective-permute-start(bf16[2,64,2048]{2,1,0:T(8,128)(2,1)S(1)} %pad_maximum_fusion.12), channel_id=1, source_target_pairs={{0,8},{1,9},{2,10},{3,11},{4,12},{5,13},{6,14},{7,15},{8,24},{9,25... | collective-permute-start | bytes 1572872 | tf_op jit(solution)/shard_map/down1_ring/ppermute | solution.py:65
  217.2 16.1 %collective-permute-start.37 = (bf16[3,512,128]{2,1,0:T(8,128)(2,1)}, bf16[3,512,128]{2,1,0:T(8,128)(2,1)S(1)}, u32[]{:S(2)}, u32[]{:S(2)}) collective-permute-start(bf16[3,512,128]{2,1,0:T(8,128)(2,1)} %get-tuple-element.247), channel_id=1, source_target_pairs={{0,6},{2,4},{4,2},{6,0},{8,14},{10,12},{12,10},{14,8},{16,22},{18,... | collective-permute-start | bytes 1179656 | tf_op jit(solution)/shard_map/ppermute | solution.py:77
  233.4 22.6 %collective-permute-start.38 = (bf16[4,64,2048]{2,1,0:T(8,128)(2,1)S(1)}, bf16[4,64,2048]{2,1,0:T(8,128)(2,1)S(1)}, u32[]{:S(2)}, u32[]{:S(2)}) collective-permute-start(bf16[4,64,2048]{2,1,0:T(8,128)(2,1)S(1)} %constant_dynamic-update-slice_fusion.4.refs_2_.refs_6_), channel_id=1, source_target_pairs={{0,4},{1,3},{2,6},{3,1},{4,0},{5,7},{6,2},{7,5},{8,12},{9,11},{10,... | collective-permute-start | bytes 3145736 | tf_op jit(solution)/shard_map/up1_two/ppermute | solution.py:65
  238.1 17.8 %collective-permute-start.40 = (bf16[3,2,512,128]{3,2,1,0:T(8,128)(2,1)S(1)}, bf16[3,2,512,128]{3,2,1,0:T(8,128)(2,1)S(1)}, u32[]{:S(2)}, u32[]{:S(2)}) collective-permute-start(bf16[3,2,512,128]{3,2,1,0:T(8,128)(2,1)S(1)} %get-tuple-element.256), channel_id=1, source_target_pairs={{8,0},{10,2},{12,4},{14,6},{16,8},{18,10},{20,12},{22,14},{24,16},... | collective-permute-start | bytes 2359304 | tf_op jit(solution)/shard_map/ppermute | solution.py:86
  255.9 18.6 %collective-permute-start.42 = (bf16[4,64,2048]{2,1,0:T(8,128)(2,1)S(1)}, bf16[4,64,2048]{2,1,0:T(8,128)(2,1)S(1)}, u32[]{:S(2)}, u32[]{:S(2)}) collective-permute-start(bf16[4,64,2048]{2,1,0:T(8,128)(2,1)S(1)} %pad_maximum_fusion.5.refs_1_), channel_id=1, source_target_pairs={{0,4},{1,3},{2,6},{3,1},{4,0},{5,7},{6,2},{7,5},{8,12},{9,11},{10,... | collective-permute-start | bytes 3145736 | tf_op jit(solution)/shard_map/down1_two/ppermute | solution.py:65
  340.1 25.3 %collective-permute-start.54 = (bf16[4,64,2048]{2,1,0:T(8,128)(2,1)S(1)}, bf16[4,64,2048]{2,1,0:T(8,128)(2,1)S(1)}, u32[]{:S(2)}, u32[]{:S(2)}) collective-permute-start(bf16[4,64,2048]{2,1,0:T(8,128)(2,1)S(1)} %add_convert_fusion.2), channel_id=1, source_target_pairs={{0,2},{1,5},{2,0},{3,7},{4,6},{5,1},{6,4},{7,3},{8,10},{9,13},{10,... | collective-permute-start | bytes 3145736 | tf_op jit(solution)/shard_map/down_grad1_one/ppermute | solution.py:65
  340.7 24.7 %collective-permute-start.55 = (bf16[4,64,2048]{2,1,0:T(8,128)(2,1)S(1)}, bf16[4,64,2048]{2,1,0:T(8,128)(2,1)S(1)}, u32[]{:S(2)}, u32[]{:S(2)}) collective-permute-start(bf16[4,64,2048]{2,1,0:T(8,128)(2,1)S(1)} %get-tuple-element.301), channel_id=1, source_target_pairs={{0,4},{1,3},{2,6},{3,1},{4,0},{5,7},{6,2},{7,5},{8,12},{9,11},{10,... | collective-permute-start | bytes 3145736 | tf_op jit(solution)/shard_map/down_grad1_two/ppermute | solution.py:65
  365.5 23.6 %collective-permute-start.61 = (bf16[4,64,2048]{2,1,0:T(8,128)(2,1)S(1)}, bf16[4,64,2048]{2,1,0:T(8,128)(2,1)S(1)}, u32[]{:S(2)}, u32[]{:S(2)}) collective-permute-start(bf16[4,64,2048]{2,1,0:T(8,128)(2,1)S(1)} %get-tuple-element.320), channel_id=1, source_target_pairs={{0,4},{1,3},{2,6},{3,1},{4,0},{5,7},{6,2},{7,5},{8,12},{9,11},{10,... | collective-permute-start | bytes 3145736 | tf_op jit(solution)/shard_map/up_grad1_two/ppermute | solution.py:65
  365.9 23.2 %collective-permute-start.60 = (bf16[3,2,512,128]{3,2,1,0:T(8,128)(2,1)S(1)}, bf16[3,2,512,128]{3,2,1,0:T(8,128)(2,1)S(1)}, u32[]{:S(2)}, u32[]{:S(2)}) collective-permute-start(bf16[3,2,512,128]{3,2,1,0:T(8,128)(2,1)S(1)} %get-tuple-element.318), channel_id=1, source_target_pairs={{0,8},{2,10},{4,12},{6,14},{8,16},{10,18},{12,20},{14,22},{16,24},... | collective-permute-start | bytes 2359304 | tf_op jit(solution)/shard_map/ppermute | solution.py:83
  367.9 21.2 %collective-permute-start.62 = (bf16[3,2,512,128]{3,2,1,0:T(8,128)(2,1)S(1)}, bf16[3,2,512,128]{3,2,1,0:T(8,128)(2,1)S(1)}, u32[]{:S(2)}, u32[]{:S(2)}) collective-permute-start(bf16[3,2,512,128]{3,2,1,0:T(8,128)(2,1)S(1)} %get-tuple-element.322), channel_id=1, source_target_pairs={{8,0},{10,2},{12,4},{14,6},{16,8},{18,10},{20,12},{22,14},{24,16},... | collective-permute-start | bytes 2359304 | tf_op jit(solution)/shard_map/ppermute | solution.py:86
  375.7 19.8 %collective-permute-start.56 = (bf16[512,1024]{1,0:T(8,128)(2,1)S(1)}, bf16[512,1024]{1,0:T(8,128)(2,1)S(1)}, u32[]{:S(2)}, u32[]{:S(2)}) collective-permute-start(bf16[512,1024]{1,0:T(8,128)(2,1)S(1)} %feed_down.3), channel_id=1, source_target_pairs={{0,1},{1,0},{2,3},{3,2},{4,5},{5,4},{6,7},{7,6},{8,9},{9,8},{10,11... | collective-permute-start | bytes 3145736 | tf_op jit(solution)/shard_map/ppermute | solution.py:68
  402.4 16.4 %collective-permute-start.68 = (bf16[4,64,2048]{2,1,0:T(8,128)(2,1)}, bf16[4,64,2048]{2,1,0:T(8,128)(2,1)}, u32[]{:S(2)}, u32[]{:S(2)}) collective-permute-start(bf16[4,64,2048]{2,1,0:T(8,128)(2,1)} %add_convert_fusion.1), channel_id=1, source_target_pairs={{0,2},{1,5},{2,0},{3,7},{4,6},{5,1},{6,4},{7,3},{8,10},{9,13},{10,... | collective-permute-start | bytes 3145736 | tf_op jit(solution)/shard_map/up_grad1_one/ppermute | solution.py:65
  418.7 17.9 %collective-permute-start.67 = (bf16[512,1024]{1,0:T(8,128)(2,1)}, bf16[512,1024]{1,0:T(8,128)(2,1)}, u32[]{:S(2)}, u32[]{:S(2)}) collective-permute-start(bf16[512,1024]{1,0:T(8,128)(2,1)} %get-tuple-element.335.refs_2_), channel_id=1, source_target_pairs={{0,1},{1,0},{2,3},{3,2},{4,5},{5,4},{6,7},{7,6},{8,9},{9,8},{10,11... | collective-permute-start | bytes 3145736 | tf_op jit(solution)/shard_map/ppermute | solution.py:68
  418.8 17.8 %collective-permute-start.70 = (bf16[4,64,2048]{2,1,0:T(8,128)(2,1)}, bf16[4,64,2048]{2,1,0:T(8,128)(2,1)}, u32[]{:S(2)}, u32[]{:S(2)}) collective-permute-start(bf16[4,64,2048]{2,1,0:T(8,128)(2,1)} %copy-done.82), channel_id=1, source_target_pairs={{0,4},{1,3},{2,6},{3,1},{4,0},{5,7},{6,2},{7,5},{8,12},{9,11},{10,... | collective-permute-start | bytes 3145736 | tf_op jit(solution)/shard_map/up_grad1_two/ppermute | solution.py:65
  452.4 22.3 %collective-permute-start.75 = (bf16[4,64,2048]{2,1,0:T(8,128)(2,1)S(1)}, bf16[4,64,2048]{2,1,0:T(8,128)(2,1)S(1)}, u32[]{:S(2)}, u32[]{:S(2)}) collective-permute-start(bf16[4,64,2048]{2,1,0:T(8,128)(2,1)S(1)} %get-tuple-element.353), channel_id=1, source_target_pairs={{0,4},{1,3},{2,6},{3,1},{4,0},{5,7},{6,2},{7,5},{8,12},{9,11},{10,... | collective-permute-start | bytes 3145736 | tf_op jit(solution)/shard_map/input_grad1_two/ppermute | solution.py:65
  456.5 18.2 %collective-permute-start.76 = (bf16[2,64,2048]{2,1,0:T(8,128)(2,1)S(1)}, bf16[2,64,2048]{2,1,0:T(8,128)(2,1)S(1)}, u32[]{:S(2)}, u32[]{:S(2)}) collective-permute-start(bf16[2,64,2048]{2,1,0:T(8,128)(2,1)S(1)} %add_convert_fusion.11), channel_id=1, source_target_pairs={{0,8},{1,9},{2,10},{3,11},{4,12},{5,13},{6,14},{7,15},{8,24},{9,25... | collective-permute-start | bytes 1572872 | tf_op jit(solution)/shard_map/input_grad1_ring/ppermute | solution.py:65
  474.8 21.1 %collective-permute-start.78 = (bf16[4,64,2048]{2,1,0:T(8,128)(2,1)S(1)}, bf16[4,64,2048]{2,1,0:T(8,128)(2,1)S(1)}, u32[]{:S(2)}, u32[]{:S(2)}) collective-permute-start(bf16[4,64,2048]{2,1,0:T(8,128)(2,1)S(1)} %get-tuple-element.363), channel_id=1, source_target_pairs={{0,4},{1,3},{2,6},{3,1},{4,0},{5,7},{6,2},{7,5},{8,12},{9,11},{10,... | collective-permute-start | bytes 3145736 | tf_op jit(solution)/shard_map/down_grad0_two/ppermute | solution.py:65
  477.1 17.7 %collective-permute-start.79 = (bf16[2,64,2048]{2,1,0:T(8,128)(2,1)S(1)}, bf16[2,64,2048]{2,1,0:T(8,128)(2,1)S(1)}, u32[]{:S(2)}, u32[]{:S(2)}) collective-permute-start(bf16[2,64,2048]{2,1,0:T(8,128)(2,1)S(1)} %add_convert_fusion.10), channel_id=1, source_target_pairs={{0,8},{1,9},{2,10},{3,11},{4,12},{5,13},{6,14},{7,15},{8,24},{9,25... | collective-permute-start | bytes 1572872 | tf_op jit(solution)/shard_map/input_grad1_ring/ppermute | solution.py:65
  495.9 31.2 %collective-permute-start.81 = (bf16[4,64,2048]{2,1,0:T(8,128)(2,1)}, bf16[4,64,2048]{2,1,0:T(8,128)(2,1)}, u32[]{:S(2)}, u32[]{:S(2)}) collective-permute-start(bf16[4,64,2048]{2,1,0:T(8,128)(2,1)} %get-tuple-element.376), channel_id=1, source_target_pairs={{0,4},{1,3},{2,6},{3,1},{4,0},{5,7},{6,2},{7,5},{8,12},{9,11},{10,... | collective-permute-start | bytes 3145736 | tf_op jit(solution)/shard_map/down_grad0_two/ppermute | solution.py:65
  496.7 30.4 %collective-permute-start.82 = (bf16[4,64,2048]{2,1,0:T(8,128)(2,1)}, bf16[4,64,2048]{2,1,0:T(8,128)(2,1)}, u32[]{:S(2)}, u32[]{:S(2)}) collective-permute-start(bf16[4,64,2048]{2,1,0:T(8,128)(2,1)} %get-tuple-element.378), channel_id=1, source_target_pairs={{0,4},{1,3},{2,6},{3,1},{4,0},{5,7},{6,2},{7,5},{8,12},{9,11},{10,... | collective-permute-start | bytes 3145736 | tf_op jit(solution)/shard_map/up_grad0_two/ppermute | solution.py:65
  497.9 27.6 %collective-permute-start.83 = (bf16[2,64,2048]{2,1,0:T(8,128)(2,1)}, bf16[2,64,2048]{2,1,0:T(8,128)(2,1)}, u32[]{:S(2)}, u32[]{:S(2)}) collective-permute-start(bf16[2,64,2048]{2,1,0:T(8,128)(2,1)} %add_convert_fusion.9), channel_id=1, source_target_pairs={{0,8},{1,9},{2,10},{3,11},{4,12},{5,13},{6,14},{7,15},{8,24},{9,25... | collective-permute-start | bytes 1572872 | tf_op jit(solution)/shard_map/input_grad1_ring/ppermute | solution.py:65
  500.4 26.7 %collective-permute-start.84 = (bf16[2,64,2048]{2,1,0:T(8,128)(2,1)}, bf16[2,64,2048]{2,1,0:T(8,128)(2,1)}, u32[]{:S(2)}, u32[]{:S(2)}) collective-permute-start(bf16[2,64,2048]{2,1,0:T(8,128)(2,1)} %add_convert_fusion.8), channel_id=1, source_target_pairs={{0,8},{1,9},{2,10},{3,11},{4,12},{5,13},{6,14},{7,15},{8,24},{9,25... | collective-permute-start | bytes 1572872 | tf_op jit(solution)/shard_map/down_grad0_ring/ppermute | solution.py:65
  527.1 18.7 %collective-permute-start.85 = (bf16[512,1024]{1,0:T(8,128)(2,1)}, bf16[512,1024]{1,0:T(8,128)(2,1)S(1)}, u32[]{:S(2)}, u32[]{:S(2)}) collective-permute-start(bf16[512,1024]{1,0:T(8,128)(2,1)} %get-tuple-element.382.refs_2_), channel_id=1, source_target_pairs={{0,1},{1,0},{2,3},{3,2},{4,5},{5,4},{6,7},{7,6},{8,9},{9,8},{10,11... | collective-permute-start | bytes 3145736 | tf_op jit(solution)/shard_map/ppermute | solution.py:68
  527.2 19.6 %collective-permute-start.86 = (bf16[4,64,2048]{2,1,0:T(8,128)(2,1)}, bf16[4,64,2048]{2,1,0:T(8,128)(2,1)S(1)}, u32[]{:S(2)}, u32[]{:S(2)}) collective-permute-start(bf16[4,64,2048]{2,1,0:T(8,128)(2,1)} %copy-done.83), channel_id=1, source_target_pairs={{0,4},{1,3},{2,6},{3,1},{4,0},{5,7},{6,2},{7,5},{8,12},{9,11},{10,... | collective-permute-start | bytes 3145736 | tf_op jit(solution)/shard_map/up_grad0_two/ppermute | solution.py:65
  528.8 17.0 %collective-permute-start.88 = (bf16[64,2048]{1,0:T(8,128)(2,1)S(1)}, bf16[64,2048]{1,0:T(8,128)(2,1)S(1)}, u32[]{:S(2)}, u32[]{:S(2)}) collective-permute-start(bf16[64,2048]{1,0:T(8,128)(2,1)S(1)} %fusion.16), channel_id=1, source_target_pairs={{0,2},{1,5},{2,0},{3,7},{4,6},{5,1},{6,4},{7,3},{8,10},{9,13},{10,... | collective-permute-start | bytes 786440 | tf_op jit(solution)/shard_map/input_grad1_one/ppermute | solution.py:65
  546.8 26.1 %collective-permute-start.89 = (bf16[4,64,2048]{2,1,0:T(8,128)(2,1)}, bf16[4,64,2048]{2,1,0:T(8,128)(2,1)}, u32[]{:S(2)}, u32[]{:S(2)}) collective-permute-start(bf16[4,64,2048]{2,1,0:T(8,128)(2,1)} %get-tuple-element.394), channel_id=1, source_target_pairs={{0,4},{1,3},{2,6},{3,1},{4,0},{5,7},{6,2},{7,5},{8,12},{9,11},{10,... | collective-permute-start | bytes 3145736 | tf_op jit(solution)/shard_map/input_grad0_two/ppermute | solution.py:65
  548.6 24.3 %collective-permute-start.90 = (bf16[4,64,2048]{2,1,0:T(8,128)(2,1)}, bf16[4,64,2048]{2,1,0:T(8,128)(2,1)}, u32[]{:S(2)}, u32[]{:S(2)}) collective-permute-start(bf16[4,64,2048]{2,1,0:T(8,128)(2,1)} %add_convert_fusion), channel_id=1, source_target_pairs={{0,2},{1,5},{2,0},{3,7},{4,6},{5,1},{6,4},{7,3},{8,10},{9,13},{10,... | collective-permute-start | bytes 3145736 | tf_op jit(solution)/shard_map/up_grad0_one/ppermute | solution.py:65
  572.9 17.7 %collective-permute-start.92 = (bf16[4,64,2048]{2,1,0:T(8,128)(2,1)S(1)}, bf16[4,64,2048]{2,1,0:T(8,128)(2,1)S(1)}, u32[]{:S(2)}, u32[]{:S(2)}) collective-permute-start(bf16[4,64,2048]{2,1,0:T(8,128)(2,1)S(1)} %copy-done.85), channel_id=1, source_target_pairs={{0,4},{1,3},{2,6},{3,1},{4,0},{5,7},{6,2},{7,5},{8,12},{9,11},{10,... | collective-permute-start | bytes 3145736 | tf_op jit(solution)/shard_map/input_grad0_two/ppermute | solution.py:65
  577.3 18.3 %collective-permute-start.96 = (bf16[64,2048]{1,0:T(8,128)(2,1)S(1)}, bf16[64,2048]{1,0:T(8,128)(2,1)S(1)}, u32[]{:S(2)}, u32[]{:S(2)}) collective-permute-start(bf16[64,2048]{1,0:T(8,128)(2,1)S(1)} %fusion.15), channel_id=1, source_target_pairs={{0,8},{1,9},{2,10},{3,11},{4,12},{5,13},{6,14},{7,15},{8,24},{9,25... | collective-permute-start | bytes 786440 | tf_op jit(solution)/shard_map/up_grad0_ring/ppermute | solution.py:65
  597.4 17.9 %collective-permute-start.100 = (bf16[64,2048]{1,0:T(8,128)(2,1)S(1)}, bf16[64,2048]{1,0:T(8,128)(2,1)S(1)}, u32[]{:S(2)}, u32[]{:S(2)}) collective-permute-start(bf16[64,2048]{1,0:T(8,128)(2,1)S(1)} %fusion.8), channel_id=1, source_target_pairs={{0,8},{1,9},{2,10},{3,11},{4,12},{5,13},{6,14},{7,15},{8,24},{9,25... | collective-permute-start | bytes 786440 | tf_op jit(solution)/shard_map/up_grad0_ring/ppermute | solution.py:65
  615.3 21.7 %collective-permute-start.101 = (bf16[2,64,2048]{2,1,0:T(8,128)(2,1)S(1)}, bf16[2,64,2048]{2,1,0:T(8,128)(2,1)S(1)}, u32[]{:S(2)}, u32[]{:S(2)}) collective-permute-start(bf16[2,64,2048]{2,1,0:T(8,128)(2,1)S(1)} %add_convert_fusion.3), channel_id=1, source_target_pairs={{0,8},{1,9},{2,10},{3,11},{4,12},{5,13},{6,14},{7,15},{8,24},{9,25... | collective-permute-start | bytes 1572872 | tf_op jit(solution)/shard_map/input_grad0_ring/ppermute | solution.py:65
  (199 other events, 2561.7 us)
